TPU v7x, 128 devices: a whole 4x4x4 slice. The times are simulated.
128 devices in a mesh: dp: 8 (over y_hi, z), ctx: 16 (over x, y_lo, core).
Axes of the slice: x: 4, y: 4 (y_hi: 2, y_lo: 2; y = y_hi * 2 + y_lo), z: 4, core: 2. Of those that a mesh axis runs over, the one named last changes fastest.
Arguments:
- queries: bfloat16 [8, 2048, 4096], P('dp', 'ctx'), may hold values from -6 to 6
- key_tensor: bfloat16 [8, 2048, 512], P('dp', 'ctx'), may hold values from -6 to 6
- value_tensor: bfloat16 [8, 2048, 512], P('dp', 'ctx'), may hold values from -6 to 6
- attention_output: bfloat16 [8, 2048, 4096], P('dp', 'ctx'), may hold values from -6 to 6
- output_gradient: bfloat16 [8, 2048, 4096], P('dp', 'ctx'), may hold values from -0.59765625 to 0.59765625
- logsumexp_rows: float32 [8, 32, 2048], P('dp', None, 'ctx'), may hold values from 1 to 5
- layer_input: bfloat16 [8, 2048, 5120], P('dp', 'ctx'), may hold values from -6 to 6
- parents: int32 [8, 16], P('dp'), may hold values from 0 to 14, as said below
Outputs:
- grad_queries: bfloat16 [8, 2048, 4096], P('dp', 'ctx')
- grad_keys: bfloat16 [8, 2048, 512], P('dp', 'ctx')
- grad_values: bfloat16 [8, 2048, 512], P('dp', 'ctx')
- grad_kv_weight: float32 [5120, 1024], P(('dp', 'ctx'))
Inputs may be any that keep to these rules, and one draw needn't show every extreme that they name: parents[0] is 0 (the root); for every block b >= 1 of a tree parents[b] < b; the last block's parent is the block before it.
All inputs are finite; a program needn't handle non-finite values.
Results may differ from a plain program's by a relative error of at most 0.0057.
Values may be sent and summed in bfloat16 or wider, within the bound.
No kernel may reach another device: no remote copies, remote signals or barrier semaphores. Data moves between devices by JAX's collectives and lax.ppermute only.
A program may use at most 128 MiB of HBM per device.

v0:
```python
import math

import jax
import jax.numpy as jnp
from jax import lax
from jax.sharding import PartitionSpec as P

QUERY_HEADS = 32
KEY_VALUE_HEADS = 4
HEAD_SIZE = 128
BLK = 128


def ancestry(parent_row, block_count):
    block_ids = jnp.arange(block_count, dtype=jnp.int32)
    parent_hop = ((parent_row[:, None] == block_ids[None, :]) & (block_ids[:, None] > 0)).astype(
        jnp.float32
    )
    reach_table = jnp.maximum(jnp.eye(block_count, dtype=jnp.float32), parent_hop)
    for level in range(block_count.bit_length()):
        reach_table = jnp.minimum(
            jnp.dot(reach_table, reach_table, precision=lax.Precision.HIGHEST), 1.0
        )
    return reach_table


def local(
    queries,
    key_tensor,
    value_tensor,
    attention_output,
    output_gradient,
    logsumexp_rows,
    layer_input,
    parents,
):
    shard_length = queries.shape[1]
    query_group_width = QUERY_HEADS // KEY_VALUE_HEADS
    score_scale = HEAD_SIZE ** (-0.5)
    key_value_width = KEY_VALUE_HEADS * HEAD_SIZE
    block_count = parents.shape[1]
    reach_table = ancestry(parents[0], block_count)
    block_ids = jnp.arange(block_count, dtype=jnp.int32)
    query_pos = lax.axis_index("ctx") * shard_length + jnp.arange(shard_length, dtype=jnp.int32)
    query_blk = query_pos // BLK
    query_onehot = (query_blk[:, None] == block_ids[None, :]).astype(jnp.float32)
    query_reach = jnp.dot(query_onehot, reach_table, precision=lax.Precision.HIGHEST)
    query_by_head = queries[0].reshape(shard_length, KEY_VALUE_HEADS, query_group_width, HEAD_SIZE)
    gradient_by_head = output_gradient[0].reshape(
        shard_length, KEY_VALUE_HEADS, query_group_width, HEAD_SIZE
    )
    output_by_head = attention_output[0].reshape(
        shard_length, KEY_VALUE_HEADS, query_group_width, HEAD_SIZE
    )
    row_delta = jnp.sum(
        gradient_by_head.astype(jnp.float32) * output_by_head.astype(jnp.float32), axis=-1
    ).transpose(1, 2, 0)
    logsumexp_row_view = logsumexp_rows[0].reshape(KEY_VALUE_HEADS, query_group_width, shard_length)

    def allowed_for(key_pos):
        key_blk = key_pos // BLK
        key_onehot = (key_blk[:, None] == block_ids[None, :]).astype(jnp.float32)
        reach_cols = lax.dot_general(
            query_reach, key_onehot, (((1,), (1,)), ((), ())), precision=lax.Precision.HIGHEST
        )
        return (reach_cols > 0.5) & (
            (query_blk[:, None] != key_blk[None, :]) | (key_pos[None, :] <= query_pos[:, None])
        )

    def key_block(query_acc, block_in):
        key_pos, key_row_view, value_row_view = block_in
        allowed = allowed_for(key_pos)
        scores = (
            jnp.einsum(
                "tkgd,nkd->kgtn", query_by_head, key_row_view, preferred_element_type=jnp.float32
            )
            * score_scale
        )
        prob_full = jnp.where(
            allowed[None, None], jnp.exp(scores - logsumexp_row_view[..., None]), 0.0
        )
        prob_low = prob_full.astype(jnp.bfloat16)
        prob_grad = jnp.einsum(
            "tkgd,nkd->kgtn", gradient_by_head, value_row_view, preferred_element_type=jnp.float32
        )
        dscore = prob_full * (prob_grad - row_delta[..., None])
        dscore_low = dscore.astype(jnp.bfloat16)
        query_acc = query_acc + jnp.einsum(
            "kgtn,nkd->tkgd", dscore_low, key_row_view, preferred_element_type=jnp.float32
        )
        key_part = (
            jnp.einsum(
                "kgtn,tkgd->nkd", dscore_low, query_by_head, preferred_element_type=jnp.float32
            )
            * score_scale
        )
        value_part = jnp.einsum(
            "kgtn,tkgd->nkd", prob_low, gradient_by_head, preferred_element_type=jnp.float32
        )
        return (query_acc, (key_part, value_part))

    query_initial_zero = jnp.zeros(
        (shard_length, KEY_VALUE_HEADS, query_group_width, HEAD_SIZE), jnp.float32
    )
    key_portion = lax.all_gather(key_tensor, "ctx", axis=1, tiled=True)
    value_portion = lax.all_gather(value_tensor, "ctx", axis=1, tiled=True)
    piece_len = key_portion.shape[1]
    partial_width = math.gcd(piece_len, 512)
    loop_step_count = piece_len // partial_width
    key_pos = jnp.arange(piece_len, dtype=jnp.int32).reshape(loop_step_count, partial_width)
    key_division = key_portion[0].reshape(
        loop_step_count, partial_width, KEY_VALUE_HEADS, HEAD_SIZE
    )
    value_division = value_portion[0].reshape(
        loop_step_count, partial_width, KEY_VALUE_HEADS, HEAD_SIZE
    )
    query_out, (key_parts, value_parts) = lax.scan(
        key_block, query_initial_zero, (key_pos, key_division, value_division)
    )
    key_grad_out = key_parts.reshape(piece_len, key_value_width)
    value_grad_out = value_parts.reshape(piece_len, key_value_width)
    query_acc = query_out
    grad_queries = (
        (query_acc * score_scale)
        .astype(jnp.bfloat16)
        .reshape(1, shard_length, QUERY_HEADS * HEAD_SIZE)
    )
    key_grad_own, value_grad_own = (
        lax.psum_scatter(key_grad_out, "ctx", scatter_dimension=0, tiled=True),
        lax.psum_scatter(value_grad_out, "ctx", scatter_dimension=0, tiled=True),
    )
    grad_keys = key_grad_own.astype(jnp.bfloat16)
    grad_values = value_grad_own.astype(jnp.bfloat16)
    kv_grads = jnp.concatenate([grad_keys, grad_values], axis=1)
    local_input = layer_input[0]
    grad_kv_weight = lax.psum_scatter(
        lax.dot_general(
            local_input, kv_grads, (((0,), (0,)), ((), ())), preferred_element_type=jnp.float32
        ),
        ("dp", "ctx"),
        scatter_dimension=0,
        tiled=True,
    )
    return (grad_queries, grad_keys[None], grad_values[None], grad_kv_weight)


def solution(mesh):
    in_specs = (
        P("dp", "ctx", None),
        P("dp", "ctx", None),
        P("dp", "ctx", None),
        P("dp", "ctx", None),
        P("dp", "ctx", None),
        P("dp", None, "ctx"),
        P("dp", "ctx", None),
        P("dp", None),
    )
    out_specs = (
        P("dp", "ctx", None),
        P("dp", "ctx", None),
        P("dp", "ctx", None),
        P(("dp", "ctx"), None),
    )
    return jax.shard_map(local, mesh=mesh, in_specs=in_specs, out_specs=out_specs, check_vma=False)
```

profile of v0, /device:TPU:1, one launch (start us, length us, event | category | flops | bytes accessed | tf_op | source)
XLA Modules:
  0.0 986.1 jit_solution(6043982258892964539)
XLA Ops:
  8.7 1.6 copy.33
  11.1 2.3 copy.35
  16.3 1.6 fusion.27
  18.9 28.4 %all-gather.3.cloned.1.call-done = bf16[1,2048,512]{2,1,0:T(8,128)(2,1)} async-done(((bf16[1,128,512]{2,1,0:T(8,128)(2,1)}), bf16[1,2048,512]{2,1,0:T(8,128)(2,1)}) %all-gather.3.cloned.1.call-update) | async-done | bytes 2097168 | tf_op jit(solution)/shard_map/all_gather | solution.py:105
  47.3 4.0 reshape_squeeze.13
  51.3 31.8 %all-gather.5.cloned.1.call-done = bf16[1,2048,512]{2,1,0:T(8,128)(2,1)} async-done(((bf16[1,128,512]{2,1,0:T(8,128)(2,1)}), bf16[1,2048,512]{2,1,0:T(8,128)(2,1)}) %all-gather.5.cloned.1.call-update) | async-done | bytes 2097168 | tf_op jit(solution)/shard_map/all_gather | solution.py:106
  83.1 4.0 reshape_squeeze.15
  87.1 56.0 %while.19 = (s32[]{:T(128)}, f32[128,4,8,128]{0,3,2,1:T(8,128)}, f32[4,512,4,128]{3,2,1,0:T(4,128)}, f32[4,512,4,128]{3,2,1,0:T(4,128)}, bf16[4,512,4,128]{3,2,1...) while((s32[]{:T(128)}, f32[128,4,8,128]{0,3,2,1:T(8,128)}, ...), condition=%wide.region_2.3_spmd.clone.clone.clone, body=%wide.region_1.2_spmd.clone.clone.clone.sunk | while | flops 2719572992 | bytes 73148656 | solution.py:117
  92.7 2.8 fusion.81
  98.4 2.7 copy_dynamic-update-slice_fusion.3
  106.7 2.8 fusion.81
  112.4 2.7 copy_dynamic-update-slice_fusion.3
  120.7 2.8 fusion.81
  126.4 2.6 copy_dynamic-update-slice_fusion.3
  134.6 2.8 fusion.81
  140.4 2.7 copy_dynamic-update-slice_fusion.3
  143.1 4.6 copy.73
  147.7 4.6 copy.74
  152.6 59.0 %reduce-scatter.8.cloned.1.call-done = f32[128,512]{1,0:T(8,128)} async-done(((f32[2048,512]{1,0:T(8,128)}), f32[128,512]{1,0:T(8,128)}) %reduce-scatter.8.cloned.1.call-update) | async-done | bytes 262160 | tf_op jit(solution)/shard_map/reduce_scatter | solution.py:130
  212.6 67.2 %reduce-scatter.6.cloned.1.call-done = f32[128,512]{1,0:T(8,128)} async-done(((f32[2048,512]{1,0:T(8,128)}), f32[128,512]{1,0:T(8,128)}) %reduce-scatter.6.cloned.1.call-update) | async-done | bytes 262160 | tf_op jit(solution)/shard_map/reduce_scatter | solution.py:129
  280.8 8.7 convolution_bitcast_fusion.1
  289.5 21.3 %copy.53 = f32[5120,1024]{1,0:T(8,128)} copy(f32[5120,1024]{0,1:T(8,128)} %convolution_bitcast_fusion.1) | data formatting | bytes 41943040
  310.9 1.9 multiply_convert_fusion
  315.5 664.0 %reduce-scatter.10.cloned.1.call-done = f32[40,1024]{1,0:T(8,128)} async-done(((f32[5120,1024]{1,0:T(8,128)}), f32[40,1024]{1,0:T(8,128)}) %reduce-scatter.10.cloned.1.call-update) | async-done | bytes 163856
  (102 shorter events, 44.9 us)
Async XLA Ops:
  7.2 273.6 %copy-start = (bf16[1,128,5120]{2,1,0:T(8,128)(2,1)S(1)}, bf16[1,128,5120]{2,1,0:T(8,128)(2,1)}, u32[]{:S(2)}) copy-start(bf16[1,128,5120]{2,1,0:T(8,128)(2,1)} %param.16) | copy-start | bytes 3932164
  7.2 40.2 %all-gather.3.cloned.1.call-start = ((), (), s32[]{:S(2)}) async-start(), calls=%async_computation.3 | async-start | bytes 2228224 | tf_op jit(solution)/shard_map/all_gather | solution.py:105
  7.9 75.2 %all-gather.5.cloned.1.call-start = ((), (), s32[]{:S(2)}) async-start(), calls=%async_computation.4 | async-start | bytes 2228224 | tf_op jit(solution)/shard_map/all_gather | solution.py:106
  8.7 203.0 %reduce-scatter.8.cloned.1.call-start = ((), (), s32[]{:S(2)}) async-start(), calls=%async_computation.6 | async-start | bytes 4456448 | tf_op jit(solution)/shard_map/reduce_scatter | solution.py:130
  11.0 6.9 copy-start.7
  18.9 68.1 %copy-start.5 = (bf16[128,4,8,128]{3,0,2,1:T(8,128)(2,1)S(1)}, bf16[128,4,8,128]{3,0,2,1:T(8,128)(2,1)}, u32[]{:S(2)}) copy-start(bf16[128,4,8,128]{3,0,2,1:T(8,128)(2,1)} %copy.39) | copy-start | bytes 3145732
  18.9 68.1 %copy-start.6 = (f32[1,32,128]{2,1,0:T(8,128)S(1)}, f32[1,32,128]{2,1,0:T(8,128)}, u32[]{:S(2)}) copy-start(f32[1,32,128]{2,1,0:T(8,128)} %param.15) | copy-start | bytes 49156
  95.4 1.6 copy-start.1
  98.4 2.7 copy-start.2
  109.4 1.6 copy-start.1
  112.4 2.7 copy-start.2
  123.4 1.6 copy-start.1
  126.4 2.7 copy-start.2
  137.4 1.6 copy-start.1
  140.4 2.7 copy-start.2
  147.7 132.1 %reduce-scatter.6.cloned.1.call-start = ((), (), s32[]{:S(2)}) async-start(), calls=%async_computation.5 | async-start | bytes 4456448 | tf_op jit(solution)/shard_map/reduce_scatter | solution.py:129
  152.4 827.2 %reduce-scatter.10.cloned.1.call-start = ((), (), s32[]{:S(2)}) async-start(), calls=%async_computation.7 | async-start | bytes 21135360
  310.8 3.3 copy-start.3
  310.9 4.0 copy-start.4
Sparse Core Ops, SparseCore 0:
  9.7 37.5 all-gather.2
  49.1 34.0 all-gather.4
  147.8 63.7 reduce-scatter.7
  213.9 65.8 reduce-scatter.5
  311.0 668.5 reduce-scatter.9
where the time goes:
time: 993 us; the launch traced here: 986 us
  waiting for transfers between devices  852 us (86%)
  local copies, waits for them, and re-layouts  69.1 us (7%)
  matrix products  43.3 us (4%)
  between operations  13.9 us (1%)
    unnamed x6, waiting for transfers between devices  665 us
    reduce_scatter x1, waiting for transfers between devices, local(): lax.psum_scatter(key_grad_out, 'ctx', scatter_dimension=0, tiled=True)  67.2 us
    reduce_scatter x1, waiting for transfers between devices, local(): lax.psum_scatter(value_grad_out, 'ctx', scatter_dimension=0, tiled=True)  59 us
    unnamed x20, local copies, waits for them, and re-layouts  38.1 us
    all_gather x1, waiting for transfers between devices, local(): value_portion = lax.all_gather(value_tensor, 'ctx', axis=1, tiled=True)  31.8 us
    all_gather x1, waiting for transfers between devices, local(): key_portion = lax.all_gather(key_tensor, 'ctx', axis=1, tiled=True)  28.4 us
  transfers between devices with their start and end apart: 5, of which 5 were waited for; matrix products, arithmetic and copies ran while one was open for 2% of the time, Pallas kernels for 0%

commit v1 on v0

v1 whole, which is shorter than its diff:
```python
import functools

import jax
import jax.numpy as jnp
from jax import lax
from jax.experimental import pallas as pl
from jax.experimental.pallas import tpu as pltpu
from jax.sharding import PartitionSpec as P

QUERY_HEADS = 32
KEY_VALUE_HEADS = 4
HEAD_SIZE = 128
BLK = 128
GROUP = QUERY_HEADS // KEY_VALUE_HEADS
RING = 4
SIDE = 4
TREES = 8
TALL = 512
ROWS = GROUP * BLK
PACK = 2 * ROWS + 32
SCALE = HEAD_SIZE ** (-0.5)
RING_ORDER = (2, 1, 3)
LOG2E = 1.4426950408889634
F32 = jnp.float32
BF16 = jnp.bfloat16
MIB = 1 << 20


def side_perm(k):
    return [(c, c ^ k) for c in range(RING * SIDE)]


def ring_perm(s):
    return [(c, ((c // SIDE + s) % RING) * SIDE + c % SIDE) for c in range(RING * SIDE)]


def smem():
    return pl.BlockSpec(memory_space=pltpu.SMEM)


def vmem():
    return pl.BlockSpec(memory_space=pltpu.VMEM)


def call(kernel, out_shape, n_smem, n_vmem, n_any=0, scratch=(), moved=0, limit=32):
    return pl.pallas_call(
        kernel,
        out_shape=out_shape,
        in_specs=[smem()] * n_smem + [vmem()] * n_vmem + [pl.BlockSpec(memory_space=pl.ANY)] * n_any,
        out_specs=[vmem()] * len(out_shape),
        scratch_shapes=list(scratch),
        compiler_params=pltpu.CompilerParams(vmem_limit_bytes=limit * MIB),
        cost_estimate=pl.CostEstimate(flops=0, bytes_accessed=moved, transcendentals=0),
    )


def split_kv_kernel(place, key_ref, value_ref, *outs):
    own = place[1]
    for k, out in enumerate(outs):
        col = pl.multiple_of((own ^ k) * HEAD_SIZE, HEAD_SIZE)
        out[0:BLK, :] = key_ref[:, pl.ds(col, HEAD_SIZE)]
        out[BLK:, :] = value_ref[:, pl.ds(col, HEAD_SIZE)]


def split_queries_kernel(place, query_ref, gradient_ref, output_ref, lse_ref, after, *outs):
    lane = lax.broadcasted_iota(jnp.int32, (BLK, 128), 1)
    columns = jnp.zeros((BLK, 128), F32)
    for h in range(GROUP):
        cols = slice(h * HEAD_SIZE, (h + 1) * HEAD_SIZE)
        prod = gradient_ref[:, cols].astype(F32) * output_ref[:, cols].astype(F32)
        columns = jnp.where(lane == h, jnp.sum(prod, axis=1, keepdims=True), columns)
    delta = columns.T[0:GROUP]
    lse = lse_ref[...] * LOG2E

    def split(rows):
        high = rows.astype(BF16)
        low = (rows - high.astype(F32)).astype(BF16)
        return jnp.concatenate([high, low], axis=0)

    for k, out in enumerate(outs):

        @pl.when(pl.program_id(0) == k)
        def _(out=out):
            for h in range(GROUP):
                cols = slice(h * HEAD_SIZE, (h + 1) * HEAD_SIZE)
                out[h * BLK : (h + 1) * BLK, :] = query_ref[:, cols]
                out[ROWS + h * BLK : ROWS + (h + 1) * BLK, :] = gradient_ref[:, cols]
            out[2 * ROWS : 2 * ROWS + 16, :] = split(lse)
            out[2 * ROWS + 16 :, :] = split(delta)


def split_queries(place, queries, gradient, output, lse, after):
    wide = pl.BlockSpec((BLK, GROUP * HEAD_SIZE), lambda k, place: (0, place[1] ^ k))
    return pl.pallas_call(
        split_queries_kernel,
        out_shape=[shape(PACK)] * SIDE,
        grid_spec=pltpu.PrefetchScalarGridSpec(
            num_scalar_prefetch=1,
            grid=(SIDE,),
            in_specs=[
                wide,
                wide,
                wide,
                pl.BlockSpec((GROUP, BLK), lambda k, place: (place[1] ^ k, 0)),
                pl.BlockSpec(memory_space=pl.ANY),
            ],
            out_specs=[pl.BlockSpec((PACK, HEAD_SIZE), lambda k, place: (0, 0))] * SIDE,
        ),
        compiler_params=pltpu.CompilerParams(vmem_limit_bytes=56 * MIB),
        cost_estimate=pl.CostEstimate(flops=0, bytes_accessed=32 * MIB, transcendentals=0),
    )(place, queries, gradient, output, lse, after)


def ring_pack_kernel(place, inputs, *refs):
    kv, refs = refs[:SIDE], refs[SIDE + 1 :]
    outs, shares = refs[:RING], refs[RING]
    _, _, quarter = shares.shape
    piece = quarter // TREES
    for r in range(RING):
        shares[r] = jnp.concatenate(
            [inputs[:, (d * RING + r) * piece : (d * RING + r + 1) * piece] for d in range(TREES)], axis=1
        )
    for s, out in enumerate(outs):
        out[:, 0:quarter] = shares[(place[0] + s) % RING]
        for k in range(SIDE):
            for half in range(2):
                col = quarter + (2 * k + half) * HEAD_SIZE
                out[:, col : col + HEAD_SIZE] = kv[k][half * BLK : (half + 1) * BLK, :]


def attention_kernel(place, parents, *refs):
    ring_in, packs, refs = refs[:RING], refs[RING : RING + SIDE], refs[RING + SIDE + 1 :]
    dq_near, dq_far, grad_own, grad_out, refs = refs[0], refs[1], refs[2], refs[3 : RING + 2], refs[RING + 2 :]
    kv, kv_t, pack, query_t, gradient_t, col_lse, col_delta, dq_acc, dq, acc = refs
    ring, own = place[0], place[1]
    start = ring_in[0].shape[1] - 2 * SIDE * HEAD_SIZE

    for s in range(RING):
        for k in range(SIDE):
            for half in range(2):
                col = start + (2 * k + half) * HEAD_SIZE
                kv[s * SIDE + k, half * BLK : (half + 1) * BLK, :] = ring_in[s][:, col : col + HEAD_SIZE]
    for k in range(SIDE):
        pack[k] = packs[k][...]
    acc[...] = jnp.zeros_like(acc)

    @pl.loop(0, RING * SIDE)
    def _(j):
        kv_t[j, :, 0:BLK] = kv[j, 0:BLK, :].T
        kv_t[j, :, BLK:] = kv[j, BLK:, :].T

    def slot_of(at):
        return ((ring - at // SIDE) % RING) * SIDE + ((at % SIDE) ^ own)

    def tile(piece, slots, diagonal):
        n = len(slots) * BLK
        keys = jnp.concatenate([kv[j, 0:BLK, :] for j in slots], axis=0)
        keys_t = jnp.concatenate([kv_t[j, :, 0:BLK] for j in slots], axis=1)
        values_t = jnp.concatenate([kv_t[j, :, BLK:] for j in slots], axis=1)
        dk = dv = None
        for p in range(ROWS // TALL):
            span = slice(p * TALL, (p + 1) * TALL)
            scores = jnp.dot(pack[piece, span, :], keys_t, preferred_element_type=F32)
            lse = jnp.concatenate([col_lse[span, :]] * len(slots), axis=1)
            delta = jnp.concatenate([col_delta[span, :]] * len(slots), axis=1)
            prob = jnp.exp2(scores * (SCALE * LOG2E) - lse)
            if diagonal:
                query_at = lax.broadcasted_iota(jnp.int32, (TALL, n), 0) % BLK
                key_at = lax.broadcasted_iota(jnp.int32, (TALL, n), 1)
                prob = jnp.where((key_at <= query_at) | (key_at >= BLK), prob, 0.0)
            prob_grad = jnp.dot(
                pack[piece, ROWS + p * TALL : ROWS + (p + 1) * TALL, :], values_t, preferred_element_type=F32
            )
            dscore = (prob * (prob_grad - delta)).astype(BF16)
            dv_part = jnp.dot(gradient_t[:, span], prob.astype(BF16), preferred_element_type=F32)
            dk_part = jnp.dot(query_t[:, span], dscore, preferred_element_type=F32)
            dv = dv_part if dv is None else dv + dv_part
            dk = dk_part if dk is None else dk + dk_part
            part = jnp.dot(dscore, keys, preferred_element_type=F32)
            if diagonal:
                dq_acc[span, :] = part
            else:
                dq_acc[span, :] += part
        for m, j in enumerate(slots):
            acc[j, 0:BLK, :] += dk[:, m * BLK : (m + 1) * BLK]
            acc[j, BLK:, :] += dv[:, m * BLK : (m + 1) * BLK]

    @pl.loop(0, SIDE)
    def _(piece):
        terms = pack[piece, 2 * ROWS :, :].astype(F32)
        lse = terms[0:8] + terms[8:16]
        delta = terms[16:24] + terms[24:32]
        for h in range(GROUP):
            cols = slice(h * BLK, (h + 1) * BLK)
            query_t[:, cols] = pack[piece, cols, :].T
            gradient_t[:, cols] = pack[piece, ROWS + h * BLK : ROWS + (h + 1) * BLK, :].T
            col_lse[cols, :] = jnp.broadcast_to(lse[h : h + 1], (BLK, BLK)).T
            col_delta[cols, :] = jnp.broadcast_to(delta[h : h + 1], (BLK, BLK)).T

        block = ring * SIDE + (own ^ piece)
        above = lax.while_loop(lambda c: c[0] > 0, lambda c: (parents[0, c[0]], c[1] + 1), (block, 0))[1]
        odd = above % 2 == 1

        @pl.when(odd)
        def _():
            tile(piece, [piece, slot_of(parents[0, block])], True)

        @pl.when(jnp.logical_not(odd))
        def _():
            tile(piece, [piece], True)

        def ancestors(at):
            one = parents[0, at]
            two = parents[0, one]
            tile(piece, [slot_of(one), slot_of(two)], False)
            return two

        lax.while_loop(lambda at: at > 0, ancestors, jnp.where(odd, parents[0, block], block))
        dq[piece] = (dq_acc[...] * SCALE).astype(BF16)

    for k in range(SIDE):
        out = dq_near if k < 2 else dq_far
        out[(k % 2) * ROWS : (k % 2 + 1) * ROWS, :] = dq[k]
    for s in range(RING):
        for k in range(SIDE):
            dk, dv = acc[s * SIDE + k, 0:BLK, :].T * SCALE, acc[s * SIDE + k, BLK:, :].T
            out = grad_own if s == 0 else grad_out[s - 1]
            out[2 * k * BLK : (2 * k + 1) * BLK, :] = dk.astype(out.dtype)
            out[(2 * k + 1) * BLK : (2 * k + 2) * BLK, :] = dv.astype(out.dtype)


def attention_call(place, parents, ring_in, packs, after):
    sum_shape = (RING * SIDE, 2 * BLK, HEAD_SIZE)
    return call(
        attention_kernel,
        [shape(2 * ROWS)] * 2 + [shape(ROWS, kind=F32)] + [shape(ROWS)] * (RING - 1),
        2,
        RING + SIDE,
        n_any=1,
        scratch=[
            pltpu.VMEM(sum_shape, BF16),
            pltpu.VMEM((RING * SIDE, HEAD_SIZE, 2 * BLK), BF16),
            pltpu.VMEM((SIDE, PACK, HEAD_SIZE), BF16),
            pltpu.VMEM((HEAD_SIZE, ROWS), BF16),
            pltpu.VMEM((HEAD_SIZE, ROWS), BF16),
            pltpu.VMEM((ROWS, 128), F32),
            pltpu.VMEM((ROWS, 128), F32),
            pltpu.VMEM((ROWS, HEAD_SIZE), F32),
            pltpu.VMEM((SIDE, ROWS, HEAD_SIZE), BF16),
            pltpu.VMEM(sum_shape, F32),
        ],
    )(place, parents, *ring_in, *packs, after)


def total_kernel(own_ref, *refs):
    parts, total = refs[:-1], refs[-1]
    value = own_ref[...]
    for part in parts:
        value = value + part[...].astype(F32)
    total[...] = value.astype(BF16)


def relay_inputs_kernel(own, side, dq_near, dq_far, total, core_out, side_out):
    rows, cols = own.shape
    core_out[0:rows, 0:cols] = own[...]
    core_out[rows:, 0:cols] = side[...]
    core_out[:, cols:] = dq_near[ROWS:, :]
    side_out[0 : 2 * ROWS, :] = dq_far[...]
    side_out[2 * ROWS :, :] = total[4 * BLK :, :]


def relay_outputs_kernel(total, side, out):
    out[0:ROWS, :] = side[ROWS : 2 * ROWS, :]
    out[ROWS : ROWS + 2 * BLK, :] = total[2 * BLK : 4 * BLK, :]
    out[ROWS + 2 * BLK :, :] = side[2 * ROWS + 2 * BLK :, :]


def join_inputs_kernel(*refs):
    pieces, out = refs[:RING], refs[-1]
    for s in range(RING):
        out[s * BLK : (s + 1) * BLK, :] = pieces[s][:, 0 : out.shape[1]]


def projection_kernel(*refs):
    grads = dict(zip((0,) + RING_ORDER, refs[:RING]))
    own, side, core = refs[RING : RING + 3]
    out, grad_t, weight_t = refs[RING + 3 :]
    rows, cols = own.shape
    inputs = (own, core.at[0:rows, 0:cols], side, core.at[rows:, 0:cols])
    for s in range(RING):
        for k in range(SIDE):
            at = 2 * k * BLK
            grad_t[k, 0:BLK, s * BLK : (s + 1) * BLK] = grads[s][at : at + BLK, :].T
            grad_t[k, BLK:, s * BLK : (s + 1) * BLK] = grads[s][at + BLK : at + 2 * BLK, :].T
    total = jnp.dot(grad_t[0], inputs[0][...], preferred_element_type=F32)
    for k in range(1, SIDE):
        total = total + jnp.dot(grad_t[k], inputs[k][...], preferred_element_type=F32)
    weight_t[...] = total
    for n in range(out.shape[0] // BLK):
        rows = slice(n * BLK, (n + 1) * BLK)
        out[rows, 0:BLK] = weight_t[0:BLK, rows].T.astype(BF16)
        out[rows, BLK:] = weight_t[BLK:, rows].T.astype(BF16)


def join_kernel(place, near, core, side, crossed, total, queries, keys, values):
    own = place[1]
    last = core.shape[1] - HEAD_SIZE
    for h in range(GROUP):
        rows = slice(h * BLK, (h + 1) * BLK)
        for k, piece in enumerate((near[rows, :], core[rows, last:], side[rows, :], crossed[rows, :])):
            col = pl.multiple_of((own ^ k) * (GROUP * HEAD_SIZE) + h * HEAD_SIZE, HEAD_SIZE)
            queries[:, pl.ds(col, HEAD_SIZE)] = piece
    for k, (ref, at) in enumerate(((total, 0), (crossed, ROWS), (side, 2 * ROWS), (crossed, ROWS + 2 * BLK))):
        col = pl.multiple_of((own ^ k) * HEAD_SIZE, HEAD_SIZE)
        keys[:, pl.ds(col, HEAD_SIZE)] = ref[at : at + BLK, :]
        values[:, pl.ds(col, HEAD_SIZE)] = ref[at + BLK : at + 2 * BLK, :]


def shape(rows, cols=HEAD_SIZE, kind=BF16):
    return jax.ShapeDtypeStruct((rows, cols), kind)


def local(
    queries,
    key_tensor,
    value_tensor,
    attention_output,
    output_gradient,
    logsumexp_rows,
    layer_input,
    parents,
    trees,
):
    width = layer_input.shape[2]
    quarter = width // RING
    share = width // (trees * RING * SIDE)
    at = lax.axis_index("ctx")
    ring, own = at // SIDE, at % SIDE
    place = jnp.stack([ring, own]).astype(jnp.int32)

    def to_side(x, k):
        return lax.ppermute(x, "ctx", side_perm(k))

    def to_ring(x, s):
        return lax.ppermute(x, "ctx", ring_perm(s % RING))

    with jax.named_scope("keys_values"):
        kv_split = call(split_kv_kernel, [shape(2 * BLK)] * SIDE, 1, 2, limit=56)(
            place, key_tensor[0], value_tensor[0]
        )
        kv_side = [kv_split[0]] + [to_side(kv_split[k], k) for k in (1, 2, 3)]

    with jax.named_scope("queries"):
        packs = split_queries(
            place, queries[0], output_gradient[0], attention_output[0], logsumexp_rows[0], kv_split[1]
        )
        packs = [packs[0]] + [to_side(packs[k], k) for k in (1, 2, 3)]

    with jax.named_scope("ring"):
        ring_out = call(
            ring_pack_kernel,
            [shape(BLK, quarter + 2 * SIDE * HEAD_SIZE)] * RING,
            1,
            1 + SIDE,
            n_any=1,
            moved=16 * MIB,
            scratch=[pltpu.VMEM((RING, BLK, quarter), BF16)],
        )(place, layer_input[0], *kv_side, packs[1])
        ring_in = {s: to_ring(ring_out[s], s) for s in RING_ORDER}
        ring_in = [ring_out[0]] + [ring_in[s] for s in (1, 2, 3)]

    with jax.named_scope("inputs_side"):
        input_own = call(join_inputs_kernel, [shape(RING * BLK, quarter)], 0, RING, n_any=3)(
            *ring_in, *packs[1:]
        )[0]
        input_y = to_side(input_own, 2)

    with jax.named_scope("attention"):
        outs = attention_call(place, parents, ring_in, packs, input_own)
        dq_near, dq_far, grad_own, grad_parts = outs[0], outs[1], outs[2], outs[3:]

    with jax.named_scope("kv_gradients"):
        received = [to_ring(grad_parts[s - 1], -s) for s in RING_ORDER]
        grad_total = call(total_kernel, [shape(ROWS)], 0, RING)(grad_own, *received)[0]
        grads = [grad_total] + [to_ring(grad_total, s) for s in RING_ORDER]

    with jax.named_scope("to_core"):
        core_out, side_out = call(
            relay_inputs_kernel,
            [shape(2 * RING * BLK, quarter + HEAD_SIZE), shape(2 * ROWS + 4 * BLK)],
            0,
            5,
        )(input_own, input_y, dq_near, dq_far, grad_total)
        core = to_side(core_out, 1)

    with jax.named_scope("own_gradients"):
        side = to_side(side_out, 2)
        crossed = to_side(call(relay_outputs_kernel, [shape(ROWS + 4 * BLK)], 0, 2)(grad_total, side)[0], 1)
        grad_queries, grad_keys, grad_values = call(
            join_kernel,
            [shape(BLK, QUERY_HEADS * HEAD_SIZE)] + [shape(BLK, KEY_VALUE_HEADS * HEAD_SIZE)] * 2,
            1,
            5,
        )(place, dq_near, core, side, crossed, grad_total)

    with jax.named_scope("projection"):
        partial = call(
            projection_kernel,
            [shape(quarter, 2 * HEAD_SIZE)],
            0,
            RING + 3,
            scratch=[
                pltpu.VMEM((SIDE, 2 * BLK, RING * BLK), BF16),
                pltpu.VMEM((2 * BLK, quarter), F32),
            ],
        )(*grads, input_own, input_y, core)[0]

    with jax.named_scope("projection_sum"):
        groups = [
            [d * RING * SIDE + r * SIDE + g for d in range(trees) for g in range(SIDE)]
            for r in range(RING)
        ]
        swapped = lax.all_to_all(
            partial.reshape(trees * SIDE, share, 2 * HEAD_SIZE),
            ("dp", "ctx"),
            0,
            0,
            axis_index_groups=groups,
            tiled=True,
        )
        summed = jnp.sum(swapped.reshape(trees, SIDE, share, 2, HEAD_SIZE).astype(F32), axis=0)
        grad_kv_weight = summed.transpose(1, 2, 0, 3).reshape(share, 2 * KEY_VALUE_HEADS * HEAD_SIZE)

    return grad_queries[None], grad_keys[None], grad_values[None], grad_kv_weight


def solution(mesh):
    in_specs = (
        P("dp", "ctx", None),
        P("dp", "ctx", None),
        P("dp", "ctx", None),
        P("dp", "ctx", None),
        P("dp", "ctx", None),
        P("dp", None, "ctx"),
        P("dp", "ctx", None),
        P("dp", None),
    )
    out_specs = (
        P("dp", "ctx", None),
        P("dp", "ctx", None),
        P("dp", "ctx", None),
        P(("dp", "ctx"), None),
    )
    return jax.shard_map(
        functools.partial(local, trees=mesh.shape["dp"]),
        mesh=mesh,
        in_specs=in_specs,
        out_specs=out_specs,
        check_vma=False,
    )
```

time: 993 us -> 137 us (0.14)
  waiting for transfers between devices: 852 us -> 58.9 us
  local copies, waits for them, and re-layouts: 69.1 us -> 3.81 us
  starting transfers between devices: 0.38 us -> 44.5 us
  matrix products: 43.3 us -> 0 us
  Pallas kernels: 0 us -> 25.4 us
  between operations: 13.9 us -> 0.85 us
    unnamed x6 -> x0, waiting for transfers between devices: 665 us -> none
    reduce_scatter x2 -> x0, waiting for transfers between devices: 126 us -> none  [the longest x1 67.2 us: local(): lax.psum_scatter(key_grad_out, 'ctx', scatter_dimension=0, tiled=True)]
    all_gather x2 -> x0, waiting for transfers between devices: 60.2 us -> none  [the longest x1 31.8 us: local(): value_portion = lax.all_gather(value_tensor, 'ctx', axis=1, tiled=True)]
    ppermute x0 -> x19, waiting for transfers between devices: none -> 51.6 us  [the longest x10 27.9 us: to_side(): return lax.ppermute(x, 'ctx', side_perm(k))]
    dot_general x31 -> x0, matrix products: 43.3 us -> none  [the longest x4 11.1 us: key_block(): jnp.einsum('tkgd,nkd->kgtn', gradient_by_head, value_row_view, preferred_...]
    unnamed x20 -> x26, local copies, waits for them, and re-layouts: 38.1 us -> 1.15 us
    ppermute x0 -> x19, starting transfers between devices: none -> 36.4 us  [the longest x9 26.9 us: to_ring(): return lax.ppermute(x, 'ctx', ring_perm(s % RING))]
    pallas_call x0 -> x10, Pallas kernels: none -> 25.4 us  [the longest x1 10.3 us: attention_call(): call(attention_kernel, [shape(2 * ROWS)] * 2 + [shape(ROWS, kind=F32)] +...]
  transfers between devices with their start and end apart: 5 -> 20, of which waited for: 5 -> 9; matrix products, arithmetic and copies ran while one was open for 2% -> 0% of each run, Pallas kernels for 0% -> 12%
where the time goes in v1:
time: 137 us; the launch traced here: 135 us
  waiting for transfers between devices  58.9 us (43%)
  starting transfers between devices  44.5 us (32%)
  Pallas kernels  25.4 us (19%)
  local copies, waits for them, and re-layouts  3.81 us (3%)
    ppermute x10, waiting for transfers between devices, to_side(): return lax.ppermute(x, 'ctx', side_perm(k))  27.9 us
    ppermute x9, starting transfers between devices, to_ring(): return lax.ppermute(x, 'ctx', ring_perm(s % RING))  26.9 us
    ppermute x9, waiting for transfers between devices, to_ring(): return lax.ppermute(x, 'ctx', ring_perm(s % RING))  23.7 us
    pallas_call x1, Pallas kernels, attention_call(): call(attention_kernel, [shape(2 * ROWS)] * 2 + [shape(ROWS, kind=F32)] +...  10.3 us
    ppermute x10, starting transfers between devices, to_side(): return lax.ppermute(x, 'ctx', side_perm(k))  9.49 us
    all_to_all x1, starting transfers between devices, local(): lax.all_to_all(partial.reshape(trees * SIDE, share, 2 * HEAD_SIZE), ('dp'...  8.09 us
    all_to_all x1, waiting for transfers between devices, local(): lax.all_to_all(partial.reshape(trees * SIDE, share, 2 * HEAD_SIZE), ('dp'...  7.34 us
    pallas_call x1, Pallas kernels, split_queries(): pl.pallas_call(split_queries_kernel, out_shape=[shape(PACK)] * SIDE, grid...  5.49 us
  transfers between devices with their start and end apart: 20, of which 9 were waited for; matrix products, arithmetic and copies ran while one was open for 0% of the time, Pallas kernels for 12%

profile of v1, /device:TPU:1, one launch (start us, length us, event | category | flops | bytes accessed | tf_op | source)
XLA Modules:
  0.0 134.6 jit_solution(10245096693542814235)
XLA Ops:
  1.2 1.7 %keys_values.1 = (bf16[256,128]{1,0:T(8,128)(2,1)}, bf16[256,128]{1,0:T(8,128)(2,1)}, bf16[256,128]{1,0:T(8,128)(2,1)}, bf16[256,128]{1,0:T(8,128)(2,1)}) custom-call(s32[2]{0:T(128)} %pad_add_fusion.place, bf16[128,512]{1,0:T(8,128)(2,1)} %bitcast.20, bf16[128,512]{1,0:T(8,128)(2,1)} %bitcast.21), custom_call_target="tpu_custom_call" | custom-call | tf_op jit(solution)/shard_map/keys_values/pallas_call | solution.py:348
  3.0 5.5 %queries.1 = (bf16[2080,128]{1,0:T(8,128)(2,1)}, bf16[2080,128]{1,0:T(8,128)(2,1)}, bf16[2080,128]{1,0:T(8,128)(2,1)}, bf16[2080,128]{1,0:T(8,128)(2,1)}) custom-call(s32[2]{0:T(128)} %pad_add_fusion.place, bf16[128,4096]{1,0:T(8,128)(2,1)} %bitcast.16, bf16[128,4096]{1,0:T(8,128)(2,1)} %bitcast.17, bf16[128,4096]{1,0:T(8,128)(2,1)} %bitcast.18, ...), custom_call_target="tpu_custom_call" | custom-call | bytes 33554432 | tf_op jit(solution)/shard_map/queries/pallas_call | solution.py:94
  8.5 1.5 %collective-permute-start.3 = (bf16[2080,128]{1,0:T(8,128)(2,1)}, bf16[2080,128]{1,0:T(8,128)(2,1)S(1)}, u32[]{:S(2)}, u32[]{:S(2)}) collective-permute-start(bf16[2080,128]{1,0:T(8,128)(2,1)} %get-tuple-element.31), channel_id=1, source_target_pairs={{0,1},{1,0},{2,3},{3,2},{4,5},{5,4},{6,7},{7,6},{8,9},{9,8},{10,11... | collective-permute-start | bytes 1597448 | tf_op jit(solution)/shard_map/queries/ppermute | solution.py:342
  10.1 1.4 %collective-permute-start.1 = (bf16[256,128]{1,0:T(8,128)(2,1)S(1)}, bf16[256,128]{1,0:T(8,128)(2,1)S(1)}, u32[]{:S(2)}, u32[]{:S(2)}) collective-permute-start(bf16[256,128]{1,0:T(8,128)(2,1)S(1)} %copy-done.12), channel_id=1, source_target_pairs={{0,2},{1,3},{2,0},{3,1},{4,6},{5,7},{6,4},{7,5},{8,10},{9,11},{10,... | collective-permute-start | bytes 196616 | tf_op jit(solution)/shard_map/keys_values/ppermute | solution.py:342
  13.2 2.9 %collective-permute-done.2.refs_3_ = bf16[256,128]{1,0:T(8,128)(2,1)S(1)} collective-permute-done((bf16[256,128]{1,0:T(8,128)(2,1)S(1)}, bf16[256,128]{1,0:T(8,128)(2,1)S(1)}, u32[]{:S(2)}, u32[]{:S(2)}) %collective-permute-start.2) | collective-permute-done | bytes 65568 | tf_op jit(solution)/shard_map/keys_values/ppermute | solution.py:342
  17.4 1.3 collective-permute-start.4
  18.7 2.5 %collective-permute-start.5 = (bf16[128,2304]{1,0:T(8,128)(2,1)S(1)}, bf16[128,2304]{1,0:T(8,128)(2,1)S(1)}, u32[]{:S(2)}, u32[]{:S(2)}) collective-permute-start(bf16[128,2304]{1,0:T(8,128)(2,1)S(1)} %get-tuple-element.34), channel_id=1, source_target_pairs={{0,8},{1,9},{2,10},{3,11},{4,12},{5,13},{6,14},{7,15},{8,0},{9,1},... | collective-permute-start | bytes 1769480 | tf_op jit(solution)/shard_map/ring/ppermute | solution.py:345
  22.9 2.3 %collective-permute-start.8 = (bf16[2080,128]{1,0:T(8,128)(2,1)S(1)}, bf16[2080,128]{1,0:T(8,128)(2,1)S(1)}, u32[]{:S(2)}, u32[]{:S(2)}) collective-permute-start(bf16[2080,128]{1,0:T(8,128)(2,1)S(1)} %copy-done.9), channel_id=1, source_target_pairs={{0,3},{1,2},{2,1},{3,0},{4,7},{5,6},{6,5},{7,4},{8,11},{9,10},{10,... | collective-permute-start | bytes 1597448 | tf_op jit(solution)/shard_map/queries/ppermute | solution.py:342
  25.2 9.5 %collective-permute-done.7.refs_5_.refs_6_ = bf16[2080,128]{1,0:T(8,128)(2,1)S(1)} collective-permute-done((bf16[2080,128]{1,0:T(8,128)(2,1)S(1)}, bf16[2080,128]{1,0:T(8,128)(2,1)S(1)}, u32[]{:S(2)}, u32[]{:S(2)}) %collective-permute-start.7) | collective-permute-done | bytes 532512 | tf_op jit(solution)/shard_map/queries/ppermute | solution.py:342
  34.6 13.0 %collective-permute-done.8.refs_6_.refs_7_ = bf16[2080,128]{1,0:T(8,128)(2,1)S(1)} collective-permute-done((bf16[2080,128]{1,0:T(8,128)(2,1)S(1)}, bf16[2080,128]{1,0:T(8,128)(2,1)S(1)}, u32[]{:S(2)}, u32[]{:S(2)}) %collective-permute-start.8) | collective-permute-done | bytes 532512 | tf_op jit(solution)/shard_map/queries/ppermute | solution.py:342
  48.7 10.3 %attention.1 = (bf16[2048,128]{1,0:T(8,128)(2,1)S(1)}, bf16[2048,128]{1,0:T(8,128)(2,1)S(1)}, f32[1024,128]{1,0:T(8,128)S(1)}, bf16[1024,128]{1,0:T(8,128)(2,1)S...) custom-call(s32[2]{0:T(128)S(1)} %copy-done.6, s32[1,16]{1,0:T(1,128)S(1)} %copy-done.7, ...), custom_call_target="tpu_custom_call" | custom-call | tf_op jit(solution)/shard_map/attention/pallas_call | solution.py:234
  59.0 10.5 %collective-permute-start.10 = (bf16[1024,128]{1,0:T(8,128)(2,1)S(1)}, bf16[1024,128]{1,0:T(8,128)(2,1)S(1)}, u32[]{:S(2)}, u32[]{:S(2)}) collective-permute-start(bf16[1024,128]{1,0:T(8,128)(2,1)S(1)} %get-tuple-element.42), channel_id=1, source_target_pairs={{0,8},{1,9},{2,10},{3,11},{4,12},{5,13},{6,14},{7,15},{8,0},{9,1},... | collective-permute-start | bytes 786440 | tf_op jit(solution)/shard_map/kv_gradients/ppermute | solution.py:345
  69.5 7.8 %collective-permute-start.11 = (bf16[1024,128]{1,0:T(8,128)(2,1)S(1)}, bf16[1024,128]{1,0:T(8,128)(2,1)S(1)}, u32[]{:S(2)}, u32[]{:S(2)}) collective-permute-start(bf16[1024,128]{1,0:T(8,128)(2,1)S(1)} %get-tuple-element.43), channel_id=1, source_target_pairs={{0,12},{1,13},{2,14},{3,15},{4,0},{5,1},{6,2},{7,3},{8,4},{9,5},{1... | collective-permute-start | bytes 786440 | tf_op jit(solution)/shard_map/kv_gradients/ppermute | solution.py:345
  77.8 11.6 %collective-permute-done.11.refs_1_ = bf16[1024,128]{1,0:T(8,128)(2,1)S(1)} collective-permute-done((bf16[1024,128]{1,0:T(8,128)(2,1)S(1)}, bf16[1024,128]{1,0:T(8,128)(2,1)S(1)}, u32[]{:S(2)}, u32[]{:S(2)}) %collective-permute-start.11) | collective-permute-done | bytes 262176 | tf_op jit(solution)/shard_map/kv_gradients/ppermute | solution.py:345
  90.6 1.3 collective-permute-start.13
  93.1 2.1 %collective-permute-start.17 = (bf16[1024,128]{1,0:T(8,128)(2,1)S(1)}, bf16[1024,128]{1,0:T(8,128)(2,1)S(1)}, u32[]{:S(2)}, u32[]{:S(2)}) collective-permute-start(bf16[1024,128]{1,0:T(8,128)(2,1)S(1)} %kv_gradients.1.total.refs_0_), channel_id=1, source_target_pairs={{0,4},{1,5},{2,6},{3,7},{4,8},{5,9},{6,10},{7,11},{8,12},{9,13},{1... | collective-permute-start | bytes 786440 | tf_op jit(solution)/shard_map/kv_gradients/ppermute | solution.py:345
  95.8 5.9 %collective-permute-done.16.refs_1_ = bf16[1024,128]{1,0:T(8,128)(2,1)S(1)} collective-permute-done((bf16[1024,128]{1,0:T(8,128)(2,1)S(1)}, bf16[1024,128]{1,0:T(8,128)(2,1)S(1)}, u32[]{:S(2)}, u32[]{:S(2)}) %collective-permute-start.16) | collective-permute-done | bytes 262176 | tf_op jit(solution)/shard_map/kv_gradients/ppermute | solution.py:345
  101.7 6.2 %collective-permute-done.17.refs_2_ = bf16[1024,128]{1,0:T(8,128)(2,1)S(1)} collective-permute-done((bf16[1024,128]{1,0:T(8,128)(2,1)S(1)}, bf16[1024,128]{1,0:T(8,128)(2,1)S(1)}, u32[]{:S(2)}, u32[]{:S(2)}) %collective-permute-start.17) | collective-permute-done | bytes 262176 | tf_op jit(solution)/shard_map/kv_gradients/ppermute | solution.py:345
  107.9 1.7 %projection.1 = bf16[1280,256]{1,0:T(8,128)(2,1)S(1)} custom-call(bf16[1024,128]{1,0:T(8,128)(2,1)S(1)} %kv_gradients.1.total.refs_0_, bf16[1024,128]{1,0:T(8,128)(2,1)S(1)} %collective-permute-done.16.refs_1_, bf16[1024,128]{1,0:T(8,128)(2,1)S(1)} %collective-permute-done.17.refs_2_, bf16[1024,128]{1,0:T(8,128)(2,1)S(1)} %collective-permute-done.18.refs_3_, ...), custom_call_target="tpu_custom_call" | custom-call | tf_op jit(solution)/shard_map/projection/pallas_call | solution.py:407
  110.4 8.1 %all-to-all-start = ((bf16[32,40,256]{2,1,0:T(8,128)(2,1)}), bf16[32,40,256]{2,1,0:T(8,128)(2,1)}, u32[]{:S(2)}, u32[]{:S(2)}) async-start(bf16[32,40,256]{2,1,0:T(8,128)(2,1)} %bitcast.14), calls=%async_computation | async-start | bytes 1310720 | tf_op jit(solution)/shard_map/projection_sum/all_to_all | solution.py:423
  120.1 1.4 %collective-permute-done.15.crossed = bf16[1536,128]{1,0:T(8,128)(2,1)S(1)} collective-permute-done((bf16[1536,128]{1,0:T(8,128)(2,1)S(1)}, bf16[1536,128]{1,0:T(8,128)(2,1)S(1)}, u32[]{:S(2)}, u32[]{:S(2)}) %collective-permute-start.15) | collective-permute-done | bytes 393248 | tf_op jit(solution)/shard_map/own_gradients/ppermute | solution.py:342
  121.5 2.5 %own_gradients.3 = (bf16[128,4096]{1,0:T(8,128)(2,1)}, bf16[128,512]{1,0:T(8,128)(2,1)}, bf16[128,512]{1,0:T(8,128)(2,1)}) custom-call(s32[2]{0:T(128)S(1)} %copy-done.6, bf16[2048,128]{1,0:T(8,128)(2,1)S(1)} %copy-done.2, bf16[1024,1408]{1,0:T(8,128)(2,1)S(1)} %collective-permute-done.13.core.refs_6_, bf16[2560,128]{1,0:T(8,128)(2,1)} %collective-permute-done.14.side, ...), custom_call_target="tpu_custom_call" | custom-call | tf_op jit(solution)/shard_map/own_gradients/pallas_call | solution.py:399
  124.0 7.3 %all-to-all-done = bf16[32,40,256]{2,1,0:T(8,128)(2,1)} async-done(((bf16[32,40,256]{2,1,0:T(8,128)(2,1)}), bf16[32,40,256]{2,1,0:T(8,128)(2,1)}, u32[]{:S(2)}, u32[]{:S(2)}) %all-to-all-start) | async-done | bytes 655392 | tf_op jit(solution)/shard_map/projection_sum/all_to_all | solution.py:423
  131.3 1.9 %reshape.19 = f32[8,4,40,2,128]{4,3,2,1,0:T(2,128)S(1)} reshape(bf16[32,40,256]{2,1,0:T(8,128)(2,1)} %all-to-all-done) | data formatting | bytes 1966080 | tf_op jit(solution)/shard_map/projection_sum/convert_element_type | solution.py:431
  (57 shorter events, 13.7 us)
Async XLA Ops:
  2.9 13.2 %copy-start.3 = (bf16[1,128,5120]{2,1,0:T(8,128)(2,1)S(1)}, bf16[1,128,5120]{2,1,0:T(8,128)(2,1)}, u32[]{:S(2)}) copy-start(bf16[1,128,5120]{2,1,0:T(8,128)(2,1)} %param.14) | copy-start | bytes 3932164
  8.5 13.8 %copy-start.10 = (bf16[2080,128]{1,0:T(8,128)(2,1)S(1)}, bf16[2080,128]{1,0:T(8,128)(2,1)}, u32[]{:S(2)}) copy-start(bf16[2080,128]{1,0:T(8,128)(2,1)} %get-tuple-element.37) | copy-start | bytes 1597444
  8.5 14.4 %copy-start.9 = (bf16[2080,128]{1,0:T(8,128)(2,1)S(1)}, bf16[2080,128]{1,0:T(8,128)(2,1)}, u32[]{:S(2)}) copy-start(bf16[2080,128]{1,0:T(8,128)(2,1)} %get-tuple-element.38) | copy-start | bytes 1597444
  8.5 7.7 %collective-permute-start.3 = (bf16[2080,128]{1,0:T(8,128)(2,1)}, bf16[2080,128]{1,0:T(8,128)(2,1)S(1)}, u32[]{:S(2)}, u32[]{:S(2)}) collective-permute-start(bf16[2080,128]{1,0:T(8,128)(2,1)} %get-tuple-element.31), channel_id=1, source_target_pairs={{0,1},{1,0},{2,3},{3,2},{4,5},{5,4},{6,7},{7,6},{8,9},{9,8},{10,11... | collective-permute-start | bytes 1597448 | tf_op jit(solution)/shard_map/queries/ppermute | solution.py:342
  10.0 2.2 %collective-permute-start = (bf16[256,128]{1,0:T(8,128)(2,1)S(1)}, bf16[256,128]{1,0:T(8,128)(2,1)S(1)}, u32[]{:S(2)}, u32[]{:S(2)}) collective-permute-start(bf16[256,128]{1,0:T(8,128)(2,1)S(1)} %copy-done.8), channel_id=1, source_target_pairs={{0,1},{1,0},{2,3},{3,2},{4,5},{5,4},{6,7},{7,6},{8,9},{9,8},{10,11... | collective-permute-start | bytes 196616 | tf_op jit(solution)/shard_map/keys_values/ppermute | solution.py:342
  10.1 3.1 %collective-permute-start.1 = (bf16[256,128]{1,0:T(8,128)(2,1)S(1)}, bf16[256,128]{1,0:T(8,128)(2,1)S(1)}, u32[]{:S(2)}, u32[]{:S(2)}) collective-permute-start(bf16[256,128]{1,0:T(8,128)(2,1)S(1)} %copy-done.12), channel_id=1, source_target_pairs={{0,2},{1,3},{2,0},{3,1},{4,6},{5,7},{6,4},{7,5},{8,10},{9,11},{10,... | collective-permute-start | bytes 196616 | tf_op jit(solution)/shard_map/keys_values/ppermute | solution.py:342
  11.5 4.7 %collective-permute-start.2 = (bf16[256,128]{1,0:T(8,128)(2,1)S(1)}, bf16[256,128]{1,0:T(8,128)(2,1)S(1)}, u32[]{:S(2)}, u32[]{:S(2)}) collective-permute-start(bf16[256,128]{1,0:T(8,128)(2,1)S(1)} %copy-done.11), channel_id=1, source_target_pairs={{0,3},{1,2},{2,1},{3,0},{4,7},{5,6},{6,5},{7,4},{8,11},{9,10},{10,... | collective-permute-start | bytes 196616 | tf_op jit(solution)/shard_map/keys_values/ppermute | solution.py:342
  17.4 30.3 %collective-permute-start.4 = (bf16[128,2304]{1,0:T(8,128)(2,1)S(1)}, bf16[128,2304]{1,0:T(8,128)(2,1)S(1)}, u32[]{:S(2)}, u32[]{:S(2)}) collective-permute-start(bf16[128,2304]{1,0:T(8,128)(2,1)S(1)} %get-tuple-element.33), channel_id=1, source_target_pairs={{0,4},{1,5},{2,6},{3,7},{4,8},{5,9},{6,10},{7,11},{8,12},{9,13},{1... | collective-permute-start | bytes 1769480 | tf_op jit(solution)/shard_map/ring/ppermute | solution.py:345
  18.7 29.0 %collective-permute-start.5 = (bf16[128,2304]{1,0:T(8,128)(2,1)S(1)}, bf16[128,2304]{1,0:T(8,128)(2,1)S(1)}, u32[]{:S(2)}, u32[]{:S(2)}) collective-permute-start(bf16[128,2304]{1,0:T(8,128)(2,1)S(1)} %get-tuple-element.34), channel_id=1, source_target_pairs={{0,8},{1,9},{2,10},{3,11},{4,12},{5,13},{6,14},{7,15},{8,0},{9,1},... | collective-permute-start | bytes 1769480 | tf_op jit(solution)/shard_map/ring/ppermute | solution.py:345
  21.1 26.5 %collective-permute-start.6 = (bf16[128,2304]{1,0:T(8,128)(2,1)S(1)}, bf16[128,2304]{1,0:T(8,128)(2,1)S(1)}, u32[]{:S(2)}, u32[]{:S(2)}) collective-permute-start(bf16[128,2304]{1,0:T(8,128)(2,1)S(1)} %get-tuple-element.35), channel_id=1, source_target_pairs={{0,12},{1,13},{2,14},{3,15},{4,0},{5,1},{6,2},{7,3},{8,4},{9,5},{1... | collective-permute-start | bytes 1769480 | tf_op jit(solution)/shard_map/ring/ppermute | solution.py:345
  22.3 12.4 %collective-permute-start.7 = (bf16[2080,128]{1,0:T(8,128)(2,1)S(1)}, bf16[2080,128]{1,0:T(8,128)(2,1)S(1)}, u32[]{:S(2)}, u32[]{:S(2)}) collective-permute-start(bf16[2080,128]{1,0:T(8,128)(2,1)S(1)} %copy-done.10), channel_id=1, source_target_pairs={{0,2},{1,3},{2,0},{3,1},{4,6},{5,7},{6,4},{7,5},{8,10},{9,11},{10,... | collective-permute-start | bytes 1597448 | tf_op jit(solution)/shard_map/queries/ppermute | solution.py:342
  22.9 24.8 %collective-permute-start.8 = (bf16[2080,128]{1,0:T(8,128)(2,1)S(1)}, bf16[2080,128]{1,0:T(8,128)(2,1)S(1)}, u32[]{:S(2)}, u32[]{:S(2)}) collective-permute-start(bf16[2080,128]{1,0:T(8,128)(2,1)S(1)} %copy-done.9), channel_id=1, source_target_pairs={{0,3},{1,2},{2,1},{3,0},{4,7},{5,6},{6,5},{7,4},{8,11},{9,10},{10,... | collective-permute-start | bytes 1597448 | tf_op jit(solution)/shard_map/queries/ppermute | solution.py:342
  47.8 41.7 %collective-permute-start.9 = (bf16[512,1280]{1,0:T(8,128)(2,1)S(1)}, bf16[512,1280]{1,0:T(8,128)(2,1)S(1)}, u32[]{:S(2)}, u32[]{:S(2)}) collective-permute-start(bf16[512,1280]{1,0:T(8,128)(2,1)S(1)} %inputs_side.1.refs_8_.own.refs_4_), channel_id=1, source_target_pairs={{0,2},{1,3},{2,0},{3,1},{4,6},{5,7},{6,4},{7,5},{8,10},{9,11},{10,... | collective-permute-start | bytes 3932168 | tf_op jit(solution)/shard_map/inputs_side/ppermute | solution.py:342
  59.0 31.6 %copy-start.1 = (bf16[2048,128]{1,0:T(8,128)(2,1)}, bf16[2048,128]{1,0:T(8,128)(2,1)S(1)}, u32[]{:S(2)}) copy-start(bf16[2048,128]{1,0:T(8,128)(2,1)S(1)} %get-tuple-element.39.dq_near.near) | copy-start | bytes 1572868
  59.0 18.8 %collective-permute-start.10 = (bf16[1024,128]{1,0:T(8,128)(2,1)S(1)}, bf16[1024,128]{1,0:T(8,128)(2,1)S(1)}, u32[]{:S(2)}, u32[]{:S(2)}) collective-permute-start(bf16[1024,128]{1,0:T(8,128)(2,1)S(1)} %get-tuple-element.42), channel_id=1, source_target_pairs={{0,8},{1,9},{2,10},{3,11},{4,12},{5,13},{6,14},{7,15},{8,0},{9,1},... | collective-permute-start | bytes 786440 | tf_op jit(solution)/shard_map/kv_gradients/ppermute | solution.py:345
  69.5 19.9 %collective-permute-start.11 = (bf16[1024,128]{1,0:T(8,128)(2,1)S(1)}, bf16[1024,128]{1,0:T(8,128)(2,1)S(1)}, u32[]{:S(2)}, u32[]{:S(2)}) collective-permute-start(bf16[1024,128]{1,0:T(8,128)(2,1)S(1)} %get-tuple-element.43), channel_id=1, source_target_pairs={{0,12},{1,13},{2,14},{3,15},{4,0},{5,1},{6,2},{7,3},{8,4},{9,5},{1... | collective-permute-start | bytes 786440 | tf_op jit(solution)/shard_map/kv_gradients/ppermute | solution.py:345
  77.3 12.1 %collective-permute-start.12 = (bf16[1024,128]{1,0:T(8,128)(2,1)S(1)}, bf16[1024,128]{1,0:T(8,128)(2,1)S(1)}, u32[]{:S(2)}, u32[]{:S(2)}) collective-permute-start(bf16[1024,128]{1,0:T(8,128)(2,1)S(1)} %get-tuple-element.44), channel_id=1, source_target_pairs={{0,4},{1,5},{2,6},{3,7},{4,8},{5,9},{6,10},{7,11},{8,12},{9,13},{1... | collective-permute-start | bytes 786440 | tf_op jit(solution)/shard_map/kv_gradients/ppermute | solution.py:345
  90.6 17.3 %collective-permute-start.13 = (bf16[1024,1408]{1,0:T(8,128)(2,1)S(1)}, bf16[1024,1408]{1,0:T(8,128)(2,1)S(1)}, u32[]{:S(2)}, u32[]{:S(2)}) collective-permute-start(bf16[1024,1408]{1,0:T(8,128)(2,1)S(1)} %get-tuple-element.45), channel_id=1, source_target_pairs={{0,1},{1,0},{2,3},{3,2},{4,5},{5,4},{6,7},{7,6},{8,9},{9,8},{10,11... | collective-permute-start | bytes 8650760 | tf_op jit(solution)/shard_map/to_core/ppermute | solution.py:342
  91.9 26.6 %collective-permute-start.14 = (bf16[2560,128]{1,0:T(8,128)(2,1)}, bf16[2560,128]{1,0:T(8,128)(2,1)}, u32[]{:S(2)}, u32[]{:S(2)}) collective-permute-start(bf16[2560,128]{1,0:T(8,128)(2,1)} %get-tuple-element.46), channel_id=1, source_target_pairs={{0,2},{1,3},{2,0},{3,1},{4,6},{5,7},{6,4},{7,5},{8,10},{9,11},{10,... | collective-permute-start | bytes 1966088 | tf_op jit(solution)/shard_map/own_gradients/ppermute | solution.py:342
  92.5 9.2 %collective-permute-start.16 = (bf16[1024,128]{1,0:T(8,128)(2,1)S(1)}, bf16[1024,128]{1,0:T(8,128)(2,1)S(1)}, u32[]{:S(2)}, u32[]{:S(2)}) collective-permute-start(bf16[1024,128]{1,0:T(8,128)(2,1)S(1)} %kv_gradients.1.total.refs_0_), channel_id=1, source_target_pairs={{0,8},{1,9},{2,10},{3,11},{4,12},{5,13},{6,14},{7,15},{8,0},{9,1},... | collective-permute-start | bytes 786440 | tf_op jit(solution)/shard_map/kv_gradients/ppermute | solution.py:345
  93.1 14.7 %collective-permute-start.17 = (bf16[1024,128]{1,0:T(8,128)(2,1)S(1)}, bf16[1024,128]{1,0:T(8,128)(2,1)S(1)}, u32[]{:S(2)}, u32[]{:S(2)}) collective-permute-start(bf16[1024,128]{1,0:T(8,128)(2,1)S(1)} %kv_gradients.1.total.refs_0_), channel_id=1, source_target_pairs={{0,4},{1,5},{2,6},{3,7},{4,8},{5,9},{6,10},{7,11},{8,12},{9,13},{1... | collective-permute-start | bytes 786440 | tf_op jit(solution)/shard_map/kv_gradients/ppermute | solution.py:345
  95.2 12.6 %collective-permute-start.18 = (bf16[1024,128]{1,0:T(8,128)(2,1)S(1)}, bf16[1024,128]{1,0:T(8,128)(2,1)S(1)}, u32[]{:S(2)}, u32[]{:S(2)}) collective-permute-start(bf16[1024,128]{1,0:T(8,128)(2,1)S(1)} %kv_gradients.1.total.refs_0_), channel_id=1, source_target_pairs={{0,12},{1,13},{2,14},{3,15},{4,0},{5,1},{6,2},{7,3},{8,4},{9,5},{1... | collective-permute-start | bytes 786440 | tf_op jit(solution)/shard_map/kv_gradients/ppermute | solution.py:345
  110.4 20.9 %all-to-all-start = ((bf16[32,40,256]{2,1,0:T(8,128)(2,1)}), bf16[32,40,256]{2,1,0:T(8,128)(2,1)}, u32[]{:S(2)}, u32[]{:S(2)}) async-start(bf16[32,40,256]{2,1,0:T(8,128)(2,1)} %bitcast.14), calls=%async_computation | async-start | bytes 1310720 | tf_op jit(solution)/shard_map/projection_sum/all_to_all | solution.py:423
  119.7 1.8 %collective-permute-start.15 = (bf16[1536,128]{1,0:T(8,128)(2,1)S(1)}, bf16[1536,128]{1,0:T(8,128)(2,1)S(1)}, u32[]{:S(2)}, u32[]{:S(2)}) collective-permute-start(bf16[1536,128]{1,0:T(8,128)(2,1)S(1)} %own_gradients.2), channel_id=1, source_target_pairs={{0,1},{1,0},{2,3},{3,2},{4,5},{5,4},{6,7},{7,6},{8,9},{9,8},{10,11... | collective-permute-start | bytes 1179656 | tf_op jit(solution)/shard_map/own_gradients/ppermute | solution.py:342
  (9 other events, 55.0 us)

commit v2 on v1

v2 whole, which is shorter than its diff:
```python
import functools

import jax
import jax.numpy as jnp
from jax import lax
from jax.experimental import pallas as pl
from jax.experimental.pallas import tpu as pltpu
from jax.sharding import PartitionSpec as P

QUERY_HEADS = 32
KEY_VALUE_HEADS = 4
HEAD_SIZE = 128
BLK = 128
GROUP = QUERY_HEADS // KEY_VALUE_HEADS
RING = 4
SIDE = 4
TREES = 8
TALL = 1024
ROWS = GROUP * BLK
PACK = 2 * ROWS + 272
SCALE = HEAD_SIZE ** (-0.5)
RING_ORDER = (2, 1, 3)
LOG2E = 1.4426950408889634
LSE_SCALE = HEAD_SIZE**0.5
F32 = jnp.float32
BF16 = jnp.bfloat16
MIB = 1 << 20


def side_perm(k):
    return [(c, c ^ k) for c in range(RING * SIDE)]


def ring_perm(s):
    return [(c, ((c // SIDE + s) % RING) * SIDE + c % SIDE) for c in range(RING * SIDE)]


def smem():
    return pl.BlockSpec(memory_space=pltpu.SMEM)


def vmem():
    return pl.BlockSpec(memory_space=pltpu.VMEM)


def call(kernel, out_shape, n_smem, n_vmem, n_any=0, scratch=(), moved=0, limit=20):
    return pl.pallas_call(
        kernel,
        out_shape=out_shape,
        in_specs=[smem()] * n_smem + [vmem()] * n_vmem + [pl.BlockSpec(memory_space=pl.ANY)] * n_any,
        out_specs=[vmem()] * len(out_shape),
        scratch_shapes=list(scratch),
        compiler_params=pltpu.CompilerParams(vmem_limit_bytes=limit * MIB),
        cost_estimate=pl.CostEstimate(flops=0, bytes_accessed=moved, transcendentals=0),
    )


def split_kv_kernel(place, key_ref, value_ref, *outs):
    own = place[1]
    for k, out in enumerate(outs):
        col = pl.multiple_of((own ^ k) * HEAD_SIZE, HEAD_SIZE)
        out[0:BLK, :] = key_ref[:, pl.ds(col, HEAD_SIZE)]
        out[BLK:, :] = value_ref[:, pl.ds(col, HEAD_SIZE)]


def split_queries_kernel(place, query_ref, gradient_ref, output_ref, lse_ref, after, *outs):
    lane = lax.broadcasted_iota(jnp.int32, (BLK, 128), 1)
    columns = jnp.zeros((BLK, 128), F32)
    for h in range(GROUP):
        cols = slice(h * HEAD_SIZE, (h + 1) * HEAD_SIZE)
        prod = gradient_ref[:, cols].astype(F32) * output_ref[:, cols].astype(F32)
        columns = jnp.where(lane == h, jnp.sum(prod, axis=1, keepdims=True), columns)
    delta = columns.T[0:GROUP]
    lse = lse_ref[...] * LSE_SCALE

    def split(rows):
        high = rows.astype(BF16)
        low = (rows - high.astype(F32)).astype(BF16)
        return jnp.concatenate([high, low], axis=0)

    for k, out in enumerate(outs):

        @pl.when(pl.program_id(0) == k)
        def _(out=out):
            for h in range(GROUP):
                cols = slice(h * HEAD_SIZE, (h + 1) * HEAD_SIZE)
                out[h * BLK : (h + 1) * BLK, :] = query_ref[:, cols]
                out[ROWS + h * BLK : ROWS + (h + 1) * BLK, :] = gradient_ref[:, cols]
            out[2 * ROWS : 2 * ROWS + 16, :] = split(lse)
            out[2 * ROWS + 16 : 2 * ROWS + 32, :] = split(delta)


def split_queries(place, queries, gradient, output, lse, after, first):
    count = SIDE // 2
    wide = pl.BlockSpec((BLK, GROUP * HEAD_SIZE), lambda k, place: (0, place[1] ^ (first + k)))
    return pl.pallas_call(
        split_queries_kernel,
        out_shape=[shape(PACK)] * count,
        grid_spec=pltpu.PrefetchScalarGridSpec(
            num_scalar_prefetch=1,
            grid=(count,),
            in_specs=[
                wide,
                wide,
                wide,
                pl.BlockSpec((GROUP, BLK), lambda k, place: (place[1] ^ (first + k), 0)),
                pl.BlockSpec(memory_space=pl.ANY),
            ],
            out_specs=[pl.BlockSpec((PACK, HEAD_SIZE), lambda k, place: (0, 0))] * count,
        ),
        compiler_params=pltpu.CompilerParams(vmem_limit_bytes=56 * MIB),
        cost_estimate=pl.CostEstimate(flops=0, bytes_accessed=32 * MIB, transcendentals=0),
    )(place, queries, gradient, output, lse, after)


def ring_pack_kernel(place, inputs, *refs):
    kv, refs = refs[:SIDE], refs[SIDE + 1 :]
    outs, token, shares = refs[:RING], refs[RING], refs[RING + 1]
    token[...] = jnp.zeros_like(token)
    _, _, quarter = shares.shape
    piece = quarter // TREES
    for r in range(RING):
        shares[r] = jnp.concatenate(
            [inputs[:, (d * RING + r) * piece : (d * RING + r + 1) * piece] for d in range(TREES)], axis=1
        )
    for s, out in enumerate(outs):
        out[:, 0:quarter] = shares[(place[0] + s) % RING]
        for k in range(SIDE):
            for half in range(2):
                col = quarter + (2 * k + half) * HEAD_SIZE
                out[:, col : col + HEAD_SIZE] = kv[k][half * BLK : (half + 1) * BLK, :]


def attention_kernel(place, parents, *refs):
    ring_in, packs, refs = refs[:RING], refs[RING : RING + SIDE], refs[RING + SIDE + 1 :]
    dq_outs, grad_outs, refs = refs[:2], refs[2 : 2 + RING], refs[2 + RING :]
    kv, kv_t, pack, query_t, gradient_t, terms, dq_acc, dq, acc, stage_own, stage, kv_sem, pack_sem, out_sem = refs
    ring, own = place[0], place[1]
    start = ring_in[0].shape[1] - 2 * SIDE * HEAD_SIZE

    loads = []
    for s in range(RING):
        for k in range(SIDE):
            for half in range(2):
                col = start + (2 * k + half) * HEAD_SIZE
                loads.append(
                    pltpu.make_async_copy(
                        ring_in[s].at[:, pl.ds(col, HEAD_SIZE)],
                        kv.at[s * SIDE + k, pl.ds(half * BLK, BLK), :],
                        kv_sem.at[len(loads)],
                    )
                )
    pack_loads = [pltpu.make_async_copy(packs[k], pack.at[k], pack_sem.at[k]) for k in range(SIDE)]
    for load in loads + pack_loads:
        load.start()
    acc[...] = jnp.zeros_like(acc)
    for load in loads:
        load.wait()

    row = lax.broadcasted_iota(jnp.int32, (BLK, BLK), 0)
    minus_lse = jnp.where(row < 16, -1.0, 0.0).astype(BF16)
    minus_delta = jnp.where((row >= 16) & (row < 32), -1.0, 0.0).astype(BF16)

    @pl.loop(0, RING * SIDE // 4)
    def _(quarter):
        for part in range(4):
            j = quarter * 4 + part
            kv_t[j, 0:BLK, 0:BLK] = kv[j, 0:BLK, :].T
            kv_t[j, 0:BLK, BLK:] = kv[j, BLK:, :].T
            kv_t[j, BLK:, 0:BLK] = minus_lse
            kv_t[j, BLK:, BLK:] = minus_delta

    for load in pack_loads:
        load.wait()

    def store_dq(k):
        place_out = dq_outs[k // 2].at[pl.ds(k % 2 * ROWS, ROWS), :]
        return pltpu.make_async_copy(dq.at[k], place_out, out_sem.at[k])

    def slot_of(at):
        return ((ring - at // SIDE) % RING) * SIDE + ((at % SIDE) ^ own)

    def tile(piece, slots, diagonal):
        n = len(slots) * BLK
        keys = jnp.concatenate([kv[j, 0:BLK, :] for j in slots], axis=0)
        keys_t = jnp.concatenate([kv_t[j, :, 0:BLK] for j in slots], axis=1)
        values_t = jnp.concatenate([kv_t[j, :, BLK:] for j in slots], axis=1)
        dk = dv = None
        for p in range(ROWS // TALL):
            span = slice(p * TALL, (p + 1) * TALL)
            extra = terms[span, :]
            scores = jnp.dot(
                jnp.concatenate([pack[piece, span, :], extra], axis=1), keys_t, preferred_element_type=F32
            )
            prob = jnp.exp2(scores * (SCALE * LOG2E))
            if diagonal:
                query_at = lax.broadcasted_iota(jnp.int32, (TALL, n), 0) % BLK
                key_at = lax.broadcasted_iota(jnp.int32, (TALL, n), 1)
                prob = jnp.where((key_at <= query_at) | (key_at >= BLK), prob, 0.0)
            prob_grad = jnp.dot(
                jnp.concatenate([pack[piece, ROWS + p * TALL : ROWS + (p + 1) * TALL, :], extra], axis=1),
                values_t,
                preferred_element_type=F32,
            )
            dscore = (prob * prob_grad).astype(BF16)
            dv_part = jnp.dot(gradient_t[:, span], prob.astype(BF16), preferred_element_type=F32)
            dk_part = jnp.dot(query_t[:, span], dscore, preferred_element_type=F32)
            dv = dv_part if dv is None else dv + dv_part
            dk = dk_part if dk is None else dk + dk_part
            part = jnp.dot(dscore, keys, preferred_element_type=F32)
            if diagonal:
                dq_acc[span, :] = part
            else:
                dq_acc[span, :] += part
        for m, j in enumerate(slots):
            acc[j, 0:BLK, :] += dk[:, m * BLK : (m + 1) * BLK]
            acc[j, BLK:, :] += dv[:, m * BLK : (m + 1) * BLK]

    @pl.loop(0, SIDE)
    def _(piece):
        lane = lax.broadcasted_iota(jnp.int32, (BLK, 128), 1)
        columns = jnp.concatenate(
            [pack[piece, 2 * ROWS : 2 * ROWS + 32, :].astype(F32), jnp.zeros((BLK - 32, BLK), F32)], axis=0
        ).T
        for h in range(GROUP):
            cols = slice(h * BLK, (h + 1) * BLK)
            query_t[:, cols] = pack[piece, cols, :].T
            gradient_t[:, cols] = pack[piece, ROWS + h * BLK : ROWS + (h + 1) * BLK, :].T
            terms[cols, :] = jnp.where(lane % GROUP == h, columns, 0.0).astype(BF16)

        block = ring * SIDE + (own ^ piece)
        above = lax.while_loop(lambda c: c[0] > 0, lambda c: (parents[0, c[0]], c[1] + 1), (block, 0))[1]
        odd = above % 2 == 1

        @pl.when(odd)
        def _():
            tile(piece, [piece, slot_of(parents[0, block])], True)

        @pl.when(jnp.logical_not(odd))
        def _():
            tile(piece, [piece], True)

        def ancestors(at):
            one = parents[0, at]
            two = parents[0, one]
            tile(piece, [slot_of(one), slot_of(two)], False)
            return two

        def quad(c):
            at, left = c
            one = parents[0, at]
            two = parents[0, one]
            three = parents[0, two]
            four = parents[0, three]
            tile(piece, [slot_of(one), slot_of(two), slot_of(three), slot_of(four)], False)
            return four, left - 4

        start = jnp.where(odd, parents[0, block], block)
        at, left = lax.while_loop(lambda c: c[1] >= 4, quad, (start, above - odd.astype(jnp.int32)))

        @pl.when(left > 0)
        def _():
            ancestors(at)

        dq[piece] = (dq_acc[...] * SCALE).astype(BF16)
        for k in range(SIDE):

            @pl.when(piece == k)
            def _(k=k):
                store_dq(k).start()

    stores = [store_dq(k) for k in range(SIDE)]
    for s in RING_ORDER + (0,):
        for k in range(SIDE):
            dk, dv = acc[s * SIDE + k, 0:BLK, :] * SCALE, acc[s * SIDE + k, BLK:, :]
            at = 2 * k * BLK
            if s == 0:
                stage_own[at : at + BLK, :] = dk.T
                stage_own[at + BLK : at + 2 * BLK, :] = dv.T
            else:
                stage[s - 1, at : at + BLK, :] = dk.astype(BF16).T
                stage[s - 1, at + BLK : at + 2 * BLK, :] = dv.astype(BF16).T
        source = stage_own if s == 0 else stage.at[s - 1]
        stores.append(pltpu.make_async_copy(source, grad_outs[s], out_sem.at[SIDE + s]))
        stores[-1].start()
    for store in stores:
        store.wait()


def attention_call(place, parents, ring_in, packs, *after):
    sum_shape = (RING * SIDE, 2 * BLK, HEAD_SIZE)
    hbm = pl.BlockSpec(memory_space=pl.ANY)
    return pl.pallas_call(
        attention_kernel,
        out_shape=[shape(2 * ROWS), shape(2 * ROWS + 4 * BLK), shape(ROWS, kind=F32)]
        + [shape(ROWS)] * (RING - 1),
        in_specs=[smem()] * 2 + [hbm] * (RING + SIDE + 1),
        out_specs=[hbm] * (2 + RING),
        scratch_shapes=[
            pltpu.VMEM(sum_shape, BF16),
            pltpu.VMEM((RING * SIDE, 2 * HEAD_SIZE, 2 * BLK), BF16),
            pltpu.VMEM((SIDE, PACK, HEAD_SIZE), BF16),
            pltpu.VMEM((HEAD_SIZE, ROWS), BF16),
            pltpu.VMEM((HEAD_SIZE, ROWS), BF16),
            pltpu.VMEM((ROWS, 128), BF16),
            pltpu.VMEM((ROWS, HEAD_SIZE), F32),
            pltpu.VMEM((SIDE, ROWS, HEAD_SIZE), BF16),
            pltpu.VMEM(sum_shape, F32),
            pltpu.VMEM((ROWS, HEAD_SIZE), F32),
            pltpu.VMEM((RING - 1, ROWS, HEAD_SIZE), BF16),
            pltpu.SemaphoreType.DMA((2 * RING * SIDE,)),
            pltpu.SemaphoreType.DMA((SIDE,)),
            pltpu.SemaphoreType.DMA((SIDE + RING,)),
        ],
        compiler_params=pltpu.CompilerParams(vmem_limit_bytes=24 * MIB),
        cost_estimate=pl.CostEstimate(flops=0, bytes_accessed=0, transcendentals=0),
    )(place, parents, *ring_in, *packs, *after)


def total_kernel(grad_own, *refs):
    parts, (total, _, side, sem) = refs[: RING - 1], refs[RING + 2 :]
    value = grad_own[...]
    for part in parts:
        value = value + part[...].astype(F32)
    total[...] = value.astype(BF16)
    store = pltpu.make_async_copy(
        total.at[pl.ds(4 * BLK, 4 * BLK), :], side.at[pl.ds(2 * ROWS, 4 * BLK), :], sem
    )
    store.start()
    store.wait()


def total_call(grad_own, received, inputs, side, after):
    hbm = pl.BlockSpec(memory_space=pl.ANY)
    return pl.pallas_call(
        total_kernel,
        out_shape=[shape(ROWS), shape(*inputs.shape), shape(*side.shape)],
        in_specs=[vmem()] * RING + [hbm] * 3,
        out_specs=[vmem(), hbm, hbm],
        scratch_shapes=[pltpu.SemaphoreType.DMA],
        input_output_aliases={RING: 1, RING + 1: 2},
        compiler_params=pltpu.CompilerParams(vmem_limit_bytes=16 * MIB),
        cost_estimate=pl.CostEstimate(flops=0, bytes_accessed=0, transcendentals=0),
    )(grad_own, *received, inputs, side, after)


def relay_kernel(near, side, total, *rest):
    out = rest[-1]
    out[0:ROWS, :] = side[ROWS : 2 * ROWS, :]
    out[ROWS : ROWS + 2 * BLK, :] = total[2 * BLK : 4 * BLK, :]
    out[ROWS + 2 * BLK : ROWS + 4 * BLK, :] = side[2 * ROWS + 2 * BLK :, :]
    out[ROWS + 4 * BLK :, :] = near[ROWS:, :]


def join_inputs_kernel(*refs):
    pieces, out = refs[:RING], refs[-1]
    for s in range(RING):
        out[s * BLK : (s + 1) * BLK, :] = pieces[s][:, 0 : out.shape[1]]


def projection_kernel(*refs):
    grads = dict(zip((0,) + RING_ORDER, refs[:RING]))
    inputs = refs[RING : RING + SIDE]
    out, grad_t, weight_t, keys, values = refs[RING + SIDE :]
    for s in range(RING):
        for k in range(SIDE):
            at = 2 * k * BLK
            grad_t[k, 0:BLK, s * BLK : (s + 1) * BLK] = grads[s][at : at + BLK, :].T
            grad_t[k, BLK:, s * BLK : (s + 1) * BLK] = grads[s][at + BLK : at + 2 * BLK, :].T
    total = jnp.dot(grad_t[0], inputs[0][...], preferred_element_type=F32)
    for k in range(1, SIDE):
        total = total + jnp.dot(grad_t[k], inputs[k][...], preferred_element_type=F32)
    weight_t[...] = total
    for n in range(keys.shape[0] // BLK):
        rows = slice(n * BLK, (n + 1) * BLK)
        keys[rows, :] = weight_t[0:BLK, rows].T
        values[rows, :] = weight_t[BLK:, rows].T
    count, both, _ = out.shape
    for j in range(count):
        rows = slice(j * (both // 2), (j + 1) * (both // 2))
        out[j] = jnp.concatenate([keys[rows, :], values[rows, :]], axis=0).astype(BF16)


def weight_kernel(parts, out):
    share = out.shape[0]
    for g in range(KEY_VALUE_HEADS):
        total = parts[g].astype(F32)
        for d in range(1, TREES):
            total = total + parts[d * SIDE + g].astype(F32)
        out[:, g * HEAD_SIZE : (g + 1) * HEAD_SIZE] = total[0:share]
        col = (KEY_VALUE_HEADS + g) * HEAD_SIZE
        out[:, col : col + HEAD_SIZE] = total[share:]


def join_kernel(place, near, side, crossed, total, queries, keys, values):
    own = place[1]
    kv_at = ROWS + 4 * BLK
    for h in range(GROUP):
        rows = slice(h * BLK, (h + 1) * BLK)
        last = slice(kv_at + h * BLK, kv_at + (h + 1) * BLK)
        for k, piece in enumerate((near[rows, :], crossed[last, :], side[rows, :], crossed[rows, :])):
            col = pl.multiple_of((own ^ k) * (GROUP * HEAD_SIZE) + h * HEAD_SIZE, HEAD_SIZE)
            queries[:, pl.ds(col, HEAD_SIZE)] = piece
    for k, (ref, at) in enumerate(((total, 0), (crossed, ROWS), (side, 2 * ROWS), (crossed, ROWS + 2 * BLK))):
        col = pl.multiple_of((own ^ k) * HEAD_SIZE, HEAD_SIZE)
        keys[:, pl.ds(col, HEAD_SIZE)] = ref[at : at + BLK, :]
        values[:, pl.ds(col, HEAD_SIZE)] = ref[at + BLK : at + 2 * BLK, :]


def shape(rows, cols=HEAD_SIZE, kind=BF16):
    return jax.ShapeDtypeStruct((rows, cols), kind)


def local(
    queries,
    key_tensor,
    value_tensor,
    attention_output,
    output_gradient,
    logsumexp_rows,
    layer_input,
    parents,
    trees,
):
    width = layer_input.shape[2]
    quarter = width // RING
    share = width // (trees * RING * SIDE)
    at = lax.axis_index("ctx")
    ring, own = at // SIDE, at % SIDE
    place = jnp.stack([ring, own]).astype(jnp.int32)

    def to_side(x, k):
        return lax.ppermute(x, "ctx", side_perm(k))

    def to_ring(x, s):
        return lax.ppermute(x, "ctx", ring_perm(s % RING))

    with jax.named_scope("keys_values"):
        kv_split = call(split_kv_kernel, [shape(2 * BLK)] * SIDE, 1, 2, limit=56)(
            place, key_tensor[0], value_tensor[0]
        )
        kv_side = [kv_split[0]] + [to_side(kv_split[k], k) for k in (1, 2, 3)]

    query_args = (queries[0], output_gradient[0], attention_output[0], logsumexp_rows[0])
    with jax.named_scope("queries_far"):
        far_own = split_queries(place, *query_args, kv_split[1], 2)
        packs_far = [to_side(far_own[k - 2], k) for k in (2, 3)]

    with jax.named_scope("ring"):
        ring_out = call(
            ring_pack_kernel,
            [shape(BLK, quarter + 2 * SIDE * HEAD_SIZE)] * RING + [shape(8, 128, F32)],
            1,
            1 + SIDE,
            n_any=1,
            moved=128 * MIB,
            scratch=[pltpu.VMEM((RING, BLK, quarter), BF16)],
        )(place, layer_input[0], *kv_side, far_own[0])
        ring_in = {s: to_ring(ring_out[s], s) for s in RING_ORDER}
        ring_in = [ring_out[0]] + [ring_in[s] for s in (1, 2, 3)]

    with jax.named_scope("queries_near"):
        near_own = split_queries(place, *query_args, ring_out[RING], 0)
        packs = [near_own[0], to_side(near_own[1], 1)] + packs_far

    with jax.named_scope("inputs_side"):
        input_own = call(join_inputs_kernel, [shape(RING * BLK, quarter)], 0, RING, n_any=3)(
            *ring_in, *packs_far, near_own[0]
        )[0]
        input_y = to_side(input_own, 2)
        input_core = to_side(input_own, 1)

    with jax.named_scope("attention"):
        outs = attention_call(place, parents, ring_in, packs, input_own)
        dq_near, side_out, grad_own, grad_parts = outs[0], outs[1], outs[2], outs[3:]

    with jax.named_scope("kv_gradients"):
        received = [to_ring(grad_parts[s - 1], -s) for s in RING_ORDER]
        grad_total, input_y, side_out = total_call(grad_own, received, input_y, side_out, input_core)
        input_last = to_side(input_y, 1)
        grads = [grad_total] + [to_ring(grad_total, s) for s in RING_ORDER]

    with jax.named_scope("projection"):
        partial = call(
            projection_kernel,
            [jax.ShapeDtypeStruct((trees * SIDE, 2 * share, HEAD_SIZE), BF16)],
            0,
            RING + SIDE,
            scratch=[
                pltpu.VMEM((SIDE, 2 * BLK, RING * BLK), BF16),
                pltpu.VMEM((2 * BLK, quarter), F32),
                pltpu.VMEM((quarter, HEAD_SIZE), F32),
                pltpu.VMEM((quarter, HEAD_SIZE), F32),
            ],
        )(*grads, input_own, input_core, input_y, input_last)[0]

    with jax.named_scope("own_gradients"):
        side = to_side(side_out, 2)
        crossed = to_side(
            call(relay_kernel, [shape(2 * ROWS + 4 * BLK)], 0, 3, n_any=3)(dq_near, side, grad_total, *grads[1:])[0], 1
        )
        grad_queries, grad_keys, grad_values = call(
            join_kernel,
            [shape(BLK, QUERY_HEADS * HEAD_SIZE)] + [shape(BLK, KEY_VALUE_HEADS * HEAD_SIZE)] * 2,
            1,
            4,
            moved=64 * MIB,
        )(place, dq_near, side, crossed, grad_total)

    with jax.named_scope("projection_sum"):
        groups = [
            [d * RING * SIDE + r * SIDE + g for d in range(trees) for g in range(SIDE)]
            for r in range(RING)
        ]
        swapped = lax.all_to_all(partial, ("dp", "ctx"), 0, 0, axis_index_groups=groups, tiled=True)
        grad_kv_weight = call(weight_kernel, [shape(share, 2 * KEY_VALUE_HEADS * HEAD_SIZE, F32)], 0, 1)(swapped)[0]

    return grad_queries[None], grad_keys[None], grad_values[None], grad_kv_weight


def solution(mesh):
    in_specs = (
        P("dp", "ctx", None),
        P("dp", "ctx", None),
        P("dp", "ctx", None),
        P("dp", "ctx", None),
        P("dp", "ctx", None),
        P("dp", None, "ctx"),
        P("dp", "ctx", None),
        P("dp", None),
    )
    out_specs = (
        P("dp", "ctx", None),
        P("dp", "ctx", None),
        P("dp", "ctx", None),
        P(("dp", "ctx"), None),
    )
    return jax.shard_map(
        functools.partial(local, trees=mesh.shape["dp"]),
        mesh=mesh,
        in_specs=in_specs,
        out_specs=out_specs,
        check_vma=False,
    )
```

time: 137 us -> 130 us (0.949); the launches traced: 135 us -> 132 us
  Pallas kernels: 25.4 us -> 24 us
    ppermute x10 -> x11, waiting for transfers between devices: 27.9 us -> 17.2 us  [to_side(): return lax.ppermute(x, 'ctx', side_perm(k))]
    ppermute x9, waiting for transfers between devices: 23.7 us -> 30.4 us  [to_ring(): return lax.ppermute(x, 'ctx', ring_perm(s % RING))]
    all_to_all x1, waiting for transfers between devices: 7.34 us -> 10.8 us  [local(): lax.all_to_all(partial, ('dp', 'ctx'), 0, 0, axis_index_groups=groups, ti...]
    ppermute x9, starting transfers between devices: 26.9 us -> 24.1 us  [to_ring(): return lax.ppermute(x, 'ctx', ring_perm(s % RING))]
    ppermute x10 -> x11, starting transfers between devices: 9.49 us -> 12 us  [to_side(): return lax.ppermute(x, 'ctx', side_perm(k))]
    convert_element_type x1 -> x0, local copies, waits for them, and re-layouts: 1.86 us -> none  [local(): swapped.reshape(trees, SIDE, share, 2, HEAD_SIZE).astype(F32)]
    unnamed x26 -> x20, local copies, waits for them, and re-layouts: 1.15 us -> 2.77 us
    pallas_call x6 -> x7, Pallas kernels: 19.8 us -> 19 us  [the longest x1 8.25 us: attention_call(): pl.pallas_call(attention_kernel, out_shape=[shape(2 * ROWS), shape(2 * RO...]
  transfers between devices with their start and end apart: 20 -> 21, of which waited for: 9 -> 9; matrix products, arithmetic and copies ran while one was open for 0% -> 0% of each run, Pallas kernels for 12% -> 16%
where the time goes in v2:
time: 130 us; the launch traced here: 132 us
  waiting for transfers between devices  58.4 us (45%)
  starting transfers between devices  45.2 us (35%)
  Pallas kernels  24 us (18%)
  local copies, waits for them, and re-layouts  2.77 us (2%)
    ppermute x9, waiting for transfers between devices, to_ring(): return lax.ppermute(x, 'ctx', ring_perm(s % RING))  30.4 us
    ppermute x9, starting transfers between devices, to_ring(): return lax.ppermute(x, 'ctx', ring_perm(s % RING))  24.1 us
    ppermute x11, waiting for transfers between devices, to_side(): return lax.ppermute(x, 'ctx', side_perm(k))  17.2 us
    ppermute x11, starting transfers between devices, to_side(): return lax.ppermute(x, 'ctx', side_perm(k))  12 us
    all_to_all x1, waiting for transfers between devices, local(): lax.all_to_all(partial, ('dp', 'ctx'), 0, 0, axis_index_groups=groups, ti...  10.8 us
    all_to_all x1, starting transfers between devices, local(): lax.all_to_all(partial, ('dp', 'ctx'), 0, 0, axis_index_groups=groups, ti...  9.14 us
    pallas_call x1, Pallas kernels, attention_call(): pl.pallas_call(attention_kernel, out_shape=[shape(2 * ROWS), shape(2 * RO...  8.25 us
    pallas_call x2, Pallas kernels, split_queries(): pl.pallas_call(split_queries_kernel, out_shape=[shape(PACK)] * count, gri...  7.09 us
  transfers between devices with their start and end apart: 21, of which 9 were waited for; matrix products, arithmetic and copies ran while one was open for 0% of the time, Pallas kernels for 16%

profile of v2, /device:TPU:1, one launch (start us, length us, event | category | flops | bytes accessed | tf_op | source)
XLA Modules:
  0.0 131.8 jit_solution(2582801829106475517)
XLA Ops:
  1.3 1.7 %keys_values.1 = (bf16[256,128]{1,0:T(8,128)(2,1)}, bf16[256,128]{1,0:T(8,128)(2,1)}, bf16[256,128]{1,0:T(8,128)(2,1)}, bf16[256,128]{1,0:T(8,128)(2,1)}) custom-call(s32[2]{0:T(128)} %pad_add_fusion.place, bf16[128,512]{1,0:T(8,128)(2,1)} %bitcast.19, bf16[128,512]{1,0:T(8,128)(2,1)} %bitcast.20), custom_call_target="tpu_custom_call" | custom-call | tf_op jit(solution)/shard_map/keys_values/pallas_call | solution.py:439
  3.0 2.1 %collective-permute-start.1 = (bf16[256,128]{1,0:T(8,128)(2,1)}, bf16[256,128]{1,0:T(8,128)(2,1)S(1)}, u32[]{:S(2)}, u32[]{:S(2)}) collective-permute-start(bf16[256,128]{1,0:T(8,128)(2,1)} %get-tuple-element.31), channel_id=1, source_target_pairs={{0,2},{1,3},{2,0},{3,1},{4,6},{5,7},{6,4},{7,5},{8,10},{9,11},{10,... | collective-permute-start | bytes 196616 | tf_op jit(solution)/shard_map/keys_values/ppermute | solution.py:433
  6.1 3.6 %queries_far.1 = (bf16[2320,128]{1,0:T(8,128)(2,1)}, bf16[2320,128]{1,0:T(8,128)(2,1)}) custom-call(s32[2]{0:T(128)} %pad_add_fusion.place, bf16[128,4096]{1,0:T(8,128)(2,1)} %bitcast.13, bf16[128,4096]{1,0:T(8,128)(2,1)} %bitcast.15, bf16[128,4096]{1,0:T(8,128)(2,1)} %bitcast.17, f32[32,128]{1,0:T(8,128)} %bitcast.21, bf16[256,128]{1,0:T(8,128)(2,1)} %get-tuple-element.30.after), custom_call_target="tpu_custom_call" | custom-call | bytes 33554432 | tf_op jit(solution)/shard_map/queries_far/pallas_call | solution.py:96
  9.7 1.7 %collective-permute-start.8 = (bf16[2320,128]{1,0:T(8,128)(2,1)}, bf16[2320,128]{1,0:T(8,128)(2,1)S(1)}, u32[]{:S(2)}, u32[]{:S(2)}) collective-permute-start(bf16[2320,128]{1,0:T(8,128)(2,1)} %get-tuple-element.41), channel_id=1, source_target_pairs={{0,3},{1,2},{2,1},{3,0},{4,7},{5,6},{6,5},{7,4},{8,11},{9,10},{10,... | collective-permute-start | bytes 1781768 | tf_op jit(solution)/shard_map/queries_far/ppermute | solution.py:433
  15.8 2.5 %collective-permute-start.4 = (bf16[128,2304]{1,0:T(8,128)(2,1)S(1)}, bf16[128,2304]{1,0:T(8,128)(2,1)S(1)}, u32[]{:S(2)}, u32[]{:S(2)}) collective-permute-start(bf16[128,2304]{1,0:T(8,128)(2,1)S(1)} %get-tuple-element.36), channel_id=1, source_target_pairs={{0,8},{1,9},{2,10},{3,11},{4,12},{5,13},{6,14},{7,15},{8,0},{9,1},... | collective-permute-start | bytes 1769480 | tf_op jit(solution)/shard_map/ring/ppermute | solution.py:436
  19.4 3.5 %queries_near.1 = (bf16[2320,128]{1,0:T(8,128)(2,1)}, bf16[2320,128]{1,0:T(8,128)(2,1)}) custom-call(s32[2]{0:T(128)} %pad_add_fusion.place, bf16[128,4096]{1,0:T(8,128)(2,1)} %bitcast.14, bf16[128,4096]{1,0:T(8,128)(2,1)} %bitcast.16, bf16[128,4096]{1,0:T(8,128)(2,1)} %bitcast.18, f32[32,128]{1,0:T(8,128)} %bitcast.22, f32[8,128]{1,0:T(8,128)} %copy-done.7), custom_call_target="tpu_custom_call" | custom-call | bytes 33554432 | tf_op jit(solution)/shard_map/queries_near/pallas_call | solution.py:96
  22.9 3.0 %collective-permute-done.8.refs_5_.refs_7_ = bf16[2320,128]{1,0:T(8,128)(2,1)S(1)} collective-permute-done((bf16[2320,128]{1,0:T(8,128)(2,1)}, bf16[2320,128]{1,0:T(8,128)(2,1)S(1)}, u32[]{:S(2)}, u32[]{:S(2)}) %collective-permute-start.8) | collective-permute-done | bytes 593952 | tf_op jit(solution)/shard_map/queries_far/ppermute | solution.py:433
  25.9 12.3 %collective-permute-done.7.refs_4_.refs_6_ = bf16[2320,128]{1,0:T(8,128)(2,1)S(1)} collective-permute-done((bf16[2320,128]{1,0:T(8,128)(2,1)}, bf16[2320,128]{1,0:T(8,128)(2,1)S(1)}, u32[]{:S(2)}, u32[]{:S(2)}) %collective-permute-start.7) | collective-permute-done | bytes 593952 | tf_op jit(solution)/shard_map/queries_far/ppermute | solution.py:433
  38.2 5.8 %collective-permute-done.4.refs_2_ = bf16[128,2304]{1,0:T(8,128)(2,1)S(1)} collective-permute-done((bf16[128,2304]{1,0:T(8,128)(2,1)S(1)}, bf16[128,2304]{1,0:T(8,128)(2,1)S(1)}, u32[]{:S(2)}, u32[]{:S(2)}) %collective-permute-start.4) | collective-permute-done | bytes 589856 | tf_op jit(solution)/shard_map/ring/ppermute | solution.py:436
  46.4 1.3 collective-permute-start.12
  48.1 1.8 %collective-permute-done.6.refs_5_ = bf16[2320,128]{1,0:T(8,128)(2,1)S(1)} collective-permute-done((bf16[2320,128]{1,0:T(8,128)(2,1)S(1)}, bf16[2320,128]{1,0:T(8,128)(2,1)S(1)}, u32[]{:S(2)}, u32[]{:S(2)}) %collective-permute-start.6) | collective-permute-done | bytes 593952 | tf_op jit(solution)/shard_map/queries_near/ppermute | solution.py:433
  49.9 8.2 %attention.1 = (bf16[2048,128]{1,0:T(8,128)(2,1)S(1)}, bf16[2560,128]{1,0:T(8,128)(2,1)S(1)}, f32[1024,128]{1,0:T(8,128)S(1)}, bf16[1024,128]{1,0:T(8,128)(2,1)S...) custom-call(s32[2]{0:T(128)S(1)} %copy-done.6, s32[1,16]{1,0:T(1,128)S(1)} %copy-done.8, ...), custom_call_target="tpu_custom_call" | custom-call | tf_op jit(solution)/shard_map/attention/pallas_call | solution.py:293
  58.2 9.5 %collective-permute-start.9 = (bf16[1024,128]{1,0:T(8,128)(2,1)S(1)}, bf16[1024,128]{1,0:T(8,128)(2,1)S(1)}, u32[]{:S(2)}, u32[]{:S(2)}) collective-permute-start(bf16[1024,128]{1,0:T(8,128)(2,1)S(1)} %get-tuple-element.44), channel_id=1, source_target_pairs={{0,8},{1,9},{2,10},{3,11},{4,12},{5,13},{6,14},{7,15},{8,0},{9,1},... | collective-permute-start | bytes 786440 | tf_op jit(solution)/shard_map/kv_gradients/ppermute | solution.py:436
  67.7 5.8 %collective-permute-start.10 = (bf16[1024,128]{1,0:T(8,128)(2,1)S(1)}, bf16[1024,128]{1,0:T(8,128)(2,1)S(1)}, u32[]{:S(2)}, u32[]{:S(2)}) collective-permute-start(bf16[1024,128]{1,0:T(8,128)(2,1)S(1)} %get-tuple-element.45), channel_id=1, source_target_pairs={{0,12},{1,13},{2,14},{3,15},{4,0},{5,1},{6,2},{7,3},{8,4},{9,5},{1... | collective-permute-start | bytes 786440 | tf_op jit(solution)/shard_map/kv_gradients/ppermute | solution.py:436
  74.1 11.6 %collective-permute-done.10.refs_1_ = bf16[1024,128]{1,0:T(8,128)(2,1)S(1)} collective-permute-done((bf16[1024,128]{1,0:T(8,128)(2,1)S(1)}, bf16[1024,128]{1,0:T(8,128)(2,1)S(1)}, u32[]{:S(2)}, u32[]{:S(2)}) %collective-permute-start.10) | collective-permute-done | bytes 262176 | tf_op jit(solution)/shard_map/kv_gradients/ppermute | solution.py:436
  87.4 1.4 %collective-permute-start.14 = (bf16[2560,128]{1,0:T(8,128)(2,1)S(1)}, bf16[2560,128]{1,0:T(8,128)(2,1)S(1)}, u32[]{:S(2)}, u32[]{:S(2)}) collective-permute-start(bf16[2560,128]{1,0:T(8,128)(2,1)S(1)} %get-tuple-element.48), channel_id=1, source_target_pairs={{0,2},{1,3},{2,0},{3,1},{4,6},{5,7},{6,4},{7,5},{8,10},{9,11},{10,... | collective-permute-start | bytes 1966088 | tf_op jit(solution)/shard_map/own_gradients/ppermute | solution.py:433
  88.7 2.1 %collective-permute-start.17 = (bf16[1024,128]{1,0:T(8,128)(2,1)S(1)}, bf16[1024,128]{1,0:T(8,128)(2,1)S(1)}, u32[]{:S(2)}, u32[]{:S(2)}) collective-permute-start(bf16[1024,128]{1,0:T(8,128)(2,1)S(1)} %get-tuple-element.49.total.refs_0_), channel_id=1, source_target_pairs={{0,12},{1,13},{2,14},{3,15},{4,0},{5,1},{6,2},{7,3},{8,4},{9,5},{1... | collective-permute-start | bytes 786440 | tf_op jit(solution)/shard_map/kv_gradients/ppermute | solution.py:436
  92.1 4.6 %collective-permute-done.17.rest_2_.refs_3_ = bf16[1024,128]{1,0:T(8,128)(2,1)S(1)} collective-permute-done((bf16[1024,128]{1,0:T(8,128)(2,1)S(1)}, bf16[1024,128]{1,0:T(8,128)(2,1)S(1)}, u32[]{:S(2)}, u32[]{:S(2)}) %collective-permute-start.17) | collective-permute-done | bytes 262176 | tf_op jit(solution)/shard_map/kv_gradients/ppermute | solution.py:436
  96.7 8.3 %collective-permute-done.16.rest_1_.refs_2_ = bf16[1024,128]{1,0:T(8,128)(2,1)S(1)} collective-permute-done((bf16[1024,128]{1,0:T(8,128)(2,1)S(1)}, bf16[1024,128]{1,0:T(8,128)(2,1)S(1)}, u32[]{:S(2)}, u32[]{:S(2)}) %collective-permute-start.16) | collective-permute-done | bytes 262176 | tf_op jit(solution)/shard_map/kv_gradients/ppermute | solution.py:436
  105.0 1.6 %collective-permute-start.18 = (bf16[2560,128]{1,0:T(8,128)(2,1)S(1)}, bf16[2560,128]{1,0:T(8,128)(2,1)S(1)}, u32[]{:S(2)}, u32[]{:S(2)}) collective-permute-start(bf16[2560,128]{1,0:T(8,128)(2,1)S(1)} %own_gradients.2), channel_id=1, source_target_pairs={{0,1},{1,0},{2,3},{3,2},{4,5},{5,4},{6,7},{7,6},{8,9},{9,8},{10,11... | collective-permute-start | bytes 1966088 | tf_op jit(solution)/shard_map/own_gradients/ppermute | solution.py:433
  106.6 2.5 %projection.1 = bf16[32,80,128]{2,1,0:T(8,128)(2,1)} custom-call(bf16[1024,128]{1,0:T(8,128)(2,1)S(1)} %get-tuple-element.49.total.refs_0_, bf16[1024,128]{1,0:T(8,128)(2,1)S(1)} %collective-permute-done.15.rest_0_.refs_1_, bf16[1024,128]{1,0:T(8,128)(2,1)S(1)} %collective-permute-done.16.rest_1_.refs_2_, ...), custom_call_target="tpu_custom_call" | custom-call | tf_op jit(solution)/shard_map/projection/pallas_call | solution.py:484
  109.1 9.1 %all-to-all-start = ((bf16[32,80,128]{2,1,0:T(8,128)(2,1)}), bf16[32,80,128]{2,1,0:T(8,128)(2,1)S(1)}, u32[]{:S(2)}, u32[]{:S(2)}) async-start(bf16[32,80,128]{2,1,0:T(8,128)(2,1)} %projection.1), calls=%async_computation | async-start | bytes 1310720 | tf_op jit(solution)/shard_map/projection_sum/all_to_all | solution.py:515
  118.3 1.9 %own_gradients.3 = (bf16[128,4096]{1,0:T(8,128)(2,1)}, bf16[128,512]{1,0:T(8,128)(2,1)}, bf16[128,512]{1,0:T(8,128)(2,1)}) custom-call(s32[2]{0:T(128)S(1)} %copy-done.6, bf16[2048,128]{1,0:T(8,128)(2,1)S(1)} %get-tuple-element.42.near, bf16[2560,128]{1,0:T(8,128)(2,1)S(1)} %collective-permute-done.14.side, ...), custom_call_target="tpu_custom_call" | custom-call | bytes 67108864 | tf_op jit(solution)/shard_map/own_gradients/pallas_call | solution.py:502
  120.2 10.8 %all-to-all-done.parts = bf16[32,80,128]{2,1,0:T(8,128)(2,1)S(1)} async-done(((bf16[32,80,128]{2,1,0:T(8,128)(2,1)}), bf16[32,80,128]{2,1,0:T(8,128)(2,1)S(1)}, u32[]{:S(2)}, u32[]{:S(2)}) %all-to-all-start) | async-done | bytes 655392 | tf_op jit(solution)/shard_map/projection_sum/all_to_all | solution.py:515
  (50 shorter events, 13.9 us)
Async XLA Ops:
  3.0 8.5 %collective-permute-start.1 = (bf16[256,128]{1,0:T(8,128)(2,1)}, bf16[256,128]{1,0:T(8,128)(2,1)S(1)}, u32[]{:S(2)}, u32[]{:S(2)}) collective-permute-start(bf16[256,128]{1,0:T(8,128)(2,1)} %get-tuple-element.31), channel_id=1, source_target_pairs={{0,2},{1,3},{2,0},{3,1},{4,6},{5,7},{6,4},{7,5},{8,10},{9,11},{10,... | collective-permute-start | bytes 196616 | tf_op jit(solution)/shard_map/keys_values/ppermute | solution.py:433
  5.1 6.4 %collective-permute-start.2 = (bf16[256,128]{1,0:T(8,128)(2,1)}, bf16[256,128]{1,0:T(8,128)(2,1)S(1)}, u32[]{:S(2)}, u32[]{:S(2)}) collective-permute-start(bf16[256,128]{1,0:T(8,128)(2,1)} %get-tuple-element.32), channel_id=1, source_target_pairs={{0,3},{1,2},{2,1},{3,0},{4,7},{5,6},{6,5},{7,4},{8,11},{9,10},{10,... | collective-permute-start | bytes 196616 | tf_op jit(solution)/shard_map/keys_values/ppermute | solution.py:433
  6.1 5.5 %collective-permute-start = (bf16[256,128]{1,0:T(8,128)(2,1)}, bf16[256,128]{1,0:T(8,128)(2,1)S(1)}, u32[]{:S(2)}, u32[]{:S(2)}) collective-permute-start(bf16[256,128]{1,0:T(8,128)(2,1)} %get-tuple-element.30.after), channel_id=1, source_target_pairs={{0,1},{1,0},{2,3},{3,2},{4,5},{5,4},{6,7},{7,6},{8,9},{9,8},{10,11... | collective-permute-start | bytes 196616 | tf_op jit(solution)/shard_map/keys_values/ppermute | solution.py:433
  6.1 5.4 %copy-start.2 = (bf16[1,128,5120]{2,1,0:T(8,128)(2,1)S(1)}, bf16[1,128,5120]{2,1,0:T(8,128)(2,1)}, u32[]{:S(2)}) copy-start(bf16[1,128,5120]{2,1,0:T(8,128)(2,1)} %param.14) | copy-start | bytes 3932164
  6.1 5.5 %copy-start.4 = (bf16[256,128]{1,0:T(8,128)(2,1)S(1)}, bf16[256,128]{1,0:T(8,128)(2,1)}, u32[]{:S(2)}) copy-start(bf16[256,128]{1,0:T(8,128)(2,1)} %get-tuple-element.29.refs_0_) | copy-start | bytes 196612
  6.1 5.5 %copy-start.5 = (s32[2]{0:T(128)S(1)}, s32[2]{0:T(128)}, u32[]{:S(2)}) copy-start(s32[2]{0:T(128)} %pad_add_fusion.place) | copy-start | bytes 28
  9.7 16.2 %collective-permute-start.8 = (bf16[2320,128]{1,0:T(8,128)(2,1)}, bf16[2320,128]{1,0:T(8,128)(2,1)S(1)}, u32[]{:S(2)}, u32[]{:S(2)}) collective-permute-start(bf16[2320,128]{1,0:T(8,128)(2,1)} %get-tuple-element.41), channel_id=1, source_target_pairs={{0,3},{1,2},{2,1},{3,0},{4,7},{5,6},{6,5},{7,4},{8,11},{9,10},{10,... | collective-permute-start | bytes 1781768 | tf_op jit(solution)/shard_map/queries_far/ppermute | solution.py:433
  11.4 26.8 %collective-permute-start.7 = (bf16[2320,128]{1,0:T(8,128)(2,1)}, bf16[2320,128]{1,0:T(8,128)(2,1)S(1)}, u32[]{:S(2)}, u32[]{:S(2)}) collective-permute-start(bf16[2320,128]{1,0:T(8,128)(2,1)} %get-tuple-element.33.refs_4_), channel_id=1, source_target_pairs={{0,2},{1,3},{2,0},{3,1},{4,6},{5,7},{6,4},{7,5},{8,10},{9,11},{10,... | collective-permute-start | bytes 1781768 | tf_op jit(solution)/shard_map/queries_far/ppermute | solution.py:433
  14.5 23.7 %collective-permute-start.3 = (bf16[128,2304]{1,0:T(8,128)(2,1)S(1)}, bf16[128,2304]{1,0:T(8,128)(2,1)S(1)}, u32[]{:S(2)}, u32[]{:S(2)}) collective-permute-start(bf16[128,2304]{1,0:T(8,128)(2,1)S(1)} %get-tuple-element.35), channel_id=1, source_target_pairs={{0,4},{1,5},{2,6},{3,7},{4,8},{5,9},{6,10},{7,11},{8,12},{9,13},{1... | collective-permute-start | bytes 1769480 | tf_op jit(solution)/shard_map/ring/ppermute | solution.py:436
  15.8 28.3 %collective-permute-start.4 = (bf16[128,2304]{1,0:T(8,128)(2,1)S(1)}, bf16[128,2304]{1,0:T(8,128)(2,1)S(1)}, u32[]{:S(2)}, u32[]{:S(2)}) collective-permute-start(bf16[128,2304]{1,0:T(8,128)(2,1)S(1)} %get-tuple-element.36), channel_id=1, source_target_pairs={{0,8},{1,9},{2,10},{3,11},{4,12},{5,13},{6,14},{7,15},{8,0},{9,1},... | collective-permute-start | bytes 1769480 | tf_op jit(solution)/shard_map/ring/ppermute | solution.py:436
  18.2 25.8 %collective-permute-start.5 = (bf16[128,2304]{1,0:T(8,128)(2,1)S(1)}, bf16[128,2304]{1,0:T(8,128)(2,1)S(1)}, u32[]{:S(2)}, u32[]{:S(2)}) collective-permute-start(bf16[128,2304]{1,0:T(8,128)(2,1)S(1)} %get-tuple-element.37), channel_id=1, source_target_pairs={{0,12},{1,13},{2,14},{3,15},{4,0},{5,1},{6,2},{7,3},{8,4},{9,5},{1... | collective-permute-start | bytes 1769480 | tf_op jit(solution)/shard_map/ring/ppermute | solution.py:436
  45.2 40.5 %collective-permute-start.13 = (bf16[512,1280]{1,0:T(8,128)(2,1)S(1)}, bf16[512,1280]{1,0:T(8,128)(2,1)S(1)}, u32[]{:S(2)}, u32[]{:S(2)}) collective-permute-start(bf16[512,1280]{1,0:T(8,128)(2,1)S(1)} %inputs_side.1.refs_8_.refs_4_), channel_id=1, source_target_pairs={{0,1},{1,0},{2,3},{3,2},{4,5},{5,4},{6,7},{7,6},{8,9},{9,8},{10,11... | collective-permute-start | bytes 3932168 | tf_op jit(solution)/shard_map/inputs_side/ppermute | solution.py:433
  46.4 39.3 %collective-permute-start.12 = (bf16[512,1280]{1,0:T(8,128)(2,1)S(1)}, bf16[512,1280]{1,0:T(8,128)(2,1)S(1)}, u32[]{:S(2)}, u32[]{:S(2)}) collective-permute-start(bf16[512,1280]{1,0:T(8,128)(2,1)S(1)} %inputs_side.1.refs_8_.refs_4_), channel_id=1, source_target_pairs={{0,2},{1,3},{2,0},{3,1},{4,6},{5,7},{6,4},{7,5},{8,10},{9,11},{10,... | collective-permute-start | bytes 3932168 | tf_op jit(solution)/shard_map/inputs_side/ppermute | solution.py:433
  47.7 2.2 %collective-permute-start.6 = (bf16[2320,128]{1,0:T(8,128)(2,1)S(1)}, bf16[2320,128]{1,0:T(8,128)(2,1)S(1)}, u32[]{:S(2)}, u32[]{:S(2)}) collective-permute-start(bf16[2320,128]{1,0:T(8,128)(2,1)S(1)} %copy-done.9), channel_id=1, source_target_pairs={{0,1},{1,0},{2,3},{3,2},{4,5},{5,4},{6,7},{7,6},{8,9},{9,8},{10,11... | collective-permute-start | bytes 1781768 | tf_op jit(solution)/shard_map/queries_near/ppermute | solution.py:433
  58.2 15.9 %collective-permute-start.9 = (bf16[1024,128]{1,0:T(8,128)(2,1)S(1)}, bf16[1024,128]{1,0:T(8,128)(2,1)S(1)}, u32[]{:S(2)}, u32[]{:S(2)}) collective-permute-start(bf16[1024,128]{1,0:T(8,128)(2,1)S(1)} %get-tuple-element.44), channel_id=1, source_target_pairs={{0,8},{1,9},{2,10},{3,11},{4,12},{5,13},{6,14},{7,15},{8,0},{9,1},... | collective-permute-start | bytes 786440 | tf_op jit(solution)/shard_map/kv_gradients/ppermute | solution.py:436
  67.7 18.0 %collective-permute-start.10 = (bf16[1024,128]{1,0:T(8,128)(2,1)S(1)}, bf16[1024,128]{1,0:T(8,128)(2,1)S(1)}, u32[]{:S(2)}, u32[]{:S(2)}) collective-permute-start(bf16[1024,128]{1,0:T(8,128)(2,1)S(1)} %get-tuple-element.45), channel_id=1, source_target_pairs={{0,12},{1,13},{2,14},{3,15},{4,0},{5,1},{6,2},{7,3},{8,4},{9,5},{1... | collective-permute-start | bytes 786440 | tf_op jit(solution)/shard_map/kv_gradients/ppermute | solution.py:436
  73.5 12.2 %collective-permute-start.11 = (bf16[1024,128]{1,0:T(8,128)(2,1)S(1)}, bf16[1024,128]{1,0:T(8,128)(2,1)S(1)}, u32[]{:S(2)}, u32[]{:S(2)}) collective-permute-start(bf16[1024,128]{1,0:T(8,128)(2,1)S(1)} %get-tuple-element.46), channel_id=1, source_target_pairs={{0,4},{1,5},{2,6},{3,7},{4,8},{5,9},{6,10},{7,11},{8,12},{9,13},{1... | collective-permute-start | bytes 786440 | tf_op jit(solution)/shard_map/kv_gradients/ppermute | solution.py:436
  86.1 20.5 %collective-permute-start.19 = (bf16[512,1280]{1,0:T(8,128)(2,1)S(1)}, bf16[512,1280]{1,0:T(8,128)(2,1)S(1)}, u32[]{:S(2)}, u32[]{:S(2)}) collective-permute-start(bf16[512,1280]{1,0:T(8,128)(2,1)S(1)} %get-tuple-element.53.refs_6_), channel_id=1, source_target_pairs={{0,1},{1,0},{2,3},{3,2},{4,5},{5,4},{6,7},{7,6},{8,9},{9,8},{10,11... | collective-permute-start | bytes 3932168 | tf_op jit(solution)/shard_map/kv_gradients/ppermute | solution.py:433
  87.4 17.6 %collective-permute-start.14 = (bf16[2560,128]{1,0:T(8,128)(2,1)S(1)}, bf16[2560,128]{1,0:T(8,128)(2,1)S(1)}, u32[]{:S(2)}, u32[]{:S(2)}) collective-permute-start(bf16[2560,128]{1,0:T(8,128)(2,1)S(1)} %get-tuple-element.48), channel_id=1, source_target_pairs={{0,2},{1,3},{2,0},{3,1},{4,6},{5,7},{6,4},{7,5},{8,10},{9,11},{10,... | collective-permute-start | bytes 1966088 | tf_op jit(solution)/shard_map/own_gradients/ppermute | solution.py:433
  88.7 7.9 %collective-permute-start.17 = (bf16[1024,128]{1,0:T(8,128)(2,1)S(1)}, bf16[1024,128]{1,0:T(8,128)(2,1)S(1)}, u32[]{:S(2)}, u32[]{:S(2)}) collective-permute-start(bf16[1024,128]{1,0:T(8,128)(2,1)S(1)} %get-tuple-element.49.total.refs_0_), channel_id=1, source_target_pairs={{0,12},{1,13},{2,14},{3,15},{4,0},{5,1},{6,2},{7,3},{8,4},{9,5},{1... | collective-permute-start | bytes 786440 | tf_op jit(solution)/shard_map/kv_gradients/ppermute | solution.py:436
  90.9 14.0 %collective-permute-start.16 = (bf16[1024,128]{1,0:T(8,128)(2,1)S(1)}, bf16[1024,128]{1,0:T(8,128)(2,1)S(1)}, u32[]{:S(2)}, u32[]{:S(2)}) collective-permute-start(bf16[1024,128]{1,0:T(8,128)(2,1)S(1)} %get-tuple-element.49.total.refs_0_), channel_id=1, source_target_pairs={{0,4},{1,5},{2,6},{3,7},{4,8},{5,9},{6,10},{7,11},{8,12},{9,13},{1... | collective-permute-start | bytes 786440 | tf_op jit(solution)/shard_map/kv_gradients/ppermute | solution.py:436
  90.9 14.0 %collective-permute-start.15 = (bf16[1024,128]{1,0:T(8,128)(2,1)S(1)}, bf16[1024,128]{1,0:T(8,128)(2,1)S(1)}, u32[]{:S(2)}, u32[]{:S(2)}) collective-permute-start(bf16[1024,128]{1,0:T(8,128)(2,1)S(1)} %get-tuple-element.49.total.refs_0_), channel_id=1, source_target_pairs={{0,8},{1,9},{2,10},{3,11},{4,12},{5,13},{6,14},{7,15},{8,0},{9,1},... | collective-permute-start | bytes 786440 | tf_op jit(solution)/shard_map/kv_gradients/ppermute | solution.py:436
  105.0 13.3 %collective-permute-start.18 = (bf16[2560,128]{1,0:T(8,128)(2,1)S(1)}, bf16[2560,128]{1,0:T(8,128)(2,1)S(1)}, u32[]{:S(2)}, u32[]{:S(2)}) collective-permute-start(bf16[2560,128]{1,0:T(8,128)(2,1)S(1)} %own_gradients.2), channel_id=1, source_target_pairs={{0,1},{1,0},{2,3},{3,2},{4,5},{5,4},{6,7},{7,6},{8,9},{9,8},{10,11... | collective-permute-start | bytes 1966088 | tf_op jit(solution)/shard_map/own_gradients/ppermute | solution.py:433
  109.1 21.9 %all-to-all-start = ((bf16[32,80,128]{2,1,0:T(8,128)(2,1)}), bf16[32,80,128]{2,1,0:T(8,128)(2,1)S(1)}, u32[]{:S(2)}, u32[]{:S(2)}) async-start(bf16[32,80,128]{2,1,0:T(8,128)(2,1)} %projection.1), calls=%async_computation | async-start | bytes 1310720 | tf_op jit(solution)/shard_map/projection_sum/all_to_all | solution.py:515
  (7 other events, 19.8 us)

commit v3 on v2

--- a/solution.py
+++ b/solution.py
@@ -15,9 +15,10 @@
 RING = 4
 SIDE = 4
 TREES = 8
+PAIR = 2
 TALL = 1024
 ROWS = GROUP * BLK
-PACK = 2 * ROWS + 272
+PACK = 2 * ROWS + 32
 SCALE = HEAD_SIZE ** (-0.5)
 RING_ORDER = (2, 1, 3)
 LOG2E = 1.4426950408889634
@@ -63,7 +64,9 @@
         out[BLK:, :] = value_ref[:, pl.ds(col, HEAD_SIZE)]
 
 
-def split_queries_kernel(place, query_ref, gradient_ref, output_ref, lse_ref, after, *outs):
+def split_queries_kernel(place, query_ref, gradient_ref, output_ref, lse_ref, kv_ref, after, *outs):
+    outs, token = outs[:-1], outs[-1]
+    token[...] = jnp.zeros_like(token)
     lane = lax.broadcasted_iota(jnp.int32, (BLK, 128), 1)
     columns = jnp.zeros((BLK, 128), F32)
     for h in range(GROUP):
@@ -88,14 +91,17 @@
                 out[ROWS + h * BLK : ROWS + (h + 1) * BLK, :] = gradient_ref[:, cols]
             out[2 * ROWS : 2 * ROWS + 16, :] = split(lse)
             out[2 * ROWS + 16 : 2 * ROWS + 32, :] = split(delta)
-
-
-def split_queries(place, queries, gradient, output, lse, after, first):
+            if out.shape[0] > PACK:
+                out[PACK:, :] = kv_ref[...]
+
+
+def split_queries(place, queries, gradient, output, lse, kv, after, first):
     count = SIDE // 2
+    rows = PACK if first else PACK + 2 * BLK
     wide = pl.BlockSpec((BLK, GROUP * HEAD_SIZE), lambda k, place: (0, place[1] ^ (first + k)))
     return pl.pallas_call(
         split_queries_kernel,
-        out_shape=[shape(PACK)] * count,
+        out_shape=[shape(rows)] * count + [shape(8, 128, F32)],
         grid_spec=pltpu.PrefetchScalarGridSpec(
             num_scalar_prefetch=1,
             grid=(count,),
@@ -104,19 +110,27 @@
                 wide,
                 wide,
                 pl.BlockSpec((GROUP, BLK), lambda k, place: (place[1] ^ (first + k), 0)),
+                pl.BlockSpec((2 * BLK, HEAD_SIZE), lambda k, place: (0, 0)),
                 pl.BlockSpec(memory_space=pl.ANY),
             ],
-            out_specs=[pl.BlockSpec((PACK, HEAD_SIZE), lambda k, place: (0, 0))] * count,
+            out_specs=[pl.BlockSpec((rows, HEAD_SIZE), lambda k, place: (0, 0))] * count
+            + [pl.BlockSpec((8, 128), lambda k, place: (0, 0))],
         ),
         compiler_params=pltpu.CompilerParams(vmem_limit_bytes=56 * MIB),
         cost_estimate=pl.CostEstimate(flops=0, bytes_accessed=32 * MIB, transcendentals=0),
-    )(place, queries, gradient, output, lse, after)
-
-
-def ring_pack_kernel(place, inputs, *refs):
-    kv, refs = refs[:SIDE], refs[SIDE + 1 :]
-    outs, token, shares = refs[:RING], refs[RING], refs[RING + 1]
+    )(place, queries, gradient, output, lse, kv, after)
+
+
+def stack_kernel(*refs):
+    out, token = refs[-2:]
     token[...] = jnp.zeros_like(token)
+    rows = refs[0].shape[0]
+    for k in range(SIDE):
+        out[k * rows : (k + 1) * rows, :] = refs[k][refs[k].shape[0] - rows :, :]
+
+
+def share_inputs_kernel(place, inputs, *refs):
+    outs, shares = refs[-1 - RING : -1], refs[-1]
     _, _, quarter = shares.shape
     piece = quarter // TREES
     for r in range(RING):
@@ -124,36 +138,34 @@
             [inputs[:, (d * RING + r) * piece : (d * RING + r + 1) * piece] for d in range(TREES)], axis=1
         )
     for s, out in enumerate(outs):
-        out[:, 0:quarter] = shares[(place[0] + s) % RING]
-        for k in range(SIDE):
-            for half in range(2):
-                col = quarter + (2 * k + half) * HEAD_SIZE
-                out[:, col : col + HEAD_SIZE] = kv[k][half * BLK : (half + 1) * BLK, :]
-
-
-def attention_kernel(place, parents, *refs):
-    ring_in, packs, refs = refs[:RING], refs[RING : RING + SIDE], refs[RING + SIDE + 1 :]
-    dq_outs, grad_outs, refs = refs[:2], refs[2 : 2 + RING], refs[2 + RING :]
+        out[...] = shares[(place[0] + s) % RING]
+
+
+def attention_kernel(first, place, parents, *refs):
+    last = first > 0
+    kv_in, packs, refs = refs[:RING], refs[RING : RING + PAIR], refs[RING + PAIR :]
+    if last:
+        sums_in, dq_out, grad_outs, refs = refs[0], refs[2], refs[3 : 3 + RING], refs[3 + RING :]
+    else:
+        dq_out, sums_out, refs = refs[0], refs[1], refs[2:]
     kv, kv_t, pack, query_t, gradient_t, terms, dq_acc, dq, acc, stage_own, stage, kv_sem, pack_sem, out_sem = refs
     ring, own = place[0], place[1]
-    start = ring_in[0].shape[1] - 2 * SIDE * HEAD_SIZE
 
     loads = []
     for s in range(RING):
         for k in range(SIDE):
-            for half in range(2):
-                col = start + (2 * k + half) * HEAD_SIZE
-                loads.append(
-                    pltpu.make_async_copy(
-                        ring_in[s].at[:, pl.ds(col, HEAD_SIZE)],
-                        kv.at[s * SIDE + k, pl.ds(half * BLK, BLK), :],
-                        kv_sem.at[len(loads)],
-                    )
-                )
-    pack_loads = [pltpu.make_async_copy(packs[k], pack.at[k], pack_sem.at[k]) for k in range(SIDE)]
+            slot = s * SIDE + k
+            source = kv_in[s].at[pl.ds(2 * k * BLK, 2 * BLK), :]
+            loads.append(pltpu.make_async_copy(source, kv.at[slot], kv_sem.at[slot]))
+    pack_loads = [
+        pltpu.make_async_copy(packs[k].at[pl.ds(0, PACK), :], pack.at[k], pack_sem.at[k]) for k in range(PAIR)
+    ]
+    if last:
+        pack_loads.append(pltpu.make_async_copy(sums_in, acc, pack_sem.at[PAIR]))
     for load in loads + pack_loads:
         load.start()
-    acc[...] = jnp.zeros_like(acc)
+    if not last:
+        acc[...] = jnp.zeros_like(acc)
     for load in loads:
         load.wait()
 
@@ -174,8 +186,7 @@
         load.wait()
 
     def store_dq(k):
-        place_out = dq_outs[k // 2].at[pl.ds(k % 2 * ROWS, ROWS), :]
-        return pltpu.make_async_copy(dq.at[k], place_out, out_sem.at[k])
+        return pltpu.make_async_copy(dq.at[k], dq_out.at[pl.ds(k * ROWS, ROWS), :], out_sem.at[k])
 
     def slot_of(at):
         return ((ring - at // SIDE) % RING) * SIDE + ((at % SIDE) ^ own)
@@ -216,7 +227,7 @@
             acc[j, 0:BLK, :] += dk[:, m * BLK : (m + 1) * BLK]
             acc[j, BLK:, :] += dv[:, m * BLK : (m + 1) * BLK]
 
-    @pl.loop(0, SIDE)
+    @pl.loop(0, PAIR)
     def _(piece):
         lane = lax.broadcasted_iota(jnp.int32, (BLK, 128), 1)
         columns = jnp.concatenate(
@@ -228,17 +239,18 @@
             gradient_t[:, cols] = pack[piece, ROWS + h * BLK : ROWS + (h + 1) * BLK, :].T
             terms[cols, :] = jnp.where(lane % GROUP == h, columns, 0.0).astype(BF16)
 
-        block = ring * SIDE + (own ^ piece)
+        side = piece + first
+        block = ring * SIDE + (own ^ side)
         above = lax.while_loop(lambda c: c[0] > 0, lambda c: (parents[0, c[0]], c[1] + 1), (block, 0))[1]
         odd = above % 2 == 1
 
         @pl.when(odd)
         def _():
-            tile(piece, [piece, slot_of(parents[0, block])], True)
+            tile(piece, [side, slot_of(parents[0, block])], True)
 
         @pl.when(jnp.logical_not(odd))
         def _():
-            tile(piece, [piece], True)
+            tile(piece, [side], True)
 
         def ancestors(at):
             one = parents[0, at]
@@ -263,13 +275,19 @@
             ancestors(at)
 
         dq[piece] = (dq_acc[...] * SCALE).astype(BF16)
-        for k in range(SIDE):
+        for k in range(PAIR):
 
             @pl.when(piece == k)
             def _(k=k):
                 store_dq(k).start()
 
-    stores = [store_dq(k) for k in range(SIDE)]
+    stores = [store_dq(k) for k in range(PAIR)]
+    if not last:
+        stores.append(pltpu.make_async_copy(acc, sums_out, out_sem.at[PAIR]))
+        stores[-1].start()
+        for store in stores:
+            store.wait()
+        return
     for s in RING_ORDER + (0,):
         for k in range(SIDE):
             dk, dv = acc[s * SIDE + k, 0:BLK, :] * SCALE, acc[s * SIDE + k, BLK:, :]
@@ -281,40 +299,43 @@
                 stage[s - 1, at : at + BLK, :] = dk.astype(BF16).T
                 stage[s - 1, at + BLK : at + 2 * BLK, :] = dv.astype(BF16).T
         source = stage_own if s == 0 else stage.at[s - 1]
-        stores.append(pltpu.make_async_copy(source, grad_outs[s], out_sem.at[SIDE + s]))
+        stores.append(pltpu.make_async_copy(source, grad_outs[s], out_sem.at[PAIR + s]))
         stores[-1].start()
     for store in stores:
         store.wait()
 
 
-def attention_call(place, parents, ring_in, packs, *after):
+def attention_call(place, parents, kv, packs, first, *rest):
     sum_shape = (RING * SIDE, 2 * BLK, HEAD_SIZE)
     hbm = pl.BlockSpec(memory_space=pl.ANY)
+    if first:
+        out_shape = [shape(PAIR * ROWS + 4 * BLK), shape(ROWS, kind=F32)] + [shape(ROWS)] * (RING - 1)
+    else:
+        out_shape = [shape(PAIR * ROWS), jax.ShapeDtypeStruct(sum_shape, F32)]
     return pl.pallas_call(
-        attention_kernel,
-        out_shape=[shape(2 * ROWS), shape(2 * ROWS + 4 * BLK), shape(ROWS, kind=F32)]
-        + [shape(ROWS)] * (RING - 1),
-        in_specs=[smem()] * 2 + [hbm] * (RING + SIDE + 1),
-        out_specs=[hbm] * (2 + RING),
+        functools.partial(attention_kernel, first),
+        out_shape=out_shape,
+        in_specs=[smem()] * 2 + [hbm] * (RING + PAIR + len(rest)),
+        out_specs=[hbm] * len(out_shape),
         scratch_shapes=[
             pltpu.VMEM(sum_shape, BF16),
             pltpu.VMEM((RING * SIDE, 2 * HEAD_SIZE, 2 * BLK), BF16),
-            pltpu.VMEM((SIDE, PACK, HEAD_SIZE), BF16),
+            pltpu.VMEM((PAIR, PACK, HEAD_SIZE), BF16),
             pltpu.VMEM((HEAD_SIZE, ROWS), BF16),
             pltpu.VMEM((HEAD_SIZE, ROWS), BF16),
             pltpu.VMEM((ROWS, 128), BF16),
             pltpu.VMEM((ROWS, HEAD_SIZE), F32),
-            pltpu.VMEM((SIDE, ROWS, HEAD_SIZE), BF16),
+            pltpu.VMEM((PAIR, ROWS, HEAD_SIZE), BF16),
             pltpu.VMEM(sum_shape, F32),
             pltpu.VMEM((ROWS, HEAD_SIZE), F32),
             pltpu.VMEM((RING - 1, ROWS, HEAD_SIZE), BF16),
-            pltpu.SemaphoreType.DMA((2 * RING * SIDE,)),
-            pltpu.SemaphoreType.DMA((SIDE,)),
-            pltpu.SemaphoreType.DMA((SIDE + RING,)),
+            pltpu.SemaphoreType.DMA((RING * SIDE,)),
+            pltpu.SemaphoreType.DMA((PAIR + 1,)),
+            pltpu.SemaphoreType.DMA((PAIR + RING,)),
         ],
         compiler_params=pltpu.CompilerParams(vmem_limit_bytes=24 * MIB),
         cost_estimate=pl.CostEstimate(flops=0, bytes_accessed=0, transcendentals=0),
-    )(place, parents, *ring_in, *packs, *after)
+    )(place, parents, *kv, *packs, *rest)
 
 
 def total_kernel(grad_own, *refs):
@@ -355,7 +376,7 @@
 def join_inputs_kernel(*refs):
     pieces, out = refs[:RING], refs[-1]
     for s in range(RING):
-        out[s * BLK : (s + 1) * BLK, :] = pieces[s][:, 0 : out.shape[1]]
+        out[s * BLK : (s + 1) * BLK, :] = pieces[s][...]
 
 
 def projection_kernel(*refs):
@@ -439,40 +460,49 @@
         kv_split = call(split_kv_kernel, [shape(2 * BLK)] * SIDE, 1, 2, limit=56)(
             place, key_tensor[0], value_tensor[0]
         )
-        kv_side = [kv_split[0]] + [to_side(kv_split[k], k) for k in (1, 2, 3)]
-
-    query_args = (queries[0], output_gradient[0], attention_output[0], logsumexp_rows[0])
+        kv_far = [to_side(kv_split[k], k) for k in (2, 3)]
+
+    query_args = (queries[0], output_gradient[0], attention_output[0], logsumexp_rows[0], kv_split[1])
+    with jax.named_scope("queries_near"):
+        near_own = split_queries(place, *query_args, kv_split[2], 0)
+        packs_near = [near_own[0], to_side(near_own[1], 1)]
+
+    with jax.named_scope("keys_values_ring"):
+        kv_own, token = call(stack_kernel, [shape(ROWS), shape(8, 128, F32)], 0, SIDE)(
+            kv_split[0], packs_near[1], *kv_far
+        )
+        kv = {s: to_ring(kv_own, s) for s in RING_ORDER}
+        kv = [kv_own] + [kv[s] for s in (1, 2, 3)]
+
     with jax.named_scope("queries_far"):
-        far_own = split_queries(place, *query_args, kv_split[1], 2)
+        far_own = split_queries(place, *query_args, token, 2)
         packs_far = [to_side(far_own[k - 2], k) for k in (2, 3)]
 
-    with jax.named_scope("ring"):
-        ring_out = call(
-            ring_pack_kernel,
-            [shape(BLK, quarter + 2 * SIDE * HEAD_SIZE)] * RING + [shape(8, 128, F32)],
+    with jax.named_scope("inputs_ring"):
+        shares = call(
+            share_inputs_kernel,
+            [shape(BLK, quarter)] * RING,
             1,
-            1 + SIDE,
-            n_any=1,
-            moved=128 * MIB,
+            1,
+            n_any=4,
             scratch=[pltpu.VMEM((RING, BLK, quarter), BF16)],
-        )(place, layer_input[0], *kv_side, far_own[0])
-        ring_in = {s: to_ring(ring_out[s], s) for s in RING_ORDER}
-        ring_in = [ring_out[0]] + [ring_in[s] for s in (1, 2, 3)]
-
-    with jax.named_scope("queries_near"):
-        near_own = split_queries(place, *query_args, ring_out[RING], 0)
-        packs = [near_own[0], to_side(near_own[1], 1)] + packs_far
+        )(place, layer_input[0], *kv[1:], packs_near[1])
+        from_ring = {s: to_ring(shares[s], s) for s in RING_ORDER}
+        from_ring = [shares[0]] + [from_ring[s] for s in (1, 2, 3)]
+
+    with jax.named_scope("attention_near"):
+        dq_near, sums = attention_call(place, parents, kv, packs_near, 0)
 
     with jax.named_scope("inputs_side"):
         input_own = call(join_inputs_kernel, [shape(RING * BLK, quarter)], 0, RING, n_any=3)(
-            *ring_in, *packs_far, near_own[0]
+            *from_ring, *packs_far, dq_near
         )[0]
         input_y = to_side(input_own, 2)
         input_core = to_side(input_own, 1)
 
-    with jax.named_scope("attention"):
-        outs = attention_call(place, parents, ring_in, packs, input_own)
-        dq_near, side_out, grad_own, grad_parts = outs[0], outs[1], outs[2], outs[3:]
+    with jax.named_scope("attention_far"):
+        outs = attention_call(place, parents, kv, packs_far, 2, sums, input_own)
+        side_out, grad_own, grad_parts = outs[0], outs[1], outs[2:]
 
     with jax.named_scope("kv_gradients"):
         received = [to_ring(grad_parts[s - 1], -s) for s in RING_ORDER]

time: 130 us -> 127 us (0.977); the launches traced: 132 us -> 127 us
  starting transfers between devices: 45.2 us -> 37.4 us
  Pallas kernels: 24 us -> 28.3 us
  local copies, waits for them, and re-layouts: 2.77 us -> 0.61 us
    ppermute x9 -> x12, starting transfers between devices: 24.1 us -> 15.2 us  [to_ring(): return lax.ppermute(x, 'ctx', ring_perm(s % RING))]
    pallas_call x4 -> x6, Pallas kernels: 16.6 us -> 20.9 us  [the longest x2 12.5 us: attention_call(): pl.pallas_call(functools.partial(attention_kernel, first), out_shape=out_...]
    ppermute x9 -> x12, waiting for transfers between devices: 30.4 us -> 34.1 us  [to_ring(): return lax.ppermute(x, 'ctx', ring_perm(s % RING))]
    ppermute x11 -> x10, waiting for transfers between devices: 17.2 us -> 13.9 us  [to_side(): return lax.ppermute(x, 'ctx', side_perm(k))]
    ppermute x11 -> x10, starting transfers between devices: 12 us -> 14.2 us  [to_side(): return lax.ppermute(x, 'ctx', side_perm(k))]
    unnamed x20 -> x16, local copies, waits for them, and re-layouts: 2.77 us -> 0.61 us
  transfers between devices with their start and end apart: 21 -> 23, of which waited for: 9 -> 12; matrix products, arithmetic and copies ran while one was open for 0% -> 0% of each run, Pallas kernels for 16% -> 17%
where the time goes in v3:
time: 127 us
  waiting for transfers between devices  58.9 us (46%)
  starting transfers between devices  37.4 us (29%)
  Pallas kernels  28.3 us (22%)
    ppermute x12, waiting for transfers between devices, to_ring(): return lax.ppermute(x, 'ctx', ring_perm(s % RING))  34.1 us
    ppermute x12, starting transfers between devices, to_ring(): return lax.ppermute(x, 'ctx', ring_perm(s % RING))  15.2 us
    ppermute x10, starting transfers between devices, to_side(): return lax.ppermute(x, 'ctx', side_perm(k))  14.2 us
    ppermute x10, waiting for transfers between devices, to_side(): return lax.ppermute(x, 'ctx', side_perm(k))  13.9 us
    pallas_call x2, Pallas kernels, attention_call(): pl.pallas_call(functools.partial(attention_kernel, first), out_shape=out_...  12.5 us
    all_to_all x1, waiting for transfers between devices, local(): lax.all_to_all(partial, ('dp', 'ctx'), 0, 0, axis_index_groups=groups, ti...  10.8 us
    all_to_all x1, starting transfers between devices, local(): lax.all_to_all(partial, ('dp', 'ctx'), 0, 0, axis_index_groups=groups, ti...  7.92 us
    pallas_call x2, Pallas kernels, split_queries(): pl.pallas_call(split_queries_kernel, out_shape=[shape(rows)] * count + [s...  7.33 us
  transfers between devices with their start and end apart: 23, of which 12 were waited for; matrix products, arithmetic and copies ran while one was open for 0% of the time, Pallas kernels for 17%

profile of v3, /device:TPU:1, one launch (start us, length us, event | category | flops | bytes accessed | tf_op | source)
XLA Modules:
  0.0 126.5 jit_solution(11430544303378432206)
XLA Ops:
  2.9 3.7 %queries_near.1 = (bf16[2336,128]{1,0:T(8,128)(2,1)}, bf16[2336,128]{1,0:T(8,128)(2,1)}, f32[8,128]{1,0:T(8,128)}) custom-call(s32[2]{0:T(128)} %pad_add_fusion.place, bf16[128,4096]{1,0:T(8,128)(2,1)} %bitcast.13, bf16[128,4096]{1,0:T(8,128)(2,1)} %bitcast.15, bf16[128,4096]{1,0:T(8,128)(2,1)} %bitcast.17, f32[32,128]{1,0:T(8,128)} %bitcast.21, ...), custom_call_target="tpu_custom_call" | custom-call | bytes 33554432 | tf_op jit(solution)/shard_map/queries_near/pallas_call | solution.py:102
  9.5 2.4 %collective-permute-done.2.refs_3_ = bf16[256,128]{1,0:T(8,128)(2,1)S(1)} collective-permute-done((bf16[256,128]{1,0:T(8,128)(2,1)S(1)}, bf16[256,128]{1,0:T(8,128)(2,1)S(1)}, u32[]{:S(2)}, u32[]{:S(2)}) %collective-permute-start.2) | collective-permute-done | bytes 65568 | tf_op jit(solution)/shard_map/keys_values/ppermute | solution.py:454
  13.2 2.6 %collective-permute-start.5 = (bf16[1024,128]{1,0:T(8,128)(2,1)S(1)}, bf16[1024,128]{1,0:T(8,128)(2,1)S(1)}, u32[]{:S(2)}, u32[]{:S(2)}) collective-permute-start(bf16[1024,128]{1,0:T(8,128)(2,1)S(1)} %get-tuple-element.36.refs_0_), channel_id=1, source_target_pairs={{0,12},{1,13},{2,14},{3,15},{4,0},{5,1},{6,2},{7,3},{8,4},{9,5},{1... | collective-permute-start | bytes 786440 | tf_op jit(solution)/shard_map/keys_values_ring/ppermute | solution.py:457
  16.9 3.6 %queries_far.1 = (bf16[2080,128]{1,0:T(8,128)(2,1)}, bf16[2080,128]{1,0:T(8,128)(2,1)}, f32[8,128]{1,0:T(8,128)}) custom-call(s32[2]{0:T(128)} %pad_add_fusion.place, bf16[128,4096]{1,0:T(8,128)(2,1)} %bitcast.14, bf16[128,4096]{1,0:T(8,128)(2,1)} %bitcast.16, bf16[128,4096]{1,0:T(8,128)(2,1)} %bitcast.18, f32[32,128]{1,0:T(8,128)} %bitcast.22, ...), custom_call_target="tpu_custom_call" | custom-call | bytes 33554432 | tf_op jit(solution)/shard_map/queries_far/pallas_call | solution.py:102
  20.5 1.7 %collective-permute-start.6 = (bf16[2080,128]{1,0:T(8,128)(2,1)}, bf16[2080,128]{1,0:T(8,128)(2,1)S(1)}, u32[]{:S(2)}, u32[]{:S(2)}) collective-permute-start(bf16[2080,128]{1,0:T(8,128)(2,1)} %get-tuple-element.40), channel_id=1, source_target_pairs={{0,2},{1,3},{2,0},{3,1},{4,6},{5,7},{6,4},{7,5},{8,10},{9,11},{10,... | collective-permute-start | bytes 1597448 | tf_op jit(solution)/shard_map/queries_far/ppermute | solution.py:454
  22.3 2.2 %collective-permute-start.7 = (bf16[2080,128]{1,0:T(8,128)(2,1)}, bf16[2080,128]{1,0:T(8,128)(2,1)S(1)}, u32[]{:S(2)}, u32[]{:S(2)}) collective-permute-start(bf16[2080,128]{1,0:T(8,128)(2,1)} %get-tuple-element.41), channel_id=1, source_target_pairs={{0,3},{1,2},{2,1},{3,0},{4,7},{5,6},{6,5},{7,4},{8,11},{9,10},{10,... | collective-permute-start | bytes 1597448 | tf_op jit(solution)/shard_map/queries_far/ppermute | solution.py:454
  24.5 6.6 %collective-permute-done.3.refs_1_.refs_0_ = bf16[1024,128]{1,0:T(8,128)(2,1)S(1)} collective-permute-done((bf16[1024,128]{1,0:T(8,128)(2,1)S(1)}, bf16[1024,128]{1,0:T(8,128)(2,1)S(1)}, u32[]{:S(2)}, u32[]{:S(2)}) %collective-permute-start.3) | collective-permute-done | bytes 262176 | tf_op jit(solution)/shard_map/keys_values_ring/ppermute | solution.py:457
  32.9 2.1 %collective-permute-start.10 = (bf16[128,1280]{1,0:T(8,128)(2,1)S(1)}, bf16[128,1280]{1,0:T(8,128)(2,1)S(1)}, u32[]{:S(2)}, u32[]{:S(2)}) collective-permute-start(bf16[128,1280]{1,0:T(8,128)(2,1)S(1)} %get-tuple-element.46), channel_id=1, source_target_pairs={{0,12},{1,13},{2,14},{3,15},{4,0},{5,1},{6,2},{7,3},{8,4},{9,5},{1... | collective-permute-start | bytes 983048 | tf_op jit(solution)/shard_map/inputs_ring/ppermute | solution.py:457
  35.0 5.2 %attention_near.1 = (bf16[2048,128]{1,0:T(8,128)(2,1)S(1)}, f32[16,256,128]{2,1,0:T(8,128)S(1)}) custom-call(s32[2]{0:T(128)S(1)} %copy-done.3, s32[1,16]{1,0:T(1,128)S(1)} %copy-done.5, bf16[1024,128]{1,0:T(8,128)(2,1)S(1)} %get-tuple-element.36.refs_0_, bf16[1024,128]{1,0:T(8,128)(2,1)S(1)} %collective-permute-done.3.refs_1_.refs_0_, ...), custom_call_target="tpu_custom_call" | custom-call | tf_op jit(solution)/shard_map/attention_near/pallas_call | solution.py:315
  40.2 6.4 %collective-permute-done.7.refs_5_ = bf16[2080,128]{1,0:T(8,128)(2,1)S(1)} collective-permute-done((bf16[2080,128]{1,0:T(8,128)(2,1)}, bf16[2080,128]{1,0:T(8,128)(2,1)S(1)}, u32[]{:S(2)}, u32[]{:S(2)}) %collective-permute-start.7) | collective-permute-done | bytes 532512 | tf_op jit(solution)/shard_map/queries_far/ppermute | solution.py:454
  46.5 2.8 %collective-permute-done.8.refs_1_ = bf16[128,1280]{1,0:T(8,128)(2,1)S(1)} collective-permute-done((bf16[128,1280]{1,0:T(8,128)(2,1)S(1)}, bf16[128,1280]{1,0:T(8,128)(2,1)S(1)}, u32[]{:S(2)}, u32[]{:S(2)}) %collective-permute-start.8) | collective-permute-done | bytes 327712 | tf_op jit(solution)/shard_map/inputs_ring/ppermute | solution.py:457
  51.4 1.7 %collective-permute-start.14 = (bf16[512,1280]{1,0:T(8,128)(2,1)S(1)}, bf16[512,1280]{1,0:T(8,128)(2,1)S(1)}, u32[]{:S(2)}, u32[]{:S(2)}) collective-permute-start(bf16[512,1280]{1,0:T(8,128)(2,1)S(1)} %inputs_side.1.refs_7_.refs_4_), channel_id=1, source_target_pairs={{0,2},{1,3},{2,0},{3,1},{4,6},{5,7},{6,4},{7,5},{8,10},{9,11},{10,... | collective-permute-start | bytes 3932168 | tf_op jit(solution)/shard_map/inputs_side/ppermute | solution.py:454
  53.2 7.3 %attention_far.1 = (bf16[2560,128]{1,0:T(8,128)(2,1)S(1)}, f32[1024,128]{1,0:T(8,128)S(1)}, bf16[1024,128]{1,0:T(8,128)(2,1)S(1)}, bf16[1024,128]{1,0:T(8,128)(2,1)S(1)}, bf16[1024,128]{1,0:T(8,128)(2,1)S(1)}) custom-call(s32[2]{0:T(128)S(1)} %copy-done.3, s32[1,16]{1,0:T(1,128)S(1)} %copy-done.5, bf16[1024,128]{1,0:T(8,128)(2,1)S(1)} %get-tuple-element.36.refs_0_, ...), custom_call_target="tpu_custom_call" | custom-call | tf_op jit(solution)/shard_map/attention_far/pallas_call | solution.py:315
  61.3 4.3 %collective-permute-start.12 = (bf16[1024,128]{1,0:T(8,128)(2,1)S(1)}, bf16[1024,128]{1,0:T(8,128)(2,1)S(1)}, u32[]{:S(2)}, u32[]{:S(2)}) collective-permute-start(bf16[1024,128]{1,0:T(8,128)(2,1)S(1)} %get-tuple-element.49), channel_id=1, source_target_pairs={{0,12},{1,13},{2,14},{3,15},{4,0},{5,1},{6,2},{7,3},{8,4},{9,5},{1... | collective-permute-start | bytes 786440 | tf_op jit(solution)/shard_map/kv_gradients/ppermute | solution.py:457
  66.1 3.3 %collective-permute-done.11.refs_0_ = bf16[1024,128]{1,0:T(8,128)(2,1)S(1)} collective-permute-done((bf16[1024,128]{1,0:T(8,128)(2,1)S(1)}, bf16[1024,128]{1,0:T(8,128)(2,1)S(1)}, u32[]{:S(2)}, u32[]{:S(2)}) %collective-permute-start.11) | collective-permute-done | bytes 262176 | tf_op jit(solution)/shard_map/kv_gradients/ppermute | solution.py:457
  69.4 8.2 %collective-permute-done.12.refs_1_ = bf16[1024,128]{1,0:T(8,128)(2,1)S(1)} collective-permute-done((bf16[1024,128]{1,0:T(8,128)(2,1)S(1)}, bf16[1024,128]{1,0:T(8,128)(2,1)S(1)}, u32[]{:S(2)}, u32[]{:S(2)}) %collective-permute-start.12) | collective-permute-done | bytes 262176 | tf_op jit(solution)/shard_map/kv_gradients/ppermute | solution.py:457
  77.6 4.5 %collective-permute-done.14.refs_3_ = bf16[512,1280]{1,0:T(8,128)(2,1)S(1)} collective-permute-done((bf16[512,1280]{1,0:T(8,128)(2,1)S(1)}, bf16[512,1280]{1,0:T(8,128)(2,1)S(1)}, u32[]{:S(2)}, u32[]{:S(2)}) %collective-permute-start.14) | collective-permute-done | bytes 1310752 | tf_op jit(solution)/shard_map/inputs_side/ppermute | solution.py:454
  84.8 2.1 %collective-permute-start.19 = (bf16[1024,128]{1,0:T(8,128)(2,1)S(1)}, bf16[1024,128]{1,0:T(8,128)(2,1)S(1)}, u32[]{:S(2)}, u32[]{:S(2)}) collective-permute-start(bf16[1024,128]{1,0:T(8,128)(2,1)S(1)} %get-tuple-element.53.total.refs_0_), channel_id=1, source_target_pairs={{0,12},{1,13},{2,14},{3,15},{4,0},{5,1},{6,2},{7,3},{8,4},{9,5},{1... | collective-permute-start | bytes 786440 | tf_op jit(solution)/shard_map/kv_gradients/ppermute | solution.py:457
  88.0 4.5 %collective-permute-done.19.rest_2_.refs_3_ = bf16[1024,128]{1,0:T(8,128)(2,1)S(1)} collective-permute-done((bf16[1024,128]{1,0:T(8,128)(2,1)S(1)}, bf16[1024,128]{1,0:T(8,128)(2,1)S(1)}, u32[]{:S(2)}, u32[]{:S(2)}) %collective-permute-start.19) | collective-permute-done | bytes 262176 | tf_op jit(solution)/shard_map/kv_gradients/ppermute | solution.py:457
  92.5 8.3 %collective-permute-done.18.rest_1_.refs_2_ = bf16[1024,128]{1,0:T(8,128)(2,1)S(1)} collective-permute-done((bf16[1024,128]{1,0:T(8,128)(2,1)S(1)}, bf16[1024,128]{1,0:T(8,128)(2,1)S(1)}, u32[]{:S(2)}, u32[]{:S(2)}) %collective-permute-start.18) | collective-permute-done | bytes 262176 | tf_op jit(solution)/shard_map/kv_gradients/ppermute | solution.py:457
  102.5 2.5 %projection.1 = bf16[32,80,128]{2,1,0:T(8,128)(2,1)} custom-call(bf16[1024,128]{1,0:T(8,128)(2,1)S(1)} %get-tuple-element.53.total.refs_0_, bf16[1024,128]{1,0:T(8,128)(2,1)S(1)} %collective-permute-done.17.rest_0_.refs_1_, bf16[1024,128]{1,0:T(8,128)(2,1)S(1)} %collective-permute-done.18.rest_1_.refs_2_, ...), custom_call_target="tpu_custom_call" | custom-call | tf_op jit(solution)/shard_map/projection/pallas_call | solution.py:514
  105.0 7.9 %all-to-all-start = ((bf16[32,80,128]{2,1,0:T(8,128)(2,1)}), bf16[32,80,128]{2,1,0:T(8,128)(2,1)S(1)}, u32[]{:S(2)}, u32[]{:S(2)}) async-start(bf16[32,80,128]{2,1,0:T(8,128)(2,1)} %projection.1), calls=%async_computation | async-start | bytes 1310720 | tf_op jit(solution)/shard_map/projection_sum/all_to_all | solution.py:545
  113.0 1.9 %own_gradients.3 = (bf16[128,4096]{1,0:T(8,128)(2,1)}, bf16[128,512]{1,0:T(8,128)(2,1)}, bf16[128,512]{1,0:T(8,128)(2,1)}) custom-call(s32[2]{0:T(128)S(1)} %copy-done.3, bf16[2048,128]{1,0:T(8,128)(2,1)S(1)} %get-tuple-element.38.refs_6_.near, bf16[2560,128]{1,0:T(8,128)(2,1)S(1)} %collective-permute-done.16.side, ...), custom_call_target="tpu_custom_call" | custom-call | bytes 67108864 | tf_op jit(solution)/shard_map/own_gradients/pallas_call | solution.py:532
  114.9 10.8 %all-to-all-done.parts = bf16[32,80,128]{2,1,0:T(8,128)(2,1)S(1)} async-done(((bf16[32,80,128]{2,1,0:T(8,128)(2,1)}), bf16[32,80,128]{2,1,0:T(8,128)(2,1)S(1)}, u32[]{:S(2)}, u32[]{:S(2)}) %all-to-all-start) | async-done | bytes 655392 | tf_op jit(solution)/shard_map/projection_sum/all_to_all | solution.py:545
  (52 shorter events, 19.0 us)
Async XLA Ops:
  6.6 5.9 %collective-permute-start = (bf16[2336,128]{1,0:T(8,128)(2,1)}, bf16[2336,128]{1,0:T(8,128)(2,1)S(1)}, u32[]{:S(2)}, u32[]{:S(2)}) collective-permute-start(bf16[2336,128]{1,0:T(8,128)(2,1)} %get-tuple-element.34), channel_id=1, source_target_pairs={{0,1},{1,0},{2,3},{3,2},{4,5},{5,4},{6,7},{7,6},{8,9},{9,8},{10,11... | collective-permute-start | bytes 1794056 | tf_op jit(solution)/shard_map/queries_near/ppermute | solution.py:454
  8.1 3.8 %collective-permute-start.2 = (bf16[256,128]{1,0:T(8,128)(2,1)S(1)}, bf16[256,128]{1,0:T(8,128)(2,1)S(1)}, u32[]{:S(2)}, u32[]{:S(2)}) collective-permute-start(bf16[256,128]{1,0:T(8,128)(2,1)S(1)} %copy-done.7), channel_id=1, source_target_pairs={{0,3},{1,2},{2,1},{3,0},{4,7},{5,6},{6,5},{7,4},{8,11},{9,10},{10,... | collective-permute-start | bytes 196616 | tf_op jit(solution)/shard_map/keys_values/ppermute | solution.py:454
  9.4 3.1 %collective-permute-start.1 = (bf16[256,128]{1,0:T(8,128)(2,1)S(1)}, bf16[256,128]{1,0:T(8,128)(2,1)S(1)}, u32[]{:S(2)}, u32[]{:S(2)}) collective-permute-start(bf16[256,128]{1,0:T(8,128)(2,1)S(1)} %copy-done.6), channel_id=1, source_target_pairs={{0,2},{1,3},{2,0},{3,1},{4,6},{5,7},{6,4},{7,5},{8,10},{9,11},{10,... | collective-permute-start | bytes 196616 | tf_op jit(solution)/shard_map/keys_values/ppermute | solution.py:454
  13.2 11.3 %collective-permute-start.5 = (bf16[1024,128]{1,0:T(8,128)(2,1)S(1)}, bf16[1024,128]{1,0:T(8,128)(2,1)S(1)}, u32[]{:S(2)}, u32[]{:S(2)}) collective-permute-start(bf16[1024,128]{1,0:T(8,128)(2,1)S(1)} %get-tuple-element.36.refs_0_), channel_id=1, source_target_pairs={{0,12},{1,13},{2,14},{3,15},{4,0},{5,1},{6,2},{7,3},{8,4},{9,5},{1... | collective-permute-start | bytes 786440 | tf_op jit(solution)/shard_map/keys_values_ring/ppermute | solution.py:457
  15.7 8.7 %collective-permute-start.4 = (bf16[1024,128]{1,0:T(8,128)(2,1)S(1)}, bf16[1024,128]{1,0:T(8,128)(2,1)S(1)}, u32[]{:S(2)}, u32[]{:S(2)}) collective-permute-start(bf16[1024,128]{1,0:T(8,128)(2,1)S(1)} %get-tuple-element.36.refs_0_), channel_id=1, source_target_pairs={{0,8},{1,9},{2,10},{3,11},{4,12},{5,13},{6,14},{7,15},{8,0},{9,1},... | collective-permute-start | bytes 786440 | tf_op jit(solution)/shard_map/keys_values_ring/ppermute | solution.py:457
  16.3 14.8 %collective-permute-start.3 = (bf16[1024,128]{1,0:T(8,128)(2,1)S(1)}, bf16[1024,128]{1,0:T(8,128)(2,1)S(1)}, u32[]{:S(2)}, u32[]{:S(2)}) collective-permute-start(bf16[1024,128]{1,0:T(8,128)(2,1)S(1)} %get-tuple-element.36.refs_0_), channel_id=1, source_target_pairs={{0,4},{1,5},{2,6},{3,7},{4,8},{5,9},{6,10},{7,11},{8,12},{9,13},{1... | collective-permute-start | bytes 786440 | tf_op jit(solution)/shard_map/keys_values_ring/ppermute | solution.py:457
  16.9 14.2 %copy-start.3 = (s32[2]{0:T(128)S(1)}, s32[2]{0:T(128)}, u32[]{:S(2)}) copy-start(s32[2]{0:T(128)} %pad_add_fusion.place) | copy-start | bytes 28
  20.5 19.7 %collective-permute-start.6 = (bf16[2080,128]{1,0:T(8,128)(2,1)}, bf16[2080,128]{1,0:T(8,128)(2,1)S(1)}, u32[]{:S(2)}, u32[]{:S(2)}) collective-permute-start(bf16[2080,128]{1,0:T(8,128)(2,1)} %get-tuple-element.40), channel_id=1, source_target_pairs={{0,2},{1,3},{2,0},{3,1},{4,6},{5,7},{6,4},{7,5},{8,10},{9,11},{10,... | collective-permute-start | bytes 1597448 | tf_op jit(solution)/shard_map/queries_far/ppermute | solution.py:454
  22.3 24.3 %collective-permute-start.7 = (bf16[2080,128]{1,0:T(8,128)(2,1)}, bf16[2080,128]{1,0:T(8,128)(2,1)S(1)}, u32[]{:S(2)}, u32[]{:S(2)}) collective-permute-start(bf16[2080,128]{1,0:T(8,128)(2,1)} %get-tuple-element.41), channel_id=1, source_target_pairs={{0,3},{1,2},{2,1},{3,0},{4,7},{5,6},{6,5},{7,4},{8,11},{9,10},{10,... | collective-permute-start | bytes 1597448 | tf_op jit(solution)/shard_map/queries_far/ppermute | solution.py:454
  32.2 17.1 %collective-permute-start.8 = (bf16[128,1280]{1,0:T(8,128)(2,1)S(1)}, bf16[128,1280]{1,0:T(8,128)(2,1)S(1)}, u32[]{:S(2)}, u32[]{:S(2)}) collective-permute-start(bf16[128,1280]{1,0:T(8,128)(2,1)S(1)} %get-tuple-element.44), channel_id=1, source_target_pairs={{0,4},{1,5},{2,6},{3,7},{4,8},{5,9},{6,10},{7,11},{8,12},{9,13},{1... | collective-permute-start | bytes 983048 | tf_op jit(solution)/shard_map/inputs_ring/ppermute | solution.py:457
  32.3 17.0 %collective-permute-start.9 = (bf16[128,1280]{1,0:T(8,128)(2,1)S(1)}, bf16[128,1280]{1,0:T(8,128)(2,1)S(1)}, u32[]{:S(2)}, u32[]{:S(2)}) collective-permute-start(bf16[128,1280]{1,0:T(8,128)(2,1)S(1)} %get-tuple-element.45), channel_id=1, source_target_pairs={{0,8},{1,9},{2,10},{3,11},{4,12},{5,13},{6,14},{7,15},{8,0},{9,1},... | collective-permute-start | bytes 983048 | tf_op jit(solution)/shard_map/inputs_ring/ppermute | solution.py:457
  32.9 16.8 %collective-permute-start.10 = (bf16[128,1280]{1,0:T(8,128)(2,1)S(1)}, bf16[128,1280]{1,0:T(8,128)(2,1)S(1)}, u32[]{:S(2)}, u32[]{:S(2)}) collective-permute-start(bf16[128,1280]{1,0:T(8,128)(2,1)S(1)} %get-tuple-element.46), channel_id=1, source_target_pairs={{0,12},{1,13},{2,14},{3,15},{4,0},{5,1},{6,2},{7,3},{8,4},{9,5},{1... | collective-permute-start | bytes 983048 | tf_op jit(solution)/shard_map/inputs_ring/ppermute | solution.py:457
  49.7 27.9 %collective-permute-start.15 = (bf16[512,1280]{1,0:T(8,128)(2,1)S(1)}, bf16[512,1280]{1,0:T(8,128)(2,1)S(1)}, u32[]{:S(2)}, u32[]{:S(2)}) collective-permute-start(bf16[512,1280]{1,0:T(8,128)(2,1)S(1)} %inputs_side.1.refs_7_.refs_4_), channel_id=1, source_target_pairs={{0,1},{1,0},{2,3},{3,2},{4,5},{5,4},{6,7},{7,6},{8,9},{9,8},{10,11... | collective-permute-start | bytes 3932168 | tf_op jit(solution)/shard_map/inputs_side/ppermute | solution.py:454
  51.4 30.7 %collective-permute-start.14 = (bf16[512,1280]{1,0:T(8,128)(2,1)S(1)}, bf16[512,1280]{1,0:T(8,128)(2,1)S(1)}, u32[]{:S(2)}, u32[]{:S(2)}) collective-permute-start(bf16[512,1280]{1,0:T(8,128)(2,1)S(1)} %inputs_side.1.refs_7_.refs_4_), channel_id=1, source_target_pairs={{0,2},{1,3},{2,0},{3,1},{4,6},{5,7},{6,4},{7,5},{8,10},{9,11},{10,... | collective-permute-start | bytes 3932168 | tf_op jit(solution)/shard_map/inputs_side/ppermute | solution.py:454
  60.5 8.9 %collective-permute-start.11 = (bf16[1024,128]{1,0:T(8,128)(2,1)S(1)}, bf16[1024,128]{1,0:T(8,128)(2,1)S(1)}, u32[]{:S(2)}, u32[]{:S(2)}) collective-permute-start(bf16[1024,128]{1,0:T(8,128)(2,1)S(1)} %get-tuple-element.48), channel_id=1, source_target_pairs={{0,8},{1,9},{2,10},{3,11},{4,12},{5,13},{6,14},{7,15},{8,0},{9,1},... | collective-permute-start | bytes 786440 | tf_op jit(solution)/shard_map/kv_gradients/ppermute | solution.py:457
  61.3 16.3 %collective-permute-start.12 = (bf16[1024,128]{1,0:T(8,128)(2,1)S(1)}, bf16[1024,128]{1,0:T(8,128)(2,1)S(1)}, u32[]{:S(2)}, u32[]{:S(2)}) collective-permute-start(bf16[1024,128]{1,0:T(8,128)(2,1)S(1)} %get-tuple-element.49), channel_id=1, source_target_pairs={{0,12},{1,13},{2,14},{3,15},{4,0},{5,1},{6,2},{7,3},{8,4},{9,5},{1... | collective-permute-start | bytes 786440 | tf_op jit(solution)/shard_map/kv_gradients/ppermute | solution.py:457
  65.6 12.0 %collective-permute-start.13 = (bf16[1024,128]{1,0:T(8,128)(2,1)S(1)}, bf16[1024,128]{1,0:T(8,128)(2,1)S(1)}, u32[]{:S(2)}, u32[]{:S(2)}) collective-permute-start(bf16[1024,128]{1,0:T(8,128)(2,1)S(1)} %get-tuple-element.50), channel_id=1, source_target_pairs={{0,4},{1,5},{2,6},{3,7},{4,8},{5,9},{6,10},{7,11},{8,12},{9,13},{1... | collective-permute-start | bytes 786440 | tf_op jit(solution)/shard_map/kv_gradients/ppermute | solution.py:457
  82.4 20.1 %collective-permute-start.21 = (bf16[512,1280]{1,0:T(8,128)(2,1)S(1)}, bf16[512,1280]{1,0:T(8,128)(2,1)S(1)}, u32[]{:S(2)}, u32[]{:S(2)}) collective-permute-start(bf16[512,1280]{1,0:T(8,128)(2,1)S(1)} %get-tuple-element.57.refs_6_), channel_id=1, source_target_pairs={{0,1},{1,0},{2,3},{3,2},{4,5},{5,4},{6,7},{7,6},{8,9},{9,8},{10,11... | collective-permute-start | bytes 3932168 | tf_op jit(solution)/shard_map/kv_gradients/ppermute | solution.py:454
  83.3 17.6 %collective-permute-start.16 = (bf16[2560,128]{1,0:T(8,128)(2,1)S(1)}, bf16[2560,128]{1,0:T(8,128)(2,1)S(1)}, u32[]{:S(2)}, u32[]{:S(2)}) collective-permute-start(bf16[2560,128]{1,0:T(8,128)(2,1)S(1)} %get-tuple-element.52), channel_id=1, source_target_pairs={{0,2},{1,3},{2,0},{3,1},{4,6},{5,7},{6,4},{7,5},{8,10},{9,11},{10,... | collective-permute-start | bytes 1966088 | tf_op jit(solution)/shard_map/own_gradients/ppermute | solution.py:454
  84.8 7.8 %collective-permute-start.19 = (bf16[1024,128]{1,0:T(8,128)(2,1)S(1)}, bf16[1024,128]{1,0:T(8,128)(2,1)S(1)}, u32[]{:S(2)}, u32[]{:S(2)}) collective-permute-start(bf16[1024,128]{1,0:T(8,128)(2,1)S(1)} %get-tuple-element.53.total.refs_0_), channel_id=1, source_target_pairs={{0,12},{1,13},{2,14},{3,15},{4,0},{5,1},{6,2},{7,3},{8,4},{9,5},{1... | collective-permute-start | bytes 786440 | tf_op jit(solution)/shard_map/kv_gradients/ppermute | solution.py:457
  86.8 14.0 %collective-permute-start.18 = (bf16[1024,128]{1,0:T(8,128)(2,1)S(1)}, bf16[1024,128]{1,0:T(8,128)(2,1)S(1)}, u32[]{:S(2)}, u32[]{:S(2)}) collective-permute-start(bf16[1024,128]{1,0:T(8,128)(2,1)S(1)} %get-tuple-element.53.total.refs_0_), channel_id=1, source_target_pairs={{0,4},{1,5},{2,6},{3,7},{4,8},{5,9},{6,10},{7,11},{8,12},{9,13},{1... | collective-permute-start | bytes 786440 | tf_op jit(solution)/shard_map/kv_gradients/ppermute | solution.py:457
  86.8 14.0 %collective-permute-start.17 = (bf16[1024,128]{1,0:T(8,128)(2,1)S(1)}, bf16[1024,128]{1,0:T(8,128)(2,1)S(1)}, u32[]{:S(2)}, u32[]{:S(2)}) collective-permute-start(bf16[1024,128]{1,0:T(8,128)(2,1)S(1)} %get-tuple-element.53.total.refs_0_), channel_id=1, source_target_pairs={{0,8},{1,9},{2,10},{3,11},{4,12},{5,13},{6,14},{7,15},{8,0},{9,1},... | collective-permute-start | bytes 786440 | tf_op jit(solution)/shard_map/kv_gradients/ppermute | solution.py:457
  100.9 12.1 %collective-permute-start.20 = (bf16[2560,128]{1,0:T(8,128)(2,1)S(1)}, bf16[2560,128]{1,0:T(8,128)(2,1)S(1)}, u32[]{:S(2)}, u32[]{:S(2)}) collective-permute-start(bf16[2560,128]{1,0:T(8,128)(2,1)S(1)} %own_gradients.2), channel_id=1, source_target_pairs={{0,1},{1,0},{2,3},{3,2},{4,5},{5,4},{6,7},{7,6},{8,9},{9,8},{10,11... | collective-permute-start | bytes 1966088 | tf_op jit(solution)/shard_map/own_gradients/ppermute | solution.py:454
  105.0 20.7 %all-to-all-start = ((bf16[32,80,128]{2,1,0:T(8,128)(2,1)}), bf16[32,80,128]{2,1,0:T(8,128)(2,1)S(1)}, u32[]{:S(2)}, u32[]{:S(2)}) async-start(bf16[32,80,128]{2,1,0:T(8,128)(2,1)} %projection.1), calls=%async_computation | async-start | bytes 1310720 | tf_op jit(solution)/shard_map/projection_sum/all_to_all | solution.py:545
  (7 other events, 43.8 us)

commit v4 on v3

--- a/solution.py
+++ b/solution.py
@@ -21,6 +21,7 @@
 PACK = 2 * ROWS + 32
 SCALE = HEAD_SIZE ** (-0.5)
 RING_ORDER = (2, 1, 3)
+KV_ORDER = (0, 1, 3, 2)
 LOG2E = 1.4426950408889634
 LSE_SCALE = HEAD_SIZE**0.5
 F32 = jnp.float32
@@ -56,15 +57,12 @@
     )
 
 
-def split_kv_kernel(place, key_ref, value_ref, *outs):
-    own = place[1]
-    for k, out in enumerate(outs):
-        col = pl.multiple_of((own ^ k) * HEAD_SIZE, HEAD_SIZE)
-        out[0:BLK, :] = key_ref[:, pl.ds(col, HEAD_SIZE)]
-        out[BLK:, :] = value_ref[:, pl.ds(col, HEAD_SIZE)]
-
-
-def split_queries_kernel(place, query_ref, gradient_ref, output_ref, lse_ref, kv_ref, after, *outs):
+def split_queries_kernel(near, place, query_ref, gradient_ref, output_ref, lse_ref, *refs):
+    if near:
+        key_ref, value_ref, outs = refs[0], refs[1], refs[2:]
+        kv_outs, outs = outs[-3:], outs[:-3]
+    else:
+        outs = refs[1:]
     outs, token = outs[:-1], outs[-1]
     token[...] = jnp.zeros_like(token)
     lane = lax.broadcasted_iota(jnp.int32, (BLK, 128), 1)
@@ -81,6 +79,15 @@
         low = (rows - high.astype(F32)).astype(BF16)
         return jnp.concatenate([high, low], axis=0)
 
+    if near:
+
+        @pl.when(pl.program_id(0) == 0)
+        def _():
+            for k, out in ((0, kv_outs[0]), (1, outs[1].at[pl.ds(PACK, 2 * BLK), :]), (2, kv_outs[1]), (3, kv_outs[2])):
+                col = pl.multiple_of((place[1] ^ k) * HEAD_SIZE, HEAD_SIZE)
+                out[0:BLK, :] = key_ref[:, pl.ds(col, HEAD_SIZE)]
+                out[BLK:, :] = value_ref[:, pl.ds(col, HEAD_SIZE)]
+
     for k, out in enumerate(outs):
 
         @pl.when(pl.program_id(0) == k)
@@ -91,17 +98,18 @@
                 out[ROWS + h * BLK : ROWS + (h + 1) * BLK, :] = gradient_ref[:, cols]
             out[2 * ROWS : 2 * ROWS + 16, :] = split(lse)
             out[2 * ROWS + 16 : 2 * ROWS + 32, :] = split(delta)
-            if out.shape[0] > PACK:
-                out[PACK:, :] = kv_ref[...]
-
-
-def split_queries(place, queries, gradient, output, lse, kv, after, first):
+
+
+def split_queries(place, queries, gradient, output, lse, first, *rest):
     count = SIDE // 2
+    near = first == 0
+    kv_whole = pl.BlockSpec((BLK, KEY_VALUE_HEADS * HEAD_SIZE), lambda k, place: (0, 0))
+    kv_piece = pl.BlockSpec((2 * BLK, HEAD_SIZE), lambda k, place: (0, 0))
     rows = PACK if first else PACK + 2 * BLK
     wide = pl.BlockSpec((BLK, GROUP * HEAD_SIZE), lambda k, place: (0, place[1] ^ (first + k)))
     return pl.pallas_call(
-        split_queries_kernel,
-        out_shape=[shape(rows)] * count + [shape(8, 128, F32)],
+        functools.partial(split_queries_kernel, near),
+        out_shape=[shape(rows)] * count + [shape(8, 128, F32)] + [shape(2 * BLK)] * (3 * near),
         grid_spec=pltpu.PrefetchScalarGridSpec(
             num_scalar_prefetch=1,
             grid=(count,),
@@ -110,20 +118,19 @@
                 wide,
                 wide,
                 pl.BlockSpec((GROUP, BLK), lambda k, place: (place[1] ^ (first + k), 0)),
-                pl.BlockSpec((2 * BLK, HEAD_SIZE), lambda k, place: (0, 0)),
-                pl.BlockSpec(memory_space=pl.ANY),
-            ],
+            ]
+            + ([kv_whole] * 2 if near else [pl.BlockSpec(memory_space=pl.ANY)]),
             out_specs=[pl.BlockSpec((rows, HEAD_SIZE), lambda k, place: (0, 0))] * count
-            + [pl.BlockSpec((8, 128), lambda k, place: (0, 0))],
+            + [pl.BlockSpec((8, 128), lambda k, place: (0, 0))]
+            + [kv_piece] * (3 * near),
         ),
         compiler_params=pltpu.CompilerParams(vmem_limit_bytes=56 * MIB),
         cost_estimate=pl.CostEstimate(flops=0, bytes_accessed=32 * MIB, transcendentals=0),
-    )(place, queries, gradient, output, lse, kv, after)
+    )(place, queries, gradient, output, lse, *rest)
 
 
 def stack_kernel(*refs):
-    out, token = refs[-2:]
-    token[...] = jnp.zeros_like(token)
+    out = refs[SIDE]
     rows = refs[0].shape[0]
     for k in range(SIDE):
         out[k * rows : (k + 1) * rows, :] = refs[k][refs[k].shape[0] - rows :, :]
@@ -144,11 +151,16 @@
 def attention_kernel(first, place, parents, *refs):
     last = first > 0
     kv_in, packs, refs = refs[:RING], refs[RING : RING + PAIR], refs[RING + PAIR :]
+    kv_in = [kv_in[KV_ORDER.index(s)] for s in range(RING)]
     if last:
         sums_in, dq_out, grad_outs, refs = refs[0], refs[2], refs[3 : 3 + RING], refs[3 + RING :]
     else:
         dq_out, sums_out, refs = refs[0], refs[1], refs[2:]
-    kv, kv_t, pack, query_t, gradient_t, terms, dq_acc, dq, acc, stage_own, stage, kv_sem, pack_sem, out_sem = refs
+    kv, kv_t, pack, query_t, gradient_t, terms, dq_acc, dq, kv_sem, pack_sem, out_sem = refs[:11]
+    if last:
+        acc, stage_own, stage = refs[11:]
+    else:
+        acc = sums_out
     ring, own = place[0], place[1]
 
     loads = []
@@ -160,12 +172,9 @@
     pack_loads = [
         pltpu.make_async_copy(packs[k].at[pl.ds(0, PACK), :], pack.at[k], pack_sem.at[k]) for k in range(PAIR)
     ]
-    if last:
-        pack_loads.append(pltpu.make_async_copy(sums_in, acc, pack_sem.at[PAIR]))
     for load in loads + pack_loads:
         load.start()
-    if not last:
-        acc[...] = jnp.zeros_like(acc)
+    acc[...] = sums_in[...] if last else jnp.zeros_like(acc)
     for load in loads:
         load.wait()
 
@@ -283,8 +292,6 @@
 
     stores = [store_dq(k) for k in range(PAIR)]
     if not last:
-        stores.append(pltpu.make_async_copy(acc, sums_out, out_sem.at[PAIR]))
-        stores[-1].start()
         for store in stores:
             store.wait()
         return
@@ -308,15 +315,21 @@
 def attention_call(place, parents, kv, packs, first, *rest):
     sum_shape = (RING * SIDE, 2 * BLK, HEAD_SIZE)
     hbm = pl.BlockSpec(memory_space=pl.ANY)
+    last_scratch = []
     if first:
+        last_scratch = [
+            pltpu.VMEM(sum_shape, F32),
+            pltpu.VMEM((ROWS, HEAD_SIZE), F32),
+            pltpu.VMEM((RING - 1, ROWS, HEAD_SIZE), BF16),
+        ]
         out_shape = [shape(PAIR * ROWS + 4 * BLK), shape(ROWS, kind=F32)] + [shape(ROWS)] * (RING - 1)
     else:
         out_shape = [shape(PAIR * ROWS), jax.ShapeDtypeStruct(sum_shape, F32)]
     return pl.pallas_call(
         functools.partial(attention_kernel, first),
         out_shape=out_shape,
-        in_specs=[smem()] * 2 + [hbm] * (RING + PAIR + len(rest)),
-        out_specs=[hbm] * len(out_shape),
+        in_specs=[smem()] * 2 + [hbm] * (RING + PAIR) + ([vmem(), hbm] if first else []),
+        out_specs=[hbm] * len(out_shape) if first else [hbm, vmem()],
         scratch_shapes=[
             pltpu.VMEM(sum_shape, BF16),
             pltpu.VMEM((RING * SIDE, 2 * HEAD_SIZE, 2 * BLK), BF16),
@@ -326,16 +339,14 @@
             pltpu.VMEM((ROWS, 128), BF16),
             pltpu.VMEM((ROWS, HEAD_SIZE), F32),
             pltpu.VMEM((PAIR, ROWS, HEAD_SIZE), BF16),
-            pltpu.VMEM(sum_shape, F32),
-            pltpu.VMEM((ROWS, HEAD_SIZE), F32),
-            pltpu.VMEM((RING - 1, ROWS, HEAD_SIZE), BF16),
             pltpu.SemaphoreType.DMA((RING * SIDE,)),
-            pltpu.SemaphoreType.DMA((PAIR + 1,)),
+            pltpu.SemaphoreType.DMA((PAIR,)),
             pltpu.SemaphoreType.DMA((PAIR + RING,)),
-        ],
+        ]
+        + last_scratch,
         compiler_params=pltpu.CompilerParams(vmem_limit_bytes=24 * MIB),
         cost_estimate=pl.CostEstimate(flops=0, bytes_accessed=0, transcendentals=0),
-    )(place, parents, *kv, *packs, *rest)
+    )(place, parents, *[kv[s] for s in KV_ORDER], *packs, *rest)
 
 
 def total_kernel(grad_own, *refs):
@@ -375,8 +386,8 @@
 
 def join_inputs_kernel(*refs):
     pieces, out = refs[:RING], refs[-1]
-    for s in range(RING):
-        out[s * BLK : (s + 1) * BLK, :] = pieces[s][...]
+    for s, piece in zip((0,) + RING_ORDER, pieces):
+        out[s * BLK : (s + 1) * BLK, :] = piece[...]
 
 
 def projection_kernel(*refs):
@@ -456,26 +467,27 @@
     def to_ring(x, s):
         return lax.ppermute(x, "ctx", ring_perm(s % RING))
 
-    with jax.named_scope("keys_values"):
-        kv_split = call(split_kv_kernel, [shape(2 * BLK)] * SIDE, 1, 2, limit=56)(
-            place, key_tensor[0], value_tensor[0]
-        )
-        kv_far = [to_side(kv_split[k], k) for k in (2, 3)]
-
-    query_args = (queries[0], output_gradient[0], attention_output[0], logsumexp_rows[0], kv_split[1])
-    with jax.named_scope("queries_near"):
-        near_own = split_queries(place, *query_args, kv_split[2], 0)
+    query_args = (queries[0], output_gradient[0], attention_output[0], logsumexp_rows[0])
+    with jax.named_scope("near"):
+        near_own = split_queries(place, *query_args, 0, key_tensor[0], value_tensor[0])
         packs_near = [near_own[0], to_side(near_own[1], 1)]
+        kv_first = near_own[3]
+        kv_far = [to_side(near_own[2 + k], k) for k in (2, 3)]
 
     with jax.named_scope("keys_values_ring"):
-        kv_own, token = call(stack_kernel, [shape(ROWS), shape(8, 128, F32)], 0, SIDE)(
-            kv_split[0], packs_near[1], *kv_far
-        )
+        kv_own, token = pl.pallas_call(
+            stack_kernel,
+            out_shape=[shape(ROWS), shape(8, 128, F32)],
+            in_specs=[vmem()] * SIDE,
+            out_specs=[vmem(), pl.BlockSpec(memory_space=pl.ANY)],
+            compiler_params=pltpu.CompilerParams(vmem_limit_bytes=20 * MIB),
+            cost_estimate=pl.CostEstimate(flops=0, bytes_accessed=0, transcendentals=0),
+        )(kv_first, packs_near[1], *kv_far)
         kv = {s: to_ring(kv_own, s) for s in RING_ORDER}
         kv = [kv_own] + [kv[s] for s in (1, 2, 3)]
 
     with jax.named_scope("queries_far"):
-        far_own = split_queries(place, *query_args, token, 2)
+        far_own = split_queries(place, *query_args, 2, token)
         packs_far = [to_side(far_own[k - 2], k) for k in (2, 3)]
 
     with jax.named_scope("inputs_ring"):
@@ -486,9 +498,8 @@
             1,
             n_any=4,
             scratch=[pltpu.VMEM((RING, BLK, quarter), BF16)],
-        )(place, layer_input[0], *kv[1:], packs_near[1])
-        from_ring = {s: to_ring(shares[s], s) for s in RING_ORDER}
-        from_ring = [shares[0]] + [from_ring[s] for s in (1, 2, 3)]
+        )(place, layer_input[0], kv[1], kv[3], kv[2], packs_near[1])
+        from_ring = [shares[0]] + [to_ring(shares[s], s) for s in RING_ORDER]
 
     with jax.named_scope("attention_near"):
         dq_near, sums = attention_call(place, parents, kv, packs_near, 0)
@@ -527,7 +538,7 @@
     with jax.named_scope("own_gradients"):
         side = to_side(side_out, 2)
         crossed = to_side(
-            call(relay_kernel, [shape(2 * ROWS + 4 * BLK)], 0, 3, n_any=3)(dq_near, side, grad_total, *grads[1:])[0], 1
+            call(relay_kernel, [shape(2 * ROWS + 4 * BLK)], 0, 3, n_any=3)(dq_near, side, grad_total, *grads[:0:-1])[0], 1
         )
         grad_queries, grad_keys, grad_values = call(
             join_kernel,

time: 127 us -> 123 us (0.969)
  waiting for transfers between devices: 58.9 us -> 53.4 us
  starting transfers between devices: 37.4 us -> 39.6 us
  Pallas kernels: 28.3 us -> 26.5 us
    ppermute x12, waiting for transfers between devices: 34.1 us -> 28.4 us  [to_ring(): return lax.ppermute(x, 'ctx', ring_perm(s % RING))]
    ppermute x12, starting transfers between devices: 15.2 us -> 20.4 us  [to_ring(): return lax.ppermute(x, 'ctx', ring_perm(s % RING))]
    ppermute x10, starting transfers between devices: 14.2 us -> 11 us  [to_side(): return lax.ppermute(x, 'ctx', side_perm(k))]
    pallas_call x4 -> x3, Pallas kernels: 9.07 us -> 7.36 us  [the longest x2 7.34 us: split_queries(): pl.pallas_call(functools.partial(split_queries_kernel, near), out_shape=[...]
  transfers between devices with their start and end apart: 23 -> 23, of which waited for: 12 -> 12; matrix products, arithmetic and copies ran while one was open for 0% -> 0% of each run, Pallas kernels for 17% -> 18%
where the time goes in v4:
time: 123 us; the launch traced here: 122 us
  waiting for transfers between devices  53.4 us (43%)
  starting transfers between devices  39.6 us (32%)
  Pallas kernels  26.5 us (22%)
  local copies, waits for them, and re-layouts  1.44 us (1%)
    ppermute x12, waiting for transfers between devices, to_ring(): return lax.ppermute(x, 'ctx', ring_perm(s % RING))  28.4 us
    ppermute x12, starting transfers between devices, to_ring(): return lax.ppermute(x, 'ctx', ring_perm(s % RING))  20.4 us
    ppermute x10, waiting for transfers between devices, to_side(): return lax.ppermute(x, 'ctx', side_perm(k))  14.1 us
    pallas_call x2, Pallas kernels, attention_call(): pl.pallas_call(functools.partial(attention_kernel, first), out_shape=out_...  12.4 us
    ppermute x10, starting transfers between devices, to_side(): return lax.ppermute(x, 'ctx', side_perm(k))  11 us
    all_to_all x1, waiting for transfers between devices, local(): lax.all_to_all(partial, ('dp', 'ctx'), 0, 0, axis_index_groups=groups, ti...  10.8 us
    all_to_all x1, starting transfers between devices, local(): lax.all_to_all(partial, ('dp', 'ctx'), 0, 0, axis_index_groups=groups, ti...  8.15 us
    pallas_call x2, Pallas kernels, split_queries(): pl.pallas_call(functools.partial(split_queries_kernel, near), out_shape=[...  7.34 us
  transfers between devices with their start and end apart: 23, of which 12 were waited for; matrix products, arithmetic and copies ran while one was open for 0% of the time, Pallas kernels for 18%

profile of v4, /device:TPU:1, one launch (start us, length us, event | category | flops | bytes accessed | tf_op | source)
XLA Modules:
  0.0 122.3 jit_solution(720599200715166777)
XLA Ops:
  1.3 3.8 %near.1 = (bf16[2336,128]{1,0:T(8,128)(2,1)}, bf16[2336,128]{1,0:T(8,128)(2,1)}, f32[8,128]{1,0:T(8,128)}, bf16[256,128]{1,0:T(8,128)(2,1)}, bf16[256,128]{1,0:T(8,128)(2,1)}, /*index=5*/bf16[256,128]{1,0:T(8,128)(2,1)}) custom-call(s32[2]{0:T(128)} %pad_add_fusion.place, bf16[128,4096]{1,0:T(8,128)(2,1)} %bitcast.13, bf16[128,4096]{1,0:T(8,128)(2,1)} %bitcast.15, ...), custom_call_target="tpu_custom_call" | custom-call | bytes 33554432 | tf_op jit(solution)/shard_map/near/pallas_call | solution.py:110
  8.2 2.1 %collective-permute-done.1.refs_2_ = bf16[256,128]{1,0:T(8,128)(2,1)S(1)} collective-permute-done((bf16[256,128]{1,0:T(8,128)(2,1)}, bf16[256,128]{1,0:T(8,128)(2,1)S(1)}, u32[]{:S(2)}, u32[]{:S(2)}) %collective-permute-start.1) | collective-permute-done | bytes 65568 | tf_op jit(solution)/shard_map/near/ppermute | solution.py:465
  10.4 1.8 %collective-permute-done.2.refs_3_ = bf16[256,128]{1,0:T(8,128)(2,1)S(1)} collective-permute-done((bf16[256,128]{1,0:T(8,128)(2,1)}, bf16[256,128]{1,0:T(8,128)(2,1)S(1)}, u32[]{:S(2)}, u32[]{:S(2)}) %collective-permute-start.2) | collective-permute-done | bytes 65568 | tf_op jit(solution)/shard_map/near/ppermute | solution.py:465
  13.6 2.7 %collective-permute-start.5 = (bf16[1024,128]{1,0:T(8,128)(2,1)S(1)}, bf16[1024,128]{1,0:T(8,128)(2,1)S(1)}, u32[]{:S(2)}, u32[]{:S(2)}) collective-permute-start(bf16[1024,128]{1,0:T(8,128)(2,1)S(1)} %get-tuple-element.34.refs_0_), channel_id=1, source_target_pairs={{0,8},{1,9},{2,10},{3,11},{4,12},{5,13},{6,14},{7,15},{8,0},{9,1},... | collective-permute-start | bytes 786440 | tf_op jit(solution)/shard_map/keys_values_ring/ppermute | solution.py:468
  17.9 3.6 %queries_far.1 = (bf16[2080,128]{1,0:T(8,128)(2,1)}, bf16[2080,128]{1,0:T(8,128)(2,1)}, f32[8,128]{1,0:T(8,128)}) custom-call(s32[2]{0:T(128)} %pad_add_fusion.place, bf16[128,4096]{1,0:T(8,128)(2,1)} %bitcast.14, bf16[128,4096]{1,0:T(8,128)(2,1)} %bitcast.16, bf16[128,4096]{1,0:T(8,128)(2,1)} %bitcast.18, f32[32,128]{1,0:T(8,128)} %bitcast.22, ...), custom_call_target="tpu_custom_call" | custom-call | bytes 33554432 | tf_op jit(solution)/shard_map/queries_far/pallas_call | solution.py:110
  22.6 1.7 %collective-permute-start.7 = (bf16[2080,128]{1,0:T(8,128)(2,1)}, bf16[2080,128]{1,0:T(8,128)(2,1)S(1)}, u32[]{:S(2)}, u32[]{:S(2)}) collective-permute-start(bf16[2080,128]{1,0:T(8,128)(2,1)} %get-tuple-element.39), channel_id=1, source_target_pairs={{0,3},{1,2},{2,1},{3,0},{4,7},{5,6},{6,5},{7,4},{8,11},{9,10},{10,... | collective-permute-start | bytes 1597448 | tf_op jit(solution)/shard_map/queries_far/ppermute | solution.py:465
  24.3 4.2 %collective-permute-done.4.refs_2_.refs_1_ = bf16[1024,128]{1,0:T(8,128)(2,1)S(1)} collective-permute-done((bf16[1024,128]{1,0:T(8,128)(2,1)S(1)}, bf16[1024,128]{1,0:T(8,128)(2,1)S(1)}, u32[]{:S(2)}, u32[]{:S(2)}) %collective-permute-start.4) | collective-permute-done | bytes 262176 | tf_op jit(solution)/shard_map/keys_values_ring/ppermute | solution.py:468
  30.1 2.8 %collective-permute-start.8 = (bf16[128,1280]{1,0:T(8,128)(2,1)S(1)}, bf16[128,1280]{1,0:T(8,128)(2,1)S(1)}, u32[]{:S(2)}, u32[]{:S(2)}) collective-permute-start(bf16[128,1280]{1,0:T(8,128)(2,1)S(1)} %get-tuple-element.42), channel_id=1, source_target_pairs={{0,8},{1,9},{2,10},{3,11},{4,12},{5,13},{6,14},{7,15},{8,0},{9,1},... | collective-permute-start | bytes 983048 | tf_op jit(solution)/shard_map/inputs_ring/ppermute | solution.py:468
  33.3 2.3 %collective-permute-start.10 = (bf16[128,1280]{1,0:T(8,128)(2,1)S(1)}, bf16[128,1280]{1,0:T(8,128)(2,1)S(1)}, u32[]{:S(2)}, u32[]{:S(2)}) collective-permute-start(bf16[128,1280]{1,0:T(8,128)(2,1)S(1)} %get-tuple-element.44), channel_id=1, source_target_pairs={{0,12},{1,13},{2,14},{3,15},{4,0},{5,1},{6,2},{7,3},{8,4},{9,5},{1... | collective-permute-start | bytes 983048 | tf_op jit(solution)/shard_map/inputs_ring/ppermute | solution.py:468
  35.6 5.0 %attention_near.1 = (bf16[2048,128]{1,0:T(8,128)(2,1)S(1)}, f32[16,256,128]{2,1,0:T(8,128)S(1)}) custom-call(s32[2]{0:T(128)S(1)} %copy-done.3, s32[1,16]{1,0:T(1,128)S(1)} %copy-done.5, bf16[1024,128]{1,0:T(8,128)(2,1)S(1)} %get-tuple-element.34.refs_0_, bf16[1024,128]{1,0:T(8,128)(2,1)S(1)} %collective-permute-done.3.refs_1_.refs_0_, ...), custom_call_target="tpu_custom_call" | custom-call | tf_op jit(solution)/shard_map/attention_near/pallas_call | solution.py:328
  40.7 6.5 %collective-permute-done.7.refs_5_ = bf16[2080,128]{1,0:T(8,128)(2,1)S(1)} collective-permute-done((bf16[2080,128]{1,0:T(8,128)(2,1)}, bf16[2080,128]{1,0:T(8,128)(2,1)S(1)}, u32[]{:S(2)}, u32[]{:S(2)}) %collective-permute-start.7) | collective-permute-done | bytes 532512 | tf_op jit(solution)/shard_map/queries_far/ppermute | solution.py:465
  50.3 7.4 %attention_far.1 = (bf16[2560,128]{1,0:T(8,128)(2,1)S(1)}, f32[1024,128]{1,0:T(8,128)S(1)}, bf16[1024,128]{1,0:T(8,128)(2,1)S(1)}, bf16[1024,128]{1,0:T(8,128)(2,1)S(1)}, bf16[1024,128]{1,0:T(8,128)(2,1)S(1)}) custom-call(s32[2]{0:T(128)S(1)} %copy-done.3, s32[1,16]{1,0:T(1,128)S(1)} %copy-done.5, bf16[1024,128]{1,0:T(8,128)(2,1)S(1)} %get-tuple-element.34.refs_0_, ...), custom_call_target="tpu_custom_call" | custom-call | tf_op jit(solution)/shard_map/attention_far/pallas_call | solution.py:328
  57.7 4.6 %collective-permute-start.11 = (bf16[1024,128]{1,0:T(8,128)(2,1)S(1)}, bf16[1024,128]{1,0:T(8,128)(2,1)S(1)}, u32[]{:S(2)}, u32[]{:S(2)}) collective-permute-start(bf16[1024,128]{1,0:T(8,128)(2,1)S(1)} %get-tuple-element.46), channel_id=1, source_target_pairs={{0,8},{1,9},{2,10},{3,11},{4,12},{5,13},{6,14},{7,15},{8,0},{9,1},... | collective-permute-start | bytes 786440 | tf_op jit(solution)/shard_map/kv_gradients/ppermute | solution.py:468
  64.0 4.4 %collective-permute-done.11.refs_0_ = bf16[1024,128]{1,0:T(8,128)(2,1)S(1)} collective-permute-done((bf16[1024,128]{1,0:T(8,128)(2,1)S(1)}, bf16[1024,128]{1,0:T(8,128)(2,1)S(1)}, u32[]{:S(2)}, u32[]{:S(2)}) %collective-permute-start.11) | collective-permute-done | bytes 262176 | tf_op jit(solution)/shard_map/kv_gradients/ppermute | solution.py:468
  68.5 7.1 %collective-permute-done.12.refs_1_ = bf16[1024,128]{1,0:T(8,128)(2,1)S(1)} collective-permute-done((bf16[1024,128]{1,0:T(8,128)(2,1)S(1)}, bf16[1024,128]{1,0:T(8,128)(2,1)S(1)}, u32[]{:S(2)}, u32[]{:S(2)}) %collective-permute-start.12) | collective-permute-done | bytes 262176 | tf_op jit(solution)/shard_map/kv_gradients/ppermute | solution.py:468
  75.6 3.7 %collective-permute-done.14.refs_3_ = bf16[512,1280]{1,0:T(8,128)(2,1)S(1)} collective-permute-done((bf16[512,1280]{1,0:T(8,128)(2,1)S(1)}, bf16[512,1280]{1,0:T(8,128)(2,1)S(1)}, u32[]{:S(2)}, u32[]{:S(2)}) %collective-permute-start.14) | collective-permute-done | bytes 1310752 | tf_op jit(solution)/shard_map/inputs_side/ppermute | solution.py:465
  81.9 1.8 %collective-permute-start.19 = (bf16[1024,128]{1,0:T(8,128)(2,1)S(1)}, bf16[1024,128]{1,0:T(8,128)(2,1)S(1)}, u32[]{:S(2)}, u32[]{:S(2)}) collective-permute-start(bf16[1024,128]{1,0:T(8,128)(2,1)S(1)} %get-tuple-element.51.total.refs_0_), channel_id=1, source_target_pairs={{0,8},{1,9},{2,10},{3,11},{4,12},{5,13},{6,14},{7,15},{8,0},{9,1},... | collective-permute-start | bytes 786440 | tf_op jit(solution)/shard_map/kv_gradients/ppermute | solution.py:468
  84.8 1.5 %collective-permute-start.17 = (bf16[1024,128]{1,0:T(8,128)(2,1)S(1)}, bf16[1024,128]{1,0:T(8,128)(2,1)S(1)}, u32[]{:S(2)}, u32[]{:S(2)}) collective-permute-start(bf16[1024,128]{1,0:T(8,128)(2,1)S(1)} %get-tuple-element.51.total.refs_0_), channel_id=1, source_target_pairs={{0,12},{1,13},{2,14},{3,15},{4,0},{5,1},{6,2},{7,3},{8,4},{9,5},{1... | collective-permute-start | bytes 786440 | tf_op jit(solution)/shard_map/kv_gradients/ppermute | solution.py:468
  86.3 4.6 %collective-permute-done.19.rest_2_.refs_1_ = bf16[1024,128]{1,0:T(8,128)(2,1)S(1)} collective-permute-done((bf16[1024,128]{1,0:T(8,128)(2,1)S(1)}, bf16[1024,128]{1,0:T(8,128)(2,1)S(1)}, u32[]{:S(2)}, u32[]{:S(2)}) %collective-permute-start.19) | collective-permute-done | bytes 262176 | tf_op jit(solution)/shard_map/kv_gradients/ppermute | solution.py:468
  91.0 6.3 %collective-permute-done.18.rest_1_.refs_2_ = bf16[1024,128]{1,0:T(8,128)(2,1)S(1)} collective-permute-done((bf16[1024,128]{1,0:T(8,128)(2,1)S(1)}, bf16[1024,128]{1,0:T(8,128)(2,1)S(1)}, u32[]{:S(2)}, u32[]{:S(2)}) %collective-permute-start.18) | collective-permute-done | bytes 262176 | tf_op jit(solution)/shard_map/kv_gradients/ppermute | solution.py:468
  98.0 2.5 %projection.1 = bf16[32,80,128]{2,1,0:T(8,128)(2,1)} custom-call(bf16[1024,128]{1,0:T(8,128)(2,1)S(1)} %get-tuple-element.51.total.refs_0_, bf16[1024,128]{1,0:T(8,128)(2,1)S(1)} %collective-permute-done.19.rest_2_.refs_1_, bf16[1024,128]{1,0:T(8,128)(2,1)S(1)} %collective-permute-done.18.rest_1_.refs_2_, ...), custom_call_target="tpu_custom_call" | custom-call | tf_op jit(solution)/shard_map/projection/pallas_call | solution.py:525
  100.6 8.2 %all-to-all-start = ((bf16[32,80,128]{2,1,0:T(8,128)(2,1)}), bf16[32,80,128]{2,1,0:T(8,128)(2,1)S(1)}, u32[]{:S(2)}, u32[]{:S(2)}) async-start(bf16[32,80,128]{2,1,0:T(8,128)(2,1)} %projection.1), calls=%async_computation | async-start | bytes 1310720 | tf_op jit(solution)/shard_map/projection_sum/all_to_all | solution.py:556
  108.7 1.9 %own_gradients.3 = (bf16[128,4096]{1,0:T(8,128)(2,1)}, bf16[128,512]{1,0:T(8,128)(2,1)}, bf16[128,512]{1,0:T(8,128)(2,1)}) custom-call(s32[2]{0:T(128)S(1)} %copy-done.3, bf16[2048,128]{1,0:T(8,128)(2,1)S(1)} %get-tuple-element.36.refs_6_.near, bf16[2560,128]{1,0:T(8,128)(2,1)S(1)} %collective-permute-done.16.side, ...), custom_call_target="tpu_custom_call" | custom-call | bytes 67108864 | tf_op jit(solution)/shard_map/own_gradients/pallas_call | solution.py:543
  110.7 10.8 %all-to-all-done.parts = bf16[32,80,128]{2,1,0:T(8,128)(2,1)S(1)} async-done(((bf16[32,80,128]{2,1,0:T(8,128)(2,1)}), bf16[32,80,128]{2,1,0:T(8,128)(2,1)S(1)}, u32[]{:S(2)}, u32[]{:S(2)}) %all-to-all-start) | async-done | bytes 655392 | tf_op jit(solution)/shard_map/projection_sum/all_to_all | solution.py:556
  (47 shorter events, 20.1 us)
Async XLA Ops:
  5.0 7.1 %collective-permute-start = (bf16[2336,128]{1,0:T(8,128)(2,1)}, bf16[2336,128]{1,0:T(8,128)(2,1)S(1)}, u32[]{:S(2)}, u32[]{:S(2)}) collective-permute-start(bf16[2336,128]{1,0:T(8,128)(2,1)} %get-tuple-element.31), channel_id=1, source_target_pairs={{0,1},{1,0},{2,3},{3,2},{4,5},{5,4},{6,7},{7,6},{8,9},{9,8},{10,11... | collective-permute-start | bytes 1794056 | tf_op jit(solution)/shard_map/near/ppermute | solution.py:465
  6.5 3.9 %collective-permute-start.1 = (bf16[256,128]{1,0:T(8,128)(2,1)}, bf16[256,128]{1,0:T(8,128)(2,1)S(1)}, u32[]{:S(2)}, u32[]{:S(2)}) collective-permute-start(bf16[256,128]{1,0:T(8,128)(2,1)} %get-tuple-element.32), channel_id=1, source_target_pairs={{0,2},{1,3},{2,0},{3,1},{4,6},{5,7},{6,4},{7,5},{8,10},{9,11},{10,... | collective-permute-start | bytes 196616 | tf_op jit(solution)/shard_map/near/ppermute | solution.py:465
  7.9 4.3 %collective-permute-start.2 = (bf16[256,128]{1,0:T(8,128)(2,1)}, bf16[256,128]{1,0:T(8,128)(2,1)S(1)}, u32[]{:S(2)}, u32[]{:S(2)}) collective-permute-start(bf16[256,128]{1,0:T(8,128)(2,1)} %get-tuple-element.33), channel_id=1, source_target_pairs={{0,3},{1,2},{2,1},{3,0},{4,7},{5,6},{6,5},{7,4},{8,11},{9,10},{10,... | collective-permute-start | bytes 196616 | tf_op jit(solution)/shard_map/near/ppermute | solution.py:465
  13.6 10.6 %collective-permute-start.5 = (bf16[1024,128]{1,0:T(8,128)(2,1)S(1)}, bf16[1024,128]{1,0:T(8,128)(2,1)S(1)}, u32[]{:S(2)}, u32[]{:S(2)}) collective-permute-start(bf16[1024,128]{1,0:T(8,128)(2,1)S(1)} %get-tuple-element.34.refs_0_), channel_id=1, source_target_pairs={{0,8},{1,9},{2,10},{3,11},{4,12},{5,13},{6,14},{7,15},{8,0},{9,1},... | collective-permute-start | bytes 786440 | tf_op jit(solution)/shard_map/keys_values_ring/ppermute | solution.py:468
  16.4 12.0 %collective-permute-start.4 = (bf16[1024,128]{1,0:T(8,128)(2,1)S(1)}, bf16[1024,128]{1,0:T(8,128)(2,1)S(1)}, u32[]{:S(2)}, u32[]{:S(2)}) collective-permute-start(bf16[1024,128]{1,0:T(8,128)(2,1)S(1)} %get-tuple-element.34.refs_0_), channel_id=1, source_target_pairs={{0,12},{1,13},{2,14},{3,15},{4,0},{5,1},{6,2},{7,3},{8,4},{9,5},{1... | collective-permute-start | bytes 786440 | tf_op jit(solution)/shard_map/keys_values_ring/ppermute | solution.py:468
  17.2 11.7 %collective-permute-start.3 = (bf16[1024,128]{1,0:T(8,128)(2,1)S(1)}, bf16[1024,128]{1,0:T(8,128)(2,1)S(1)}, u32[]{:S(2)}, u32[]{:S(2)}) collective-permute-start(bf16[1024,128]{1,0:T(8,128)(2,1)S(1)} %get-tuple-element.34.refs_0_), channel_id=1, source_target_pairs={{0,4},{1,5},{2,6},{3,7},{4,8},{5,9},{6,10},{7,11},{8,12},{9,13},{1... | collective-permute-start | bytes 786440 | tf_op jit(solution)/shard_map/keys_values_ring/ppermute | solution.py:468
  17.9 11.1 %copy-start.3 = (s32[2]{0:T(128)S(1)}, s32[2]{0:T(128)}, u32[]{:S(2)}) copy-start(s32[2]{0:T(128)} %pad_add_fusion.place) | copy-start | bytes 28
  21.4 19.3 %collective-permute-start.6 = (bf16[2080,128]{1,0:T(8,128)(2,1)}, bf16[2080,128]{1,0:T(8,128)(2,1)S(1)}, u32[]{:S(2)}, u32[]{:S(2)}) collective-permute-start(bf16[2080,128]{1,0:T(8,128)(2,1)} %get-tuple-element.38), channel_id=1, source_target_pairs={{0,2},{1,3},{2,0},{3,1},{4,6},{5,7},{6,4},{7,5},{8,10},{9,11},{10,... | collective-permute-start | bytes 1597448 | tf_op jit(solution)/shard_map/queries_far/ppermute | solution.py:465
  22.6 24.6 %collective-permute-start.7 = (bf16[2080,128]{1,0:T(8,128)(2,1)}, bf16[2080,128]{1,0:T(8,128)(2,1)S(1)}, u32[]{:S(2)}, u32[]{:S(2)}) collective-permute-start(bf16[2080,128]{1,0:T(8,128)(2,1)} %get-tuple-element.39), channel_id=1, source_target_pairs={{0,3},{1,2},{2,1},{3,0},{4,7},{5,6},{6,5},{7,4},{8,11},{9,10},{10,... | collective-permute-start | bytes 1597448 | tf_op jit(solution)/shard_map/queries_far/ppermute | solution.py:465
  30.1 17.1 %collective-permute-start.8 = (bf16[128,1280]{1,0:T(8,128)(2,1)S(1)}, bf16[128,1280]{1,0:T(8,128)(2,1)S(1)}, u32[]{:S(2)}, u32[]{:S(2)}) collective-permute-start(bf16[128,1280]{1,0:T(8,128)(2,1)S(1)} %get-tuple-element.42), channel_id=1, source_target_pairs={{0,8},{1,9},{2,10},{3,11},{4,12},{5,13},{6,14},{7,15},{8,0},{9,1},... | collective-permute-start | bytes 983048 | tf_op jit(solution)/shard_map/inputs_ring/ppermute | solution.py:468
  32.9 15.4 %collective-permute-start.9 = (bf16[128,1280]{1,0:T(8,128)(2,1)S(1)}, bf16[128,1280]{1,0:T(8,128)(2,1)S(1)}, u32[]{:S(2)}, u32[]{:S(2)}) collective-permute-start(bf16[128,1280]{1,0:T(8,128)(2,1)S(1)} %get-tuple-element.43), channel_id=1, source_target_pairs={{0,4},{1,5},{2,6},{3,7},{4,8},{5,9},{6,10},{7,11},{8,12},{9,13},{1... | collective-permute-start | bytes 983048 | tf_op jit(solution)/shard_map/inputs_ring/ppermute | solution.py:468
  33.3 15.1 %collective-permute-start.10 = (bf16[128,1280]{1,0:T(8,128)(2,1)S(1)}, bf16[128,1280]{1,0:T(8,128)(2,1)S(1)}, u32[]{:S(2)}, u32[]{:S(2)}) collective-permute-start(bf16[128,1280]{1,0:T(8,128)(2,1)S(1)} %get-tuple-element.44), channel_id=1, source_target_pairs={{0,12},{1,13},{2,14},{3,15},{4,0},{5,1},{6,2},{7,3},{8,4},{9,5},{1... | collective-permute-start | bytes 983048 | tf_op jit(solution)/shard_map/inputs_ring/ppermute | solution.py:468
  48.4 27.1 %collective-permute-start.15 = (bf16[512,1280]{1,0:T(8,128)(2,1)S(1)}, bf16[512,1280]{1,0:T(8,128)(2,1)S(1)}, u32[]{:S(2)}, u32[]{:S(2)}) collective-permute-start(bf16[512,1280]{1,0:T(8,128)(2,1)S(1)} %inputs_side.1.refs_7_.refs_4_), channel_id=1, source_target_pairs={{0,1},{1,0},{2,3},{3,2},{4,5},{5,4},{6,7},{7,6},{8,9},{9,8},{10,11... | collective-permute-start | bytes 3932168 | tf_op jit(solution)/shard_map/inputs_side/ppermute | solution.py:465
  49.2 30.1 %collective-permute-start.14 = (bf16[512,1280]{1,0:T(8,128)(2,1)S(1)}, bf16[512,1280]{1,0:T(8,128)(2,1)S(1)}, u32[]{:S(2)}, u32[]{:S(2)}) collective-permute-start(bf16[512,1280]{1,0:T(8,128)(2,1)S(1)} %inputs_side.1.refs_7_.refs_4_), channel_id=1, source_target_pairs={{0,2},{1,3},{2,0},{3,1},{4,6},{5,7},{6,4},{7,5},{8,10},{9,11},{10,... | collective-permute-start | bytes 3932168 | tf_op jit(solution)/shard_map/inputs_side/ppermute | solution.py:465
  57.7 10.8 %collective-permute-start.11 = (bf16[1024,128]{1,0:T(8,128)(2,1)S(1)}, bf16[1024,128]{1,0:T(8,128)(2,1)S(1)}, u32[]{:S(2)}, u32[]{:S(2)}) collective-permute-start(bf16[1024,128]{1,0:T(8,128)(2,1)S(1)} %get-tuple-element.46), channel_id=1, source_target_pairs={{0,8},{1,9},{2,10},{3,11},{4,12},{5,13},{6,14},{7,15},{8,0},{9,1},... | collective-permute-start | bytes 786440 | tf_op jit(solution)/shard_map/kv_gradients/ppermute | solution.py:468
  62.3 13.3 %collective-permute-start.12 = (bf16[1024,128]{1,0:T(8,128)(2,1)S(1)}, bf16[1024,128]{1,0:T(8,128)(2,1)S(1)}, u32[]{:S(2)}, u32[]{:S(2)}) collective-permute-start(bf16[1024,128]{1,0:T(8,128)(2,1)S(1)} %get-tuple-element.47), channel_id=1, source_target_pairs={{0,12},{1,13},{2,14},{3,15},{4,0},{5,1},{6,2},{7,3},{8,4},{9,5},{1... | collective-permute-start | bytes 786440 | tf_op jit(solution)/shard_map/kv_gradients/ppermute | solution.py:468
  63.5 12.0 %collective-permute-start.13 = (bf16[1024,128]{1,0:T(8,128)(2,1)S(1)}, bf16[1024,128]{1,0:T(8,128)(2,1)S(1)}, u32[]{:S(2)}, u32[]{:S(2)}) collective-permute-start(bf16[1024,128]{1,0:T(8,128)(2,1)S(1)} %get-tuple-element.48), channel_id=1, source_target_pairs={{0,4},{1,5},{2,6},{3,7},{4,8},{5,9},{6,10},{7,11},{8,12},{9,13},{1... | collective-permute-start | bytes 786440 | tf_op jit(solution)/shard_map/kv_gradients/ppermute | solution.py:468
  79.6 18.5 %collective-permute-start.21 = (bf16[512,1280]{1,0:T(8,128)(2,1)S(1)}, bf16[512,1280]{1,0:T(8,128)(2,1)S(1)}, u32[]{:S(2)}, u32[]{:S(2)}) collective-permute-start(bf16[512,1280]{1,0:T(8,128)(2,1)S(1)} %get-tuple-element.55.refs_6_), channel_id=1, source_target_pairs={{0,1},{1,0},{2,3},{3,2},{4,5},{5,4},{6,7},{7,6},{8,9},{9,8},{10,11... | collective-permute-start | bytes 3932168 | tf_op jit(solution)/shard_map/kv_gradients/ppermute | solution.py:465
  80.7 16.5 %collective-permute-start.16 = (bf16[2560,128]{1,0:T(8,128)(2,1)S(1)}, bf16[2560,128]{1,0:T(8,128)(2,1)S(1)}, u32[]{:S(2)}, u32[]{:S(2)}) collective-permute-start(bf16[2560,128]{1,0:T(8,128)(2,1)S(1)} %get-tuple-element.50), channel_id=1, source_target_pairs={{0,2},{1,3},{2,0},{3,1},{4,6},{5,7},{6,4},{7,5},{8,10},{9,11},{10,... | collective-permute-start | bytes 1966088 | tf_op jit(solution)/shard_map/own_gradients/ppermute | solution.py:465
  81.9 9.1 %collective-permute-start.19 = (bf16[1024,128]{1,0:T(8,128)(2,1)S(1)}, bf16[1024,128]{1,0:T(8,128)(2,1)S(1)}, u32[]{:S(2)}, u32[]{:S(2)}) collective-permute-start(bf16[1024,128]{1,0:T(8,128)(2,1)S(1)} %get-tuple-element.51.total.refs_0_), channel_id=1, source_target_pairs={{0,8},{1,9},{2,10},{3,11},{4,12},{5,13},{6,14},{7,15},{8,0},{9,1},... | collective-permute-start | bytes 786440 | tf_op jit(solution)/shard_map/kv_gradients/ppermute | solution.py:468
  83.7 13.6 %collective-permute-start.18 = (bf16[1024,128]{1,0:T(8,128)(2,1)S(1)}, bf16[1024,128]{1,0:T(8,128)(2,1)S(1)}, u32[]{:S(2)}, u32[]{:S(2)}) collective-permute-start(bf16[1024,128]{1,0:T(8,128)(2,1)S(1)} %get-tuple-element.51.total.refs_0_), channel_id=1, source_target_pairs={{0,4},{1,5},{2,6},{3,7},{4,8},{5,9},{6,10},{7,11},{8,12},{9,13},{1... | collective-permute-start | bytes 786440 | tf_op jit(solution)/shard_map/kv_gradients/ppermute | solution.py:468
  84.8 12.4 %collective-permute-start.17 = (bf16[1024,128]{1,0:T(8,128)(2,1)S(1)}, bf16[1024,128]{1,0:T(8,128)(2,1)S(1)}, u32[]{:S(2)}, u32[]{:S(2)}) collective-permute-start(bf16[1024,128]{1,0:T(8,128)(2,1)S(1)} %get-tuple-element.51.total.refs_0_), channel_id=1, source_target_pairs={{0,12},{1,13},{2,14},{3,15},{4,0},{5,1},{6,2},{7,3},{8,4},{9,5},{1... | collective-permute-start | bytes 786440 | tf_op jit(solution)/shard_map/kv_gradients/ppermute | solution.py:468
  97.3 11.4 %collective-permute-start.20 = (bf16[2560,128]{1,0:T(8,128)(2,1)S(1)}, bf16[2560,128]{1,0:T(8,128)(2,1)S(1)}, u32[]{:S(2)}, u32[]{:S(2)}) collective-permute-start(bf16[2560,128]{1,0:T(8,128)(2,1)S(1)} %own_gradients.2), channel_id=1, source_target_pairs={{0,1},{1,0},{2,3},{3,2},{4,5},{5,4},{6,7},{7,6},{8,9},{9,8},{10,11... | collective-permute-start | bytes 1966088 | tf_op jit(solution)/shard_map/own_gradients/ppermute | solution.py:465
  100.6 20.9 %all-to-all-start = ((bf16[32,80,128]{2,1,0:T(8,128)(2,1)}), bf16[32,80,128]{2,1,0:T(8,128)(2,1)S(1)}, u32[]{:S(2)}, u32[]{:S(2)}) async-start(bf16[32,80,128]{2,1,0:T(8,128)(2,1)} %projection.1), calls=%async_computation | async-start | bytes 1310720 | tf_op jit(solution)/shard_map/projection_sum/all_to_all | solution.py:556
  (5 other events, 25.8 us)

commit v5 on v4

--- a/solution.py
+++ b/solution.py
@@ -487,7 +487,7 @@
         kv = [kv_own] + [kv[s] for s in (1, 2, 3)]
 
     with jax.named_scope("queries_far"):
-        far_own = split_queries(place, *query_args, 2, token)
+        far_own = split_queries(place, *query_args, 2, near_own[2])
         packs_far = [to_side(far_own[k - 2], k) for k in (2, 3)]
 
     with jax.named_scope("inputs_ring"):

time: 123 us -> 123 us (level)
    ppermute x10, waiting for transfers between devices: 14.1 us -> 17 us  [to_side(): return lax.ppermute(x, 'ctx', side_perm(k))]
    ppermute x12, waiting for transfers between devices: 28.4 us -> 26.3 us  [to_ring(): return lax.ppermute(x, 'ctx', ring_perm(s % RING))]
    all_to_all x1, starting transfers between devices: 8.15 us -> 9.79 us  [local(): lax.all_to_all(partial, ('dp', 'ctx'), 0, 0, axis_index_groups=groups, ti...]
where the time goes in v5:
time: 123 us
  waiting for transfers between devices  54.1 us (44%)
  starting transfers between devices  40.5 us (33%)
  Pallas kernels  26.6 us (22%)
    ppermute x12, waiting for transfers between devices, to_ring(): return lax.ppermute(x, 'ctx', ring_perm(s % RING))  26.3 us
    ppermute x12, starting transfers between devices, to_ring(): return lax.ppermute(x, 'ctx', ring_perm(s % RING))  19.7 us
    ppermute x10, waiting for transfers between devices, to_side(): return lax.ppermute(x, 'ctx', side_perm(k))  17 us
    pallas_call x2, Pallas kernels, attention_call(): pl.pallas_call(functools.partial(attention_kernel, first), out_shape=out_...  12.4 us
    ppermute x10, starting transfers between devices, to_side(): return lax.ppermute(x, 'ctx', side_perm(k))  11 us
    all_to_all x1, waiting for transfers between devices, local(): lax.all_to_all(partial, ('dp', 'ctx'), 0, 0, axis_index_groups=groups, ti...  10.8 us
    all_to_all x1, starting transfers between devices, local(): lax.all_to_all(partial, ('dp', 'ctx'), 0, 0, axis_index_groups=groups, ti...  9.79 us
    pallas_call x2, Pallas kernels, split_queries(): pl.pallas_call(functools.partial(split_queries_kernel, near), out_shape=[...  7.36 us
  transfers between devices with their start and end apart: 23, of which 12 were waited for; matrix products, arithmetic and copies ran while one was open for 0% of the time, Pallas kernels for 18%

profile of v5, /device:TPU:1, one launch (start us, length us, event | category | flops | bytes accessed | tf_op | source)
XLA Modules:
  0.0 123.4 jit_solution(9578634045084866495)
XLA Ops:
  1.3 3.8 %near.1 = (bf16[2336,128]{1,0:T(8,128)(2,1)}, bf16[2336,128]{1,0:T(8,128)(2,1)}, f32[8,128]{1,0:T(8,128)}, bf16[256,128]{1,0:T(8,128)(2,1)}, bf16[256,128]{1,0:T(8,128)(2,1)}, /*index=5*/bf16[256,128]{1,0:T(8,128)(2,1)}) custom-call(s32[2]{0:T(128)} %pad_add_fusion.place, bf16[128,4096]{1,0:T(8,128)(2,1)} %bitcast.13, bf16[128,4096]{1,0:T(8,128)(2,1)} %bitcast.15, ...), custom_call_target="tpu_custom_call" | custom-call | bytes 33554432 | tf_op jit(solution)/shard_map/near/pallas_call | solution.py:110
  8.2 2.1 %collective-permute-done.1.refs_2_ = bf16[256,128]{1,0:T(8,128)(2,1)S(1)} collective-permute-done((bf16[256,128]{1,0:T(8,128)(2,1)}, bf16[256,128]{1,0:T(8,128)(2,1)S(1)}, u32[]{:S(2)}, u32[]{:S(2)}) %collective-permute-start.1) | collective-permute-done | bytes 65568 | tf_op jit(solution)/shard_map/near/ppermute | solution.py:465
  10.4 1.8 %collective-permute-done.2.refs_3_ = bf16[256,128]{1,0:T(8,128)(2,1)S(1)} collective-permute-done((bf16[256,128]{1,0:T(8,128)(2,1)}, bf16[256,128]{1,0:T(8,128)(2,1)S(1)}, u32[]{:S(2)}, u32[]{:S(2)}) %collective-permute-start.2) | collective-permute-done | bytes 65568 | tf_op jit(solution)/shard_map/near/ppermute | solution.py:465
  13.0 2.8 %collective-permute-start.5 = (bf16[1024,128]{1,0:T(8,128)(2,1)S(1)}, bf16[1024,128]{1,0:T(8,128)(2,1)S(1)}, u32[]{:S(2)}, u32[]{:S(2)}) collective-permute-start(bf16[1024,128]{1,0:T(8,128)(2,1)S(1)} %get-tuple-element.34.refs_0_), channel_id=1, source_target_pairs={{0,8},{1,9},{2,10},{3,11},{4,12},{5,13},{6,14},{7,15},{8,0},{9,1},... | collective-permute-start | bytes 786440 | tf_op jit(solution)/shard_map/keys_values_ring/ppermute | solution.py:468
  17.3 3.6 %queries_far.1 = (bf16[2080,128]{1,0:T(8,128)(2,1)}, bf16[2080,128]{1,0:T(8,128)(2,1)}, f32[8,128]{1,0:T(8,128)}) custom-call(s32[2]{0:T(128)} %pad_add_fusion.place, bf16[128,4096]{1,0:T(8,128)(2,1)} %bitcast.14, bf16[128,4096]{1,0:T(8,128)(2,1)} %bitcast.16, bf16[128,4096]{1,0:T(8,128)(2,1)} %bitcast.18, f32[32,128]{1,0:T(8,128)} %bitcast.22, ...), custom_call_target="tpu_custom_call" | custom-call | bytes 33554432 | tf_op jit(solution)/shard_map/queries_far/pallas_call | solution.py:110
  22.1 1.7 %collective-permute-start.7 = (bf16[2080,128]{1,0:T(8,128)(2,1)}, bf16[2080,128]{1,0:T(8,128)(2,1)S(1)}, u32[]{:S(2)}, u32[]{:S(2)}) collective-permute-start(bf16[2080,128]{1,0:T(8,128)(2,1)} %get-tuple-element.39), channel_id=1, source_target_pairs={{0,3},{1,2},{2,1},{3,0},{4,7},{5,6},{6,5},{7,4},{8,11},{9,10},{10,... | collective-permute-start | bytes 1597448 | tf_op jit(solution)/shard_map/queries_far/ppermute | solution.py:465
  23.8 4.2 %collective-permute-done.4.refs_2_.refs_1_ = bf16[1024,128]{1,0:T(8,128)(2,1)S(1)} collective-permute-done((bf16[1024,128]{1,0:T(8,128)(2,1)S(1)}, bf16[1024,128]{1,0:T(8,128)(2,1)S(1)}, u32[]{:S(2)}, u32[]{:S(2)}) %collective-permute-start.4) | collective-permute-done | bytes 262176 | tf_op jit(solution)/shard_map/keys_values_ring/ppermute | solution.py:468
  29.6 2.8 %collective-permute-start.8 = (bf16[128,1280]{1,0:T(8,128)(2,1)S(1)}, bf16[128,1280]{1,0:T(8,128)(2,1)S(1)}, u32[]{:S(2)}, u32[]{:S(2)}) collective-permute-start(bf16[128,1280]{1,0:T(8,128)(2,1)S(1)} %get-tuple-element.42), channel_id=1, source_target_pairs={{0,8},{1,9},{2,10},{3,11},{4,12},{5,13},{6,14},{7,15},{8,0},{9,1},... | collective-permute-start | bytes 983048 | tf_op jit(solution)/shard_map/inputs_ring/ppermute | solution.py:468
  32.8 2.3 %collective-permute-start.10 = (bf16[128,1280]{1,0:T(8,128)(2,1)S(1)}, bf16[128,1280]{1,0:T(8,128)(2,1)S(1)}, u32[]{:S(2)}, u32[]{:S(2)}) collective-permute-start(bf16[128,1280]{1,0:T(8,128)(2,1)S(1)} %get-tuple-element.44), channel_id=1, source_target_pairs={{0,12},{1,13},{2,14},{3,15},{4,0},{5,1},{6,2},{7,3},{8,4},{9,5},{1... | collective-permute-start | bytes 983048 | tf_op jit(solution)/shard_map/inputs_ring/ppermute | solution.py:468
  35.1 5.0 %attention_near.1 = (bf16[2048,128]{1,0:T(8,128)(2,1)S(1)}, f32[16,256,128]{2,1,0:T(8,128)S(1)}) custom-call(s32[2]{0:T(128)S(1)} %copy-done.3, s32[1,16]{1,0:T(1,128)S(1)} %copy-done.4, bf16[1024,128]{1,0:T(8,128)(2,1)S(1)} %get-tuple-element.34.refs_0_, bf16[1024,128]{1,0:T(8,128)(2,1)S(1)} %collective-permute-done.3.refs_1_.refs_0_, ...), custom_call_target="tpu_custom_call" | custom-call | tf_op jit(solution)/shard_map/attention_near/pallas_call | solution.py:328
  40.2 6.5 %collective-permute-done.7.refs_5_ = bf16[2080,128]{1,0:T(8,128)(2,1)S(1)} collective-permute-done((bf16[2080,128]{1,0:T(8,128)(2,1)}, bf16[2080,128]{1,0:T(8,128)(2,1)S(1)}, u32[]{:S(2)}, u32[]{:S(2)}) %collective-permute-start.7) | collective-permute-done | bytes 532512 | tf_op jit(solution)/shard_map/queries_far/ppermute | solution.py:465
  49.8 7.4 %attention_far.1 = (bf16[2560,128]{1,0:T(8,128)(2,1)S(1)}, f32[1024,128]{1,0:T(8,128)S(1)}, bf16[1024,128]{1,0:T(8,128)(2,1)S(1)}, bf16[1024,128]{1,0:T(8,128)(2,1)S(1)}, bf16[1024,128]{1,0:T(8,128)(2,1)S(1)}) custom-call(s32[2]{0:T(128)S(1)} %copy-done.3, s32[1,16]{1,0:T(1,128)S(1)} %copy-done.4, bf16[1024,128]{1,0:T(8,128)(2,1)S(1)} %get-tuple-element.34.refs_0_, ...), custom_call_target="tpu_custom_call" | custom-call | tf_op jit(solution)/shard_map/attention_far/pallas_call | solution.py:328
  57.2 2.4 %collective-permute-start.11 = (bf16[1024,128]{1,0:T(8,128)(2,1)S(1)}, bf16[1024,128]{1,0:T(8,128)(2,1)S(1)}, u32[]{:S(2)}, u32[]{:S(2)}) collective-permute-start(bf16[1024,128]{1,0:T(8,128)(2,1)S(1)} %get-tuple-element.46), channel_id=1, source_target_pairs={{0,8},{1,9},{2,10},{3,11},{4,12},{5,13},{6,14},{7,15},{8,0},{9,1},... | collective-permute-start | bytes 786440 | tf_op jit(solution)/shard_map/kv_gradients/ppermute | solution.py:468
  59.6 3.1 %collective-permute-start.12 = (bf16[1024,128]{1,0:T(8,128)(2,1)S(1)}, bf16[1024,128]{1,0:T(8,128)(2,1)S(1)}, u32[]{:S(2)}, u32[]{:S(2)}) collective-permute-start(bf16[1024,128]{1,0:T(8,128)(2,1)S(1)} %get-tuple-element.47), channel_id=1, source_target_pairs={{0,12},{1,13},{2,14},{3,15},{4,0},{5,1},{6,2},{7,3},{8,4},{9,5},{1... | collective-permute-start | bytes 786440 | tf_op jit(solution)/shard_map/kv_gradients/ppermute | solution.py:468
  62.7 3.4 %collective-permute-done.11.refs_0_ = bf16[1024,128]{1,0:T(8,128)(2,1)S(1)} collective-permute-done((bf16[1024,128]{1,0:T(8,128)(2,1)S(1)}, bf16[1024,128]{1,0:T(8,128)(2,1)S(1)}, u32[]{:S(2)}, u32[]{:S(2)}) %collective-permute-start.11) | collective-permute-done | bytes 262176 | tf_op jit(solution)/shard_map/kv_gradients/ppermute | solution.py:468
  66.1 6.1 %collective-permute-done.12.refs_1_ = bf16[1024,128]{1,0:T(8,128)(2,1)S(1)} collective-permute-done((bf16[1024,128]{1,0:T(8,128)(2,1)S(1)}, bf16[1024,128]{1,0:T(8,128)(2,1)S(1)}, u32[]{:S(2)}, u32[]{:S(2)}) %collective-permute-start.12) | collective-permute-done | bytes 262176 | tf_op jit(solution)/shard_map/kv_gradients/ppermute | solution.py:468
  72.2 6.5 %collective-permute-done.14.refs_3_ = bf16[512,1280]{1,0:T(8,128)(2,1)S(1)} collective-permute-done((bf16[512,1280]{1,0:T(8,128)(2,1)S(1)}, bf16[512,1280]{1,0:T(8,128)(2,1)S(1)}, u32[]{:S(2)}, u32[]{:S(2)}) %collective-permute-start.14) | collective-permute-done | bytes 1310752 | tf_op jit(solution)/shard_map/inputs_side/ppermute | solution.py:465
  81.4 1.8 %collective-permute-start.19 = (bf16[1024,128]{1,0:T(8,128)(2,1)S(1)}, bf16[1024,128]{1,0:T(8,128)(2,1)S(1)}, u32[]{:S(2)}, u32[]{:S(2)}) collective-permute-start(bf16[1024,128]{1,0:T(8,128)(2,1)S(1)} %get-tuple-element.51.total.refs_0_), channel_id=1, source_target_pairs={{0,8},{1,9},{2,10},{3,11},{4,12},{5,13},{6,14},{7,15},{8,0},{9,1},... | collective-permute-start | bytes 786440 | tf_op jit(solution)/shard_map/kv_gradients/ppermute | solution.py:468
  85.8 4.6 %collective-permute-done.19.rest_2_.refs_1_ = bf16[1024,128]{1,0:T(8,128)(2,1)S(1)} collective-permute-done((bf16[1024,128]{1,0:T(8,128)(2,1)S(1)}, bf16[1024,128]{1,0:T(8,128)(2,1)S(1)}, u32[]{:S(2)}, u32[]{:S(2)}) %collective-permute-start.19) | collective-permute-done | bytes 262176 | tf_op jit(solution)/shard_map/kv_gradients/ppermute | solution.py:468
  90.5 6.3 %collective-permute-done.18.rest_1_.refs_2_ = bf16[1024,128]{1,0:T(8,128)(2,1)S(1)} collective-permute-done((bf16[1024,128]{1,0:T(8,128)(2,1)S(1)}, bf16[1024,128]{1,0:T(8,128)(2,1)S(1)}, u32[]{:S(2)}, u32[]{:S(2)}) %collective-permute-start.18) | collective-permute-done | bytes 262176 | tf_op jit(solution)/shard_map/kv_gradients/ppermute | solution.py:468
  97.5 2.5 %projection.1 = bf16[32,80,128]{2,1,0:T(8,128)(2,1)} custom-call(bf16[1024,128]{1,0:T(8,128)(2,1)S(1)} %get-tuple-element.51.total.refs_0_, bf16[1024,128]{1,0:T(8,128)(2,1)S(1)} %collective-permute-done.19.rest_2_.refs_1_, bf16[1024,128]{1,0:T(8,128)(2,1)S(1)} %collective-permute-done.18.rest_1_.refs_2_, ...), custom_call_target="tpu_custom_call" | custom-call | tf_op jit(solution)/shard_map/projection/pallas_call | solution.py:525
  100.0 9.8 %all-to-all-start = ((bf16[32,80,128]{2,1,0:T(8,128)(2,1)}), bf16[32,80,128]{2,1,0:T(8,128)(2,1)S(1)}, u32[]{:S(2)}, u32[]{:S(2)}) async-start(bf16[32,80,128]{2,1,0:T(8,128)(2,1)} %projection.1), calls=%async_computation | async-start | bytes 1310720 | tf_op jit(solution)/shard_map/projection_sum/all_to_all | solution.py:556
  109.9 1.9 %own_gradients.3 = (bf16[128,4096]{1,0:T(8,128)(2,1)}, bf16[128,512]{1,0:T(8,128)(2,1)}, bf16[128,512]{1,0:T(8,128)(2,1)}) custom-call(s32[2]{0:T(128)S(1)} %copy-done.3, bf16[2048,128]{1,0:T(8,128)(2,1)S(1)} %get-tuple-element.36.refs_6_.near, bf16[2560,128]{1,0:T(8,128)(2,1)S(1)} %collective-permute-done.16.side, ...), custom_call_target="tpu_custom_call" | custom-call | bytes 67108864 | tf_op jit(solution)/shard_map/own_gradients/pallas_call | solution.py:543
  111.8 10.8 %all-to-all-done.parts = bf16[32,80,128]{2,1,0:T(8,128)(2,1)S(1)} async-done(((bf16[32,80,128]{2,1,0:T(8,128)(2,1)}), bf16[32,80,128]{2,1,0:T(8,128)(2,1)S(1)}, u32[]{:S(2)}, u32[]{:S(2)}) %all-to-all-start) | async-done | bytes 655392 | tf_op jit(solution)/shard_map/projection_sum/all_to_all | solution.py:556
  (45 shorter events, 19.3 us)
Async XLA Ops:
  5.0 7.1 %collective-permute-start = (bf16[2336,128]{1,0:T(8,128)(2,1)}, bf16[2336,128]{1,0:T(8,128)(2,1)S(1)}, u32[]{:S(2)}, u32[]{:S(2)}) collective-permute-start(bf16[2336,128]{1,0:T(8,128)(2,1)} %get-tuple-element.31), channel_id=1, source_target_pairs={{0,1},{1,0},{2,3},{3,2},{4,5},{5,4},{6,7},{7,6},{8,9},{9,8},{10,11... | collective-permute-start | bytes 1794056 | tf_op jit(solution)/shard_map/near/ppermute | solution.py:465
  6.5 3.9 %collective-permute-start.1 = (bf16[256,128]{1,0:T(8,128)(2,1)}, bf16[256,128]{1,0:T(8,128)(2,1)S(1)}, u32[]{:S(2)}, u32[]{:S(2)}) collective-permute-start(bf16[256,128]{1,0:T(8,128)(2,1)} %get-tuple-element.32), channel_id=1, source_target_pairs={{0,2},{1,3},{2,0},{3,1},{4,6},{5,7},{6,4},{7,5},{8,10},{9,11},{10,... | collective-permute-start | bytes 196616 | tf_op jit(solution)/shard_map/near/ppermute | solution.py:465
  7.9 4.3 %collective-permute-start.2 = (bf16[256,128]{1,0:T(8,128)(2,1)}, bf16[256,128]{1,0:T(8,128)(2,1)S(1)}, u32[]{:S(2)}, u32[]{:S(2)}) collective-permute-start(bf16[256,128]{1,0:T(8,128)(2,1)} %get-tuple-element.33), channel_id=1, source_target_pairs={{0,3},{1,2},{2,1},{3,0},{4,7},{5,6},{6,5},{7,4},{8,11},{9,10},{10,... | collective-permute-start | bytes 196616 | tf_op jit(solution)/shard_map/near/ppermute | solution.py:465
  13.0 10.7 %collective-permute-start.5 = (bf16[1024,128]{1,0:T(8,128)(2,1)S(1)}, bf16[1024,128]{1,0:T(8,128)(2,1)S(1)}, u32[]{:S(2)}, u32[]{:S(2)}) collective-permute-start(bf16[1024,128]{1,0:T(8,128)(2,1)S(1)} %get-tuple-element.34.refs_0_), channel_id=1, source_target_pairs={{0,8},{1,9},{2,10},{3,11},{4,12},{5,13},{6,14},{7,15},{8,0},{9,1},... | collective-permute-start | bytes 786440 | tf_op jit(solution)/shard_map/keys_values_ring/ppermute | solution.py:468
  15.9 12.0 %collective-permute-start.4 = (bf16[1024,128]{1,0:T(8,128)(2,1)S(1)}, bf16[1024,128]{1,0:T(8,128)(2,1)S(1)}, u32[]{:S(2)}, u32[]{:S(2)}) collective-permute-start(bf16[1024,128]{1,0:T(8,128)(2,1)S(1)} %get-tuple-element.34.refs_0_), channel_id=1, source_target_pairs={{0,12},{1,13},{2,14},{3,15},{4,0},{5,1},{6,2},{7,3},{8,4},{9,5},{1... | collective-permute-start | bytes 786440 | tf_op jit(solution)/shard_map/keys_values_ring/ppermute | solution.py:468
  16.7 11.7 %collective-permute-start.3 = (bf16[1024,128]{1,0:T(8,128)(2,1)S(1)}, bf16[1024,128]{1,0:T(8,128)(2,1)S(1)}, u32[]{:S(2)}, u32[]{:S(2)}) collective-permute-start(bf16[1024,128]{1,0:T(8,128)(2,1)S(1)} %get-tuple-element.34.refs_0_), channel_id=1, source_target_pairs={{0,4},{1,5},{2,6},{3,7},{4,8},{5,9},{6,10},{7,11},{8,12},{9,13},{1... | collective-permute-start | bytes 786440 | tf_op jit(solution)/shard_map/keys_values_ring/ppermute | solution.py:468
  17.3 11.1 %copy-start.3 = (s32[2]{0:T(128)S(1)}, s32[2]{0:T(128)}, u32[]{:S(2)}) copy-start(s32[2]{0:T(128)} %pad_add_fusion.place) | copy-start | bytes 28
  20.9 19.2 %collective-permute-start.6 = (bf16[2080,128]{1,0:T(8,128)(2,1)}, bf16[2080,128]{1,0:T(8,128)(2,1)S(1)}, u32[]{:S(2)}, u32[]{:S(2)}) collective-permute-start(bf16[2080,128]{1,0:T(8,128)(2,1)} %get-tuple-element.38), channel_id=1, source_target_pairs={{0,2},{1,3},{2,0},{3,1},{4,6},{5,7},{6,4},{7,5},{8,10},{9,11},{10,... | collective-permute-start | bytes 1597448 | tf_op jit(solution)/shard_map/queries_far/ppermute | solution.py:465
  22.1 24.6 %collective-permute-start.7 = (bf16[2080,128]{1,0:T(8,128)(2,1)}, bf16[2080,128]{1,0:T(8,128)(2,1)S(1)}, u32[]{:S(2)}, u32[]{:S(2)}) collective-permute-start(bf16[2080,128]{1,0:T(8,128)(2,1)} %get-tuple-element.39), channel_id=1, source_target_pairs={{0,3},{1,2},{2,1},{3,0},{4,7},{5,6},{6,5},{7,4},{8,11},{9,10},{10,... | collective-permute-start | bytes 1597448 | tf_op jit(solution)/shard_map/queries_far/ppermute | solution.py:465
  29.6 17.1 %collective-permute-start.8 = (bf16[128,1280]{1,0:T(8,128)(2,1)S(1)}, bf16[128,1280]{1,0:T(8,128)(2,1)S(1)}, u32[]{:S(2)}, u32[]{:S(2)}) collective-permute-start(bf16[128,1280]{1,0:T(8,128)(2,1)S(1)} %get-tuple-element.42), channel_id=1, source_target_pairs={{0,8},{1,9},{2,10},{3,11},{4,12},{5,13},{6,14},{7,15},{8,0},{9,1},... | collective-permute-start | bytes 983048 | tf_op jit(solution)/shard_map/inputs_ring/ppermute | solution.py:468
  32.4 15.4 %collective-permute-start.9 = (bf16[128,1280]{1,0:T(8,128)(2,1)S(1)}, bf16[128,1280]{1,0:T(8,128)(2,1)S(1)}, u32[]{:S(2)}, u32[]{:S(2)}) collective-permute-start(bf16[128,1280]{1,0:T(8,128)(2,1)S(1)} %get-tuple-element.43), channel_id=1, source_target_pairs={{0,4},{1,5},{2,6},{3,7},{4,8},{5,9},{6,10},{7,11},{8,12},{9,13},{1... | collective-permute-start | bytes 983048 | tf_op jit(solution)/shard_map/inputs_ring/ppermute | solution.py:468
  32.8 15.1 %collective-permute-start.10 = (bf16[128,1280]{1,0:T(8,128)(2,1)S(1)}, bf16[128,1280]{1,0:T(8,128)(2,1)S(1)}, u32[]{:S(2)}, u32[]{:S(2)}) collective-permute-start(bf16[128,1280]{1,0:T(8,128)(2,1)S(1)} %get-tuple-element.44), channel_id=1, source_target_pairs={{0,12},{1,13},{2,14},{3,15},{4,0},{5,1},{6,2},{7,3},{8,4},{9,5},{1... | collective-permute-start | bytes 983048 | tf_op jit(solution)/shard_map/inputs_ring/ppermute | solution.py:468
  47.9 24.3 %collective-permute-start.15 = (bf16[512,1280]{1,0:T(8,128)(2,1)S(1)}, bf16[512,1280]{1,0:T(8,128)(2,1)S(1)}, u32[]{:S(2)}, u32[]{:S(2)}) collective-permute-start(bf16[512,1280]{1,0:T(8,128)(2,1)S(1)} %inputs_side.1.refs_7_.refs_4_), channel_id=1, source_target_pairs={{0,1},{1,0},{2,3},{3,2},{4,5},{5,4},{6,7},{7,6},{8,9},{9,8},{10,11... | collective-permute-start | bytes 3932168 | tf_op jit(solution)/shard_map/inputs_side/ppermute | solution.py:465
  48.6 30.1 %collective-permute-start.14 = (bf16[512,1280]{1,0:T(8,128)(2,1)S(1)}, bf16[512,1280]{1,0:T(8,128)(2,1)S(1)}, u32[]{:S(2)}, u32[]{:S(2)}) collective-permute-start(bf16[512,1280]{1,0:T(8,128)(2,1)S(1)} %inputs_side.1.refs_7_.refs_4_), channel_id=1, source_target_pairs={{0,2},{1,3},{2,0},{3,1},{4,6},{5,7},{6,4},{7,5},{8,10},{9,11},{10,... | collective-permute-start | bytes 3932168 | tf_op jit(solution)/shard_map/inputs_side/ppermute | solution.py:465
  57.2 8.9 %collective-permute-start.11 = (bf16[1024,128]{1,0:T(8,128)(2,1)S(1)}, bf16[1024,128]{1,0:T(8,128)(2,1)S(1)}, u32[]{:S(2)}, u32[]{:S(2)}) collective-permute-start(bf16[1024,128]{1,0:T(8,128)(2,1)S(1)} %get-tuple-element.46), channel_id=1, source_target_pairs={{0,8},{1,9},{2,10},{3,11},{4,12},{5,13},{6,14},{7,15},{8,0},{9,1},... | collective-permute-start | bytes 786440 | tf_op jit(solution)/shard_map/kv_gradients/ppermute | solution.py:468
  59.6 12.6 %collective-permute-start.12 = (bf16[1024,128]{1,0:T(8,128)(2,1)S(1)}, bf16[1024,128]{1,0:T(8,128)(2,1)S(1)}, u32[]{:S(2)}, u32[]{:S(2)}) collective-permute-start(bf16[1024,128]{1,0:T(8,128)(2,1)S(1)} %get-tuple-element.47), channel_id=1, source_target_pairs={{0,12},{1,13},{2,14},{3,15},{4,0},{5,1},{6,2},{7,3},{8,4},{9,5},{1... | collective-permute-start | bytes 786440 | tf_op jit(solution)/shard_map/kv_gradients/ppermute | solution.py:468
  62.7 9.5 %collective-permute-start.13 = (bf16[1024,128]{1,0:T(8,128)(2,1)S(1)}, bf16[1024,128]{1,0:T(8,128)(2,1)S(1)}, u32[]{:S(2)}, u32[]{:S(2)}) collective-permute-start(bf16[1024,128]{1,0:T(8,128)(2,1)S(1)} %get-tuple-element.48), channel_id=1, source_target_pairs={{0,4},{1,5},{2,6},{3,7},{4,8},{5,9},{6,10},{7,11},{8,12},{9,13},{1... | collective-permute-start | bytes 786440 | tf_op jit(solution)/shard_map/kv_gradients/ppermute | solution.py:468
  79.0 18.5 %collective-permute-start.21 = (bf16[512,1280]{1,0:T(8,128)(2,1)S(1)}, bf16[512,1280]{1,0:T(8,128)(2,1)S(1)}, u32[]{:S(2)}, u32[]{:S(2)}) collective-permute-start(bf16[512,1280]{1,0:T(8,128)(2,1)S(1)} %get-tuple-element.55.refs_6_), channel_id=1, source_target_pairs={{0,1},{1,0},{2,3},{3,2},{4,5},{5,4},{6,7},{7,6},{8,9},{9,8},{10,11... | collective-permute-start | bytes 3932168 | tf_op jit(solution)/shard_map/kv_gradients/ppermute | solution.py:465
  80.2 16.5 %collective-permute-start.16 = (bf16[2560,128]{1,0:T(8,128)(2,1)S(1)}, bf16[2560,128]{1,0:T(8,128)(2,1)S(1)}, u32[]{:S(2)}, u32[]{:S(2)}) collective-permute-start(bf16[2560,128]{1,0:T(8,128)(2,1)S(1)} %get-tuple-element.50), channel_id=1, source_target_pairs={{0,2},{1,3},{2,0},{3,1},{4,6},{5,7},{6,4},{7,5},{8,10},{9,11},{10,... | collective-permute-start | bytes 1966088 | tf_op jit(solution)/shard_map/own_gradients/ppermute | solution.py:465
  81.4 9.1 %collective-permute-start.19 = (bf16[1024,128]{1,0:T(8,128)(2,1)S(1)}, bf16[1024,128]{1,0:T(8,128)(2,1)S(1)}, u32[]{:S(2)}, u32[]{:S(2)}) collective-permute-start(bf16[1024,128]{1,0:T(8,128)(2,1)S(1)} %get-tuple-element.51.total.refs_0_), channel_id=1, source_target_pairs={{0,8},{1,9},{2,10},{3,11},{4,12},{5,13},{6,14},{7,15},{8,0},{9,1},... | collective-permute-start | bytes 786440 | tf_op jit(solution)/shard_map/kv_gradients/ppermute | solution.py:468
  83.2 13.6 %collective-permute-start.18 = (bf16[1024,128]{1,0:T(8,128)(2,1)S(1)}, bf16[1024,128]{1,0:T(8,128)(2,1)S(1)}, u32[]{:S(2)}, u32[]{:S(2)}) collective-permute-start(bf16[1024,128]{1,0:T(8,128)(2,1)S(1)} %get-tuple-element.51.total.refs_0_), channel_id=1, source_target_pairs={{0,4},{1,5},{2,6},{3,7},{4,8},{5,9},{6,10},{7,11},{8,12},{9,13},{1... | collective-permute-start | bytes 786440 | tf_op jit(solution)/shard_map/kv_gradients/ppermute | solution.py:468
  84.3 12.4 %collective-permute-start.17 = (bf16[1024,128]{1,0:T(8,128)(2,1)S(1)}, bf16[1024,128]{1,0:T(8,128)(2,1)S(1)}, u32[]{:S(2)}, u32[]{:S(2)}) collective-permute-start(bf16[1024,128]{1,0:T(8,128)(2,1)S(1)} %get-tuple-element.51.total.refs_0_), channel_id=1, source_target_pairs={{0,12},{1,13},{2,14},{3,15},{4,0},{5,1},{6,2},{7,3},{8,4},{9,5},{1... | collective-permute-start | bytes 786440 | tf_op jit(solution)/shard_map/kv_gradients/ppermute | solution.py:468
  96.8 13.0 %collective-permute-start.20 = (bf16[2560,128]{1,0:T(8,128)(2,1)S(1)}, bf16[2560,128]{1,0:T(8,128)(2,1)S(1)}, u32[]{:S(2)}, u32[]{:S(2)}) collective-permute-start(bf16[2560,128]{1,0:T(8,128)(2,1)S(1)} %own_gradients.2), channel_id=1, source_target_pairs={{0,1},{1,0},{2,3},{3,2},{4,5},{5,4},{6,7},{7,6},{8,9},{9,8},{10,11... | collective-permute-start | bytes 1966088 | tf_op jit(solution)/shard_map/own_gradients/ppermute | solution.py:465
  100.0 22.6 %all-to-all-start = ((bf16[32,80,128]{2,1,0:T(8,128)(2,1)}), bf16[32,80,128]{2,1,0:T(8,128)(2,1)S(1)}, u32[]{:S(2)}, u32[]{:S(2)}) async-start(bf16[32,80,128]{2,1,0:T(8,128)(2,1)} %projection.1), calls=%async_computation | async-start | bytes 1310720 | tf_op jit(solution)/shard_map/projection_sum/all_to_all | solution.py:556
  (4 other events, 25.2 us)
